TPU v7x, 512 devices: a whole 4x8x8 slice. The times are simulated.
512 devices in a mesh: blk: 64 (over x, z_lo, y), rep: 8 (over z_hi, core).
Axes of the slice: x: 4, y: 8, z: 8 (z_hi: 4, z_lo: 2; z = z_hi * 2 + z_lo), core: 2. Of those that a mesh axis runs over, the one named last changes fastest.
Arguments:
- features: float32 [24576, 128], P('blk'), may hold values from -6 to 6
- tile_values: float32 [192, 96, 128, 128], P('blk', 'rep'), may hold values from -0.125 to 0.125
- tile_cols: int32 [192, 96], P('blk', 'rep'), may hold values from 0 to 191, as said below
- tile_counts: int32 [192, 8], P('blk', 'rep'), may hold values from 1 to 12, as said below
- degrees: int32 [24576], P('blk'), may hold values from 1 to 2
- curve_order: int32 [24576], P('blk'), may hold values from 0 to 24575, as said below
Outputs:
- hop_tokens: float32 [5, 24576, 128], P(None, 'blk')
Inputs may be any that keep to these rules, and one draw needn't show every extreme that they name: With p = i // 3 and w = s // 12, block tile_cols[i, s] lies in cycle position (p - w * 8 - j) mod 64 for some j in 0 to 7, where cycle position q holds blocks q * 3 to (q + 1) * 3 - 1; the 12 slots of one block-row and one w name distinct blocks. tile_counts[i, 0] = 12 for every block-row. `curve_order`: each aligned run of 384 curve positions is a permutation of the node numbers of the same run.
All inputs are finite; a program needn't handle non-finite values.
Results may differ from a plain program's by a relative error of at most 0.00013.
Values sent between devices are 32-bit elements; how exact they have to be, the bound alone decides.
No kernel may reach another device: no remote copies, remote signals or barrier semaphores. Data moves between devices by JAX's collectives and lax.ppermute only.
A program may use at most 64 MiB of HBM per device.

v0:
```python
import jax
import jax.numpy as jnp
from jax import lax
from jax.sharding import PartitionSpec as P

HOPS = 4


def from_behind(block, axis, distance):
    devices = range(lax.axis_size(axis))
    route = [((i - distance) % len(devices), i) for i in devices]
    return lax.ppermute(block, axis, route)


def realign_field(field, rank_rep, span_len, group_count):
    bit_count = group_count.bit_length() - 1
    for level in range(bit_count):
        moved = from_behind(field, "blk", span_len << level)
        chosen = jnp.bitwise_and(jnp.right_shift(rank_rep, level), 1) == 1
        field = jnp.where(chosen, moved, field)
    return field


def source_window(field, span_len):
    pieces = [field]
    walker = field
    for offset in range(1, span_len):
        walker = from_behind(walker, "blk", 1)
        pieces.append(walker)
    return pieces


def local(features, tile_values, tile_cols, tile_counts, degrees, curve_order):
    rank_blk = lax.axis_index("blk")
    rank_rep = lax.axis_index("rep")
    cycle_len = lax.axis_size("blk")
    group_count = lax.axis_size("rep")
    span_len = cycle_len // group_count
    row_count = features.shape[0]
    feat_width = features.shape[1]
    block_count = tile_values.shape[0]
    slot_count = tile_values.shape[1]
    tile_size = tile_values.shape[2]
    current = jnp.take(features, curve_order - rank_blk * row_count, axis=0)
    inv_root = lax.rsqrt(degrees.astype(jnp.float32))
    source_pos = tile_cols // block_count
    distance = jnp.mod(rank_blk - rank_rep * span_len - source_pos, cycle_len)
    slot_index = distance * block_count + tile_cols % block_count
    live_mask = (jnp.arange(slot_count, dtype=jnp.int32)[None, :] < tile_counts).astype(jnp.float32)
    tokens = [current]
    for hop_number in range(HOPS):
        sent = inv_root[:, None] * current
        aligned = realign_field(sent, rank_rep, span_len, group_count)
        pieces = source_window(aligned, span_len)
        stacked = jnp.stack(pieces).reshape(span_len * block_count, tile_size, feat_width)
        gathered = jnp.take(stacked, slot_index, axis=0) * live_mask[:, :, None, None]
        partial_value = jnp.einsum(
            "isab,isbc->iac", tile_values, gathered, precision=lax.Precision.HIGHEST
        )
        summed = lax.psum(partial_value.reshape(row_count, feat_width), "rep")
        current = inv_root[:, None] * summed
        tokens.append(current)
    return jnp.stack(tokens)


def solution(mesh):
    return jax.shard_map(
        local,
        mesh=mesh,
        in_specs=(
            P("blk", None),
            P("blk", "rep", None, None),
            P("blk", "rep"),
            P("blk", "rep"),
            P("blk"),
            P("blk"),
        ),
        out_specs=P(None, "blk", None),
        check_vma=False,
    )
```

profile of v0, /device:TPU:1, one launch (start us, length us, event | category | flops | bytes accessed | tf_op | source)
XLA Modules:
  0.0 800.5 jit_solution(2419111084597956695)
XLA Ops:
  10.3 4.8 collective-permute-start
  15.2 5.2 collective-permute-done
  20.6 2.4 collective-permute-start.1
  23.0 5.3 collective-permute-done.1
  28.3 3.0 collective-permute-start.2
  31.3 5.0 collective-permute-done.2
  37.0 5.2 collective-permute-start.3
  42.4 5.9 collective-permute-done.3
  51.0 8.0 %collective-permute-done.4 = f32[384,128]{1,0:T(8,128)S(1)} collective-permute-done((f32[384,128]{1,0:T(8,128)S(1)}, f32[384,128]{1,0:T(8,128)S(1)}, u32[]{:S(2)}, u32[]{:S(2)}) %collective-permute-start.4) | collective-permute-done | bytes 196640 | tf_op jit(solution)/shard_map/ppermute | solution.py:12
  61.6 8.0 %collective-permute-done.5 = f32[384,128]{1,0:T(8,128)S(1)} collective-permute-done((f32[384,128]{1,0:T(8,128)S(1)}, f32[384,128]{1,0:T(8,128)S(1)}, u32[]{:S(2)}, u32[]{:S(2)}) %collective-permute-start.5) | collective-permute-done | bytes 196640 | tf_op jit(solution)/shard_map/ppermute | solution.py:12
  72.2 8.0 %collective-permute-done.6 = f32[384,128]{1,0:T(8,128)S(1)} collective-permute-done((f32[384,128]{1,0:T(8,128)S(1)}, f32[384,128]{1,0:T(8,128)S(1)}, u32[]{:S(2)}, u32[]{:S(2)}) %collective-permute-start.6) | collective-permute-done | bytes 196640 | tf_op jit(solution)/shard_map/ppermute | solution.py:12
  82.8 8.0 %collective-permute-done.7 = f32[384,128]{1,0:T(8,128)S(1)} collective-permute-done((f32[384,128]{1,0:T(8,128)S(1)}, f32[384,128]{1,0:T(8,128)S(1)}, u32[]{:S(2)}, u32[]{:S(2)}) %collective-permute-start.7) | collective-permute-done | bytes 196640 | tf_op jit(solution)/shard_map/ppermute | solution.py:12
  93.4 8.0 %collective-permute-done.8 = f32[384,128]{1,0:T(8,128)S(1)} collective-permute-done((f32[384,128]{1,0:T(8,128)S(1)}, f32[384,128]{1,0:T(8,128)S(1)}, u32[]{:S(2)}, u32[]{:S(2)}) %collective-permute-start.8) | collective-permute-done | bytes 196640 | tf_op jit(solution)/shard_map/ppermute | solution.py:12
  104.1 8.0 %collective-permute-done.9 = f32[384,128]{1,0:T(8,128)S(1)} collective-permute-done((f32[384,128]{1,0:T(8,128)S(1)}, f32[384,128]{1,0:T(8,128)S(1)}, u32[]{:S(2)}, u32[]{:S(2)}) %collective-permute-start.9) | collective-permute-done | bytes 196640 | tf_op jit(solution)/shard_map/ppermute | solution.py:12
  112.8 3.5 gather_fusion.1
  116.3 5.2 fusion.3
  121.6 86.8 %all-reduce.5.cloned.1.call-done = f32[384,128]{1,0:T(8,128)} async-done(((f32[384,128]{1,0:T(8,128)}), f32[384,128]{1,0:T(8,128)}) %all-reduce.5.cloned.1.call-update) | async-done | bytes 196624 | tf_op jit(solution)/shard_map/psum | solution.py:60
  209.4 2.4 collective-permute-start.10
  211.8 6.1 collective-permute-done.10
  220.9 5.7 collective-permute-done.11
  226.6 2.2 collective-permute-start.12
  228.8 5.7 collective-permute-done.12
  235.2 3.1 collective-permute-start.13
  238.4 7.5 collective-permute-done.13
  248.5 8.0 %collective-permute-done.14 = f32[384,128]{1,0:T(8,128)S(1)} collective-permute-done((f32[384,128]{1,0:T(8,128)S(1)}, f32[384,128]{1,0:T(8,128)S(1)}, u32[]{:S(2)}, u32[]{:S(2)}) %collective-permute-start.14) | collective-permute-done | bytes 196640 | tf_op jit(solution)/shard_map/ppermute | solution.py:12
  259.1 8.0 %collective-permute-done.15 = f32[384,128]{1,0:T(8,128)S(1)} collective-permute-done((f32[384,128]{1,0:T(8,128)S(1)}, f32[384,128]{1,0:T(8,128)S(1)}, u32[]{:S(2)}, u32[]{:S(2)}) %collective-permute-start.15) | collective-permute-done | bytes 196640 | tf_op jit(solution)/shard_map/ppermute | solution.py:12
  269.7 8.0 %collective-permute-done.16 = f32[384,128]{1,0:T(8,128)S(1)} collective-permute-done((f32[384,128]{1,0:T(8,128)S(1)}, f32[384,128]{1,0:T(8,128)S(1)}, u32[]{:S(2)}, u32[]{:S(2)}) %collective-permute-start.16) | collective-permute-done | bytes 196640 | tf_op jit(solution)/shard_map/ppermute | solution.py:12
  280.3 8.7 %collective-permute-done.17 = f32[384,128]{1,0:T(8,128)S(1)} collective-permute-done((f32[384,128]{1,0:T(8,128)S(1)}, f32[384,128]{1,0:T(8,128)S(1)}, u32[]{:S(2)}, u32[]{:S(2)}) %collective-permute-start.17) | collective-permute-done | bytes 196640 | tf_op jit(solution)/shard_map/ppermute | solution.py:12
  291.7 9.9 %collective-permute-done.18 = f32[384,128]{1,0:T(8,128)S(1)} collective-permute-done((f32[384,128]{1,0:T(8,128)S(1)}, f32[384,128]{1,0:T(8,128)S(1)}, u32[]{:S(2)}, u32[]{:S(2)}) %collective-permute-start.18) | collective-permute-done | bytes 196640 | tf_op jit(solution)/shard_map/ppermute | solution.py:12
  304.1 9.6 %collective-permute-done.19 = f32[384,128]{1,0:T(8,128)S(1)} collective-permute-done((f32[384,128]{1,0:T(8,128)S(1)}, f32[384,128]{1,0:T(8,128)S(1)}, u32[]{:S(2)}, u32[]{:S(2)}) %collective-permute-start.19) | collective-permute-done | bytes 196640 | tf_op jit(solution)/shard_map/ppermute | solution.py:12
  314.4 3.5 gather_fusion.2
  317.9 5.2 fusion.2
  323.2 79.8 %all-reduce.7.cloned.1.call-done = f32[384,128]{1,0:T(8,128)} async-done(((f32[384,128]{1,0:T(8,128)}), f32[384,128]{1,0:T(8,128)}) %all-reduce.7.cloned.1.call-update) | async-done | bytes 196624 | tf_op jit(solution)/shard_map/psum | solution.py:60
  404.0 2.4 collective-permute-start.20
  406.4 6.1 collective-permute-done.20
  415.5 5.7 collective-permute-done.21
  423.4 5.7 collective-permute-done.22
  429.9 3.1 collective-permute-start.23
  433.0 7.5 collective-permute-done.23
  443.1 8.0 %collective-permute-done.24 = f32[384,128]{1,0:T(8,128)S(1)} collective-permute-done((f32[384,128]{1,0:T(8,128)S(1)}, f32[384,128]{1,0:T(8,128)S(1)}, u32[]{:S(2)}, u32[]{:S(2)}) %collective-permute-start.24) | collective-permute-done | bytes 196640 | tf_op jit(solution)/shard_map/ppermute | solution.py:12
  453.7 8.0 %collective-permute-done.25 = f32[384,128]{1,0:T(8,128)S(1)} collective-permute-done((f32[384,128]{1,0:T(8,128)S(1)}, f32[384,128]{1,0:T(8,128)S(1)}, u32[]{:S(2)}, u32[]{:S(2)}) %collective-permute-start.25) | collective-permute-done | bytes 196640 | tf_op jit(solution)/shard_map/ppermute | solution.py:12
  464.3 8.0 %collective-permute-done.26 = f32[384,128]{1,0:T(8,128)S(1)} collective-permute-done((f32[384,128]{1,0:T(8,128)S(1)}, f32[384,128]{1,0:T(8,128)S(1)}, u32[]{:S(2)}, u32[]{:S(2)}) %collective-permute-start.26) | collective-permute-done | bytes 196640 | tf_op jit(solution)/shard_map/ppermute | solution.py:12
  475.0 8.7 %collective-permute-done.27 = f32[384,128]{1,0:T(8,128)S(1)} collective-permute-done((f32[384,128]{1,0:T(8,128)S(1)}, f32[384,128]{1,0:T(8,128)S(1)}, u32[]{:S(2)}, u32[]{:S(2)}) %collective-permute-start.27) | collective-permute-done | bytes 196640 | tf_op jit(solution)/shard_map/ppermute | solution.py:12
  486.3 9.9 %collective-permute-done.28 = f32[384,128]{1,0:T(8,128)S(1)} collective-permute-done((f32[384,128]{1,0:T(8,128)S(1)}, f32[384,128]{1,0:T(8,128)S(1)}, u32[]{:S(2)}, u32[]{:S(2)}) %collective-permute-start.28) | collective-permute-done | bytes 196640 | tf_op jit(solution)/shard_map/ppermute | solution.py:12
  498.9 9.4 %collective-permute-done.29 = f32[384,128]{1,0:T(8,128)S(1)} collective-permute-done((f32[384,128]{1,0:T(8,128)S(1)}, f32[384,128]{1,0:T(8,128)S(1)}, u32[]{:S(2)}, u32[]{:S(2)}) %collective-permute-start.29) | collective-permute-done | bytes 196640 | tf_op jit(solution)/shard_map/ppermute | solution.py:12
  509.0 3.5 gather_fusion.3
  512.6 5.2 fusion.1
  517.8 79.8 %all-reduce.9.cloned.1.call-done = f32[384,128]{1,0:T(8,128)} async-done(((f32[384,128]{1,0:T(8,128)}), f32[384,128]{1,0:T(8,128)}) %all-reduce.9.cloned.1.call-update) | async-done | bytes 196624 | tf_op jit(solution)/shard_map/psum | solution.py:60
  598.6 2.4 collective-permute-start.30
  601.0 6.1 collective-permute-done.30
  610.3 5.6 collective-permute-done.31
  615.9 2.2 collective-permute-start.32
  618.2 5.6 collective-permute-done.32
  624.5 3.1 collective-permute-start.33
  627.8 7.4 collective-permute-done.33
  637.7 8.0 %collective-permute-done.34 = f32[384,128]{1,0:T(8,128)S(1)} collective-permute-done((f32[384,128]{1,0:T(8,128)S(1)}, f32[384,128]{1,0:T(8,128)S(1)}, u32[]{:S(2)}, u32[]{:S(2)}) %collective-permute-start.34) | collective-permute-done | bytes 196640 | tf_op jit(solution)/shard_map/ppermute | solution.py:12
  648.3 8.0 %collective-permute-done.35 = f32[384,128]{1,0:T(8,128)S(1)} collective-permute-done((f32[384,128]{1,0:T(8,128)S(1)}, f32[384,128]{1,0:T(8,128)S(1)}, u32[]{:S(2)}, u32[]{:S(2)}) %collective-permute-start.35) | collective-permute-done | bytes 196640 | tf_op jit(solution)/shard_map/ppermute | solution.py:12
  659.0 8.0 %collective-permute-done.36 = f32[384,128]{1,0:T(8,128)S(1)} collective-permute-done((f32[384,128]{1,0:T(8,128)S(1)}, f32[384,128]{1,0:T(8,128)S(1)}, u32[]{:S(2)}, u32[]{:S(2)}) %collective-permute-start.36) | collective-permute-done | bytes 196640 | tf_op jit(solution)/shard_map/ppermute | solution.py:12
  669.6 8.7 %collective-permute-done.37 = f32[384,128]{1,0:T(8,128)S(1)} collective-permute-done((f32[384,128]{1,0:T(8,128)S(1)}, f32[384,128]{1,0:T(8,128)S(1)}, u32[]{:S(2)}, u32[]{:S(2)}) %collective-permute-start.37) | collective-permute-done | bytes 196640 | tf_op jit(solution)/shard_map/ppermute | solution.py:12
  680.9 9.9 %collective-permute-done.38 = f32[384,128]{1,0:T(8,128)S(1)} collective-permute-done((f32[384,128]{1,0:T(8,128)S(1)}, f32[384,128]{1,0:T(8,128)S(1)}, u32[]{:S(2)}, u32[]{:S(2)}) %collective-permute-start.38) | collective-permute-done | bytes 196640 | tf_op jit(solution)/shard_map/ppermute | solution.py:12
  693.4 9.6 %collective-permute-done.39 = f32[384,128]{1,0:T(8,128)S(1)} collective-permute-done((f32[384,128]{1,0:T(8,128)S(1)}, f32[384,128]{1,0:T(8,128)S(1)}, u32[]{:S(2)}, u32[]{:S(2)}) %collective-permute-start.39) | collective-permute-done | bytes 196640 | tf_op jit(solution)/shard_map/ppermute | solution.py:12
  703.7 3.5 gather_fusion.4
  707.2 5.2 fusion
  713.2 79.0 %all-reduce.11.cloned.1.call-done = f32[384,128]{1,0:T(8,128)} async-done(((f32[384,128]{1,0:T(8,128)}), f32[384,128]{1,0:T(8,128)}) %all-reduce.11.cloned.1.call-update) | async-done | bytes 196624 | tf_op jit(solution)/shard_map/psum | solution.py:60
  (106 shorter events, 89.5 us)
Async XLA Ops:
  6.5 109.8 %copy-start = (f32[3,12,128,128]{3,2,1,0:T(8,128)S(1)}, f32[3,12,128,128]{3,2,1,0:T(8,128)}, u32[]{:S(2)}) copy-start(f32[3,12,128,128]{3,2,1,0:T(8,128)} %param.9) | copy-start | bytes 7077892
  6.5 201.8 %all-reduce.5.cloned.1.call-start = ((), (), s32[]{:S(2)}) async-start(), calls=%async_computation | async-start | bytes 393216 | tf_op jit(solution)/shard_map/psum | solution.py:60
  10.1 32.1 %copy-start.5 = (s32[3,12]{1,0:T(4,128)S(1)}, s32[3,12]{1,0:T(4,128)}, u32[]{:S(2)}) copy-start(s32[3,12]{1,0:T(4,128)} %param.10) | copy-start | bytes 436
  10.1 32.1 %copy-start.6 = (s32[3,1]{0,1:T(1,128)S(1)}, s32[3,1]{0,1:T(1,128)}, u32[]{:S(2)}) copy-start(s32[3,1]{0,1:T(1,128)} %param.11) | copy-start | bytes 40
  10.3 10.1 %collective-permute-start = (f32[384,128]{1,0:T(8,128)S(1)}, f32[384,128]{1,0:T(8,128)S(1)}, u32[]{:S(2)}, u32[]{:S(2)}) collective-permute-start(f32[384,128]{1,0:T(8,128)S(1)} %select_multiply_fusion.8), channel_id=1, source_target_pairs={{448,0},{456,8},{464,16},{472,24},{480,32},{488,40},{496,48},{504,... | collective-permute-start | bytes 589832 | tf_op jit(solution)/shard_map/ppermute | solution.py:12
  20.6 7.7 collective-permute-start.1
  28.3 8.0 %collective-permute-start.2 = (f32[384,128]{1,0:T(8,128)S(1)}, f32[384,128]{1,0:T(8,128)S(1)}, u32[]{:S(2)}, u32[]{:S(2)}) collective-permute-start(f32[384,128]{1,0:T(8,128)S(1)} %broadcast_select_fusion.7), channel_id=1, source_target_pairs={{256,0},{264,8},{272,16},{280,24},{288,32},{296,40},{304,48},{312,... | collective-permute-start | bytes 589832 | tf_op jit(solution)/shard_map/ppermute | solution.py:12
  37.0 11.3 %collective-permute-start.3 = (f32[384,128]{1,0:T(8,128)S(1)}, f32[384,128]{1,0:T(8,128)S(1)}, u32[]{:S(2)}, u32[]{:S(2)}) collective-permute-start(f32[384,128]{1,0:T(8,128)S(1)} %get-tuple-element.15), channel_id=1, source_target_pairs={{504,0},{0,8},{8,16},{16,24},{24,32},{32,40},{40,48},{48,56},{56,6... | collective-permute-start | bytes 589832 | tf_op jit(solution)/shard_map/ppermute | solution.py:12
  48.4 10.6 %collective-permute-start.4 = (f32[384,128]{1,0:T(8,128)S(1)}, f32[384,128]{1,0:T(8,128)S(1)}, u32[]{:S(2)}, u32[]{:S(2)}) collective-permute-start(f32[384,128]{1,0:T(8,128)S(1)} %collective-permute-done.3), channel_id=1, source_target_pairs={{504,0},{0,8},{8,16},{16,24},{24,32},{32,40},{40,48},{48,56},{56,6... | collective-permute-start | bytes 589832 | tf_op jit(solution)/shard_map/ppermute | solution.py:12
  59.0 10.6 %collective-permute-start.5 = (f32[384,128]{1,0:T(8,128)S(1)}, f32[384,128]{1,0:T(8,128)S(1)}, u32[]{:S(2)}, u32[]{:S(2)}) collective-permute-start(f32[384,128]{1,0:T(8,128)S(1)} %collective-permute-done.4), channel_id=1, source_target_pairs={{504,0},{0,8},{8,16},{16,24},{24,32},{32,40},{40,48},{48,56},{56,6... | collective-permute-start | bytes 589832 | tf_op jit(solution)/shard_map/ppermute | solution.py:12
  69.6 10.6 %collective-permute-start.6 = (f32[384,128]{1,0:T(8,128)S(1)}, f32[384,128]{1,0:T(8,128)S(1)}, u32[]{:S(2)}, u32[]{:S(2)}) collective-permute-start(f32[384,128]{1,0:T(8,128)S(1)} %collective-permute-done.5), channel_id=1, source_target_pairs={{504,0},{0,8},{8,16},{16,24},{24,32},{32,40},{40,48},{48,56},{56,6... | collective-permute-start | bytes 589832 | tf_op jit(solution)/shard_map/ppermute | solution.py:12
  80.2 10.6 %collective-permute-start.7 = (f32[384,128]{1,0:T(8,128)S(1)}, f32[384,128]{1,0:T(8,128)S(1)}, u32[]{:S(2)}, u32[]{:S(2)}) collective-permute-start(f32[384,128]{1,0:T(8,128)S(1)} %collective-permute-done.6), channel_id=1, source_target_pairs={{504,0},{0,8},{8,16},{16,24},{24,32},{32,40},{40,48},{48,56},{56,6... | collective-permute-start | bytes 589832 | tf_op jit(solution)/shard_map/ppermute | solution.py:12
  90.8 10.6 %collective-permute-start.8 = (f32[384,128]{1,0:T(8,128)S(1)}, f32[384,128]{1,0:T(8,128)S(1)}, u32[]{:S(2)}, u32[]{:S(2)}) collective-permute-start(f32[384,128]{1,0:T(8,128)S(1)} %collective-permute-done.7), channel_id=1, source_target_pairs={{504,0},{0,8},{8,16},{16,24},{24,32},{32,40},{40,48},{48,56},{56,6... | collective-permute-start | bytes 589832 | tf_op jit(solution)/shard_map/ppermute | solution.py:12
  101.5 10.6 %collective-permute-start.9 = (f32[384,128]{1,0:T(8,128)S(1)}, f32[384,128]{1,0:T(8,128)S(1)}, u32[]{:S(2)}, u32[]{:S(2)}) collective-permute-start(f32[384,128]{1,0:T(8,128)S(1)} %collective-permute-done.8), channel_id=1, source_target_pairs={{504,0},{0,8},{8,16},{16,24},{24,32},{32,40},{40,48},{48,56},{56,6... | collective-permute-start | bytes 589832 | tf_op jit(solution)/shard_map/ppermute | solution.py:12
  121.5 281.5 %all-reduce.7.cloned.1.call-start = ((), (), s32[]{:S(2)}) async-start(), calls=%async_computation.1 | async-start | bytes 393216 | tf_op jit(solution)/shard_map/psum | solution.py:60
  209.4 8.5 %collective-permute-start.10 = (f32[384,128]{1,0:T(8,128)S(1)}, f32[384,128]{1,0:T(8,128)S(1)}, u32[]{:S(2)}, u32[]{:S(2)}) collective-permute-start(f32[384,128]{1,0:T(8,128)S(1)} %multiply_multiply_fusion.2), channel_id=1, source_target_pairs={{448,0},{456,8},{464,16},{472,24},{480,32},{488,40},{496,48},{504,... | collective-permute-start | bytes 589832 | tf_op jit(solution)/shard_map/ppermute | solution.py:12
  219.0 7.6 collective-permute-start.11
  226.6 7.9 collective-permute-start.12
  235.2 10.6 %collective-permute-start.13 = (f32[384,128]{1,0:T(8,128)S(1)}, f32[384,128]{1,0:T(8,128)S(1)}, u32[]{:S(2)}, u32[]{:S(2)}) collective-permute-start(f32[384,128]{1,0:T(8,128)S(1)} %get-tuple-element.11), channel_id=1, source_target_pairs={{504,0},{0,8},{8,16},{16,24},{24,32},{32,40},{40,48},{48,56},{56,6... | collective-permute-start | bytes 589832 | tf_op jit(solution)/shard_map/ppermute | solution.py:12
  245.9 10.6 %collective-permute-start.14 = (f32[384,128]{1,0:T(8,128)S(1)}, f32[384,128]{1,0:T(8,128)S(1)}, u32[]{:S(2)}, u32[]{:S(2)}) collective-permute-start(f32[384,128]{1,0:T(8,128)S(1)} %collective-permute-done.13), channel_id=1, source_target_pairs={{504,0},{0,8},{8,16},{16,24},{24,32},{32,40},{40,48},{48,56},{56,6... | collective-permute-start | bytes 589832 | tf_op jit(solution)/shard_map/ppermute | solution.py:12
  256.5 10.6 %collective-permute-start.15 = (f32[384,128]{1,0:T(8,128)S(1)}, f32[384,128]{1,0:T(8,128)S(1)}, u32[]{:S(2)}, u32[]{:S(2)}) collective-permute-start(f32[384,128]{1,0:T(8,128)S(1)} %collective-permute-done.14), channel_id=1, source_target_pairs={{504,0},{0,8},{8,16},{16,24},{24,32},{32,40},{40,48},{48,56},{56,6... | collective-permute-start | bytes 589832 | tf_op jit(solution)/shard_map/ppermute | solution.py:12
  267.1 10.6 %collective-permute-start.16 = (f32[384,128]{1,0:T(8,128)S(1)}, f32[384,128]{1,0:T(8,128)S(1)}, u32[]{:S(2)}, u32[]{:S(2)}) collective-permute-start(f32[384,128]{1,0:T(8,128)S(1)} %collective-permute-done.15), channel_id=1, source_target_pairs={{504,0},{0,8},{8,16},{16,24},{24,32},{32,40},{40,48},{48,56},{56,6... | collective-permute-start | bytes 589832 | tf_op jit(solution)/shard_map/ppermute | solution.py:12
  277.7 11.3 %collective-permute-start.17 = (f32[384,128]{1,0:T(8,128)S(1)}, f32[384,128]{1,0:T(8,128)S(1)}, u32[]{:S(2)}, u32[]{:S(2)}) collective-permute-start(f32[384,128]{1,0:T(8,128)S(1)} %collective-permute-done.16), channel_id=1, source_target_pairs={{504,0},{0,8},{8,16},{16,24},{24,32},{32,40},{40,48},{48,56},{56,6... | collective-permute-start | bytes 589832 | tf_op jit(solution)/shard_map/ppermute | solution.py:12
  289.1 12.4 %collective-permute-start.18 = (f32[384,128]{1,0:T(8,128)S(1)}, f32[384,128]{1,0:T(8,128)S(1)}, u32[]{:S(2)}, u32[]{:S(2)}) collective-permute-start(f32[384,128]{1,0:T(8,128)S(1)} %collective-permute-done.17), channel_id=1, source_target_pairs={{504,0},{0,8},{8,16},{16,24},{24,32},{32,40},{40,48},{48,56},{56,6... | collective-permute-start | bytes 589832 | tf_op jit(solution)/shard_map/ppermute | solution.py:12
  301.5 12.2 %collective-permute-start.19 = (f32[384,128]{1,0:T(8,128)S(1)}, f32[384,128]{1,0:T(8,128)S(1)}, u32[]{:S(2)}, u32[]{:S(2)}) collective-permute-start(f32[384,128]{1,0:T(8,128)S(1)} %collective-permute-done.18), channel_id=1, source_target_pairs={{504,0},{0,8},{8,16},{16,24},{24,32},{32,40},{40,48},{48,56},{56,6... | collective-permute-start | bytes 589832 | tf_op jit(solution)/shard_map/ppermute | solution.py:12
  323.1 274.5 %all-reduce.9.cloned.1.call-start = ((), (), s32[]{:S(2)}) async-start(), calls=%async_computation.2 | async-start | bytes 393216 | tf_op jit(solution)/shard_map/psum | solution.py:60
  404.0 8.5 %collective-permute-start.20 = (f32[384,128]{1,0:T(8,128)S(1)}, f32[384,128]{1,0:T(8,128)S(1)}, u32[]{:S(2)}, u32[]{:S(2)}) collective-permute-start(f32[384,128]{1,0:T(8,128)S(1)} %multiply_multiply_fusion.1), channel_id=1, source_target_pairs={{448,0},{456,8},{464,16},{472,24},{480,32},{488,40},{496,48},{504,... | collective-permute-start | bytes 589832 | tf_op jit(solution)/shard_map/ppermute | solution.py:12
  413.6 7.6 collective-permute-start.21
  421.3 7.9 collective-permute-start.22
  429.9 10.6 %collective-permute-start.23 = (f32[384,128]{1,0:T(8,128)S(1)}, f32[384,128]{1,0:T(8,128)S(1)}, u32[]{:S(2)}, u32[]{:S(2)}) collective-permute-start(f32[384,128]{1,0:T(8,128)S(1)} %get-tuple-element.9), channel_id=1, source_target_pairs={{504,0},{0,8},{8,16},{16,24},{24,32},{32,40},{40,48},{48,56},{56,6... | collective-permute-start | bytes 589832 | tf_op jit(solution)/shard_map/ppermute | solution.py:12
  440.5 10.6 %collective-permute-start.24 = (f32[384,128]{1,0:T(8,128)S(1)}, f32[384,128]{1,0:T(8,128)S(1)}, u32[]{:S(2)}, u32[]{:S(2)}) collective-permute-start(f32[384,128]{1,0:T(8,128)S(1)} %collective-permute-done.23), channel_id=1, source_target_pairs={{504,0},{0,8},{8,16},{16,24},{24,32},{32,40},{40,48},{48,56},{56,6... | collective-permute-start | bytes 589832 | tf_op jit(solution)/shard_map/ppermute | solution.py:12
  451.1 10.6 %collective-permute-start.25 = (f32[384,128]{1,0:T(8,128)S(1)}, f32[384,128]{1,0:T(8,128)S(1)}, u32[]{:S(2)}, u32[]{:S(2)}) collective-permute-start(f32[384,128]{1,0:T(8,128)S(1)} %collective-permute-done.24), channel_id=1, source_target_pairs={{504,0},{0,8},{8,16},{16,24},{24,32},{32,40},{40,48},{48,56},{56,6... | collective-permute-start | bytes 589832 | tf_op jit(solution)/shard_map/ppermute | solution.py:12
  461.7 10.6 %collective-permute-start.26 = (f32[384,128]{1,0:T(8,128)S(1)}, f32[384,128]{1,0:T(8,128)S(1)}, u32[]{:S(2)}, u32[]{:S(2)}) collective-permute-start(f32[384,128]{1,0:T(8,128)S(1)} %collective-permute-done.25), channel_id=1, source_target_pairs={{504,0},{0,8},{8,16},{16,24},{24,32},{32,40},{40,48},{48,56},{56,6... | collective-permute-start | bytes 589832 | tf_op jit(solution)/shard_map/ppermute | solution.py:12
  472.4 11.3 %collective-permute-start.27 = (f32[384,128]{1,0:T(8,128)S(1)}, f32[384,128]{1,0:T(8,128)S(1)}, u32[]{:S(2)}, u32[]{:S(2)}) collective-permute-start(f32[384,128]{1,0:T(8,128)S(1)} %collective-permute-done.26), channel_id=1, source_target_pairs={{504,0},{0,8},{8,16},{16,24},{24,32},{32,40},{40,48},{48,56},{56,6... | collective-permute-start | bytes 589832 | tf_op jit(solution)/shard_map/ppermute | solution.py:12
  483.7 12.4 %collective-permute-start.28 = (f32[384,128]{1,0:T(8,128)S(1)}, f32[384,128]{1,0:T(8,128)S(1)}, u32[]{:S(2)}, u32[]{:S(2)}) collective-permute-start(f32[384,128]{1,0:T(8,128)S(1)} %collective-permute-done.27), channel_id=1, source_target_pairs={{504,0},{0,8},{8,16},{16,24},{24,32},{32,40},{40,48},{48,56},{56,6... | collective-permute-start | bytes 589832 | tf_op jit(solution)/shard_map/ppermute | solution.py:12
  496.2 12.2 %collective-permute-start.29 = (f32[384,128]{1,0:T(8,128)S(1)}, f32[384,128]{1,0:T(8,128)S(1)}, u32[]{:S(2)}, u32[]{:S(2)}) collective-permute-start(f32[384,128]{1,0:T(8,128)S(1)} %collective-permute-done.28), channel_id=1, source_target_pairs={{504,0},{0,8},{8,16},{16,24},{24,32},{32,40},{40,48},{48,56},{56,6... | collective-permute-start | bytes 589832 | tf_op jit(solution)/shard_map/ppermute | solution.py:12
  517.8 100.3 %copy-start.1 = (f32[384,128]{1,0:T(8,128)S(1)}, f32[384,128]{1,0:T(8,128)}, u32[]{:S(2)}) copy-start(f32[384,128]{1,0:T(8,128)} %all-reduce.5.cloned.1.call-done) | copy-start | bytes 589828
  517.8 109.8 %copy-start.2 = (f32[384,128]{1,0:T(8,128)S(1)}, f32[384,128]{1,0:T(8,128)}, u32[]{:S(2)}) copy-start(f32[384,128]{1,0:T(8,128)} %all-reduce.7.cloned.1.call-done) | copy-start | bytes 589828
  517.8 274.5 %all-reduce.11.cloned.1.call-start = ((), (), s32[]{:S(2)}) async-start(), calls=%async_computation.3 | async-start | bytes 393216 | tf_op jit(solution)/shard_map/psum | solution.py:60
  598.6 8.5 %collective-permute-start.30 = (f32[384,128]{1,0:T(8,128)S(1)}, f32[384,128]{1,0:T(8,128)S(1)}, u32[]{:S(2)}, u32[]{:S(2)}) collective-permute-start(f32[384,128]{1,0:T(8,128)S(1)} %multiply_multiply_fusion), channel_id=1, source_target_pairs={{448,0},{456,8},{464,16},{472,24},{480,32},{488,40},{496,48},{504,... | collective-permute-start | bytes 589832 | tf_op jit(solution)/shard_map/ppermute | solution.py:12
  608.2 7.6 collective-permute-start.31
  615.9 7.9 collective-permute-start.32
  624.5 10.6 %collective-permute-start.33 = (f32[384,128]{1,0:T(8,128)S(1)}, f32[384,128]{1,0:T(8,128)S(1)}, u32[]{:S(2)}, u32[]{:S(2)}) collective-permute-start(f32[384,128]{1,0:T(8,128)S(1)} %get-tuple-element.7), channel_id=1, source_target_pairs={{504,0},{0,8},{8,16},{16,24},{24,32},{32,40},{40,48},{48,56},{56,6... | collective-permute-start | bytes 589832 | tf_op jit(solution)/shard_map/ppermute | solution.py:12
  627.7 75.9 %copy-start.4 = (f32[5,384,128]{2,1,0:T(8,128)}, f32[5,384,128]{2,1,0:T(8,128)S(1)}, u32[]{:S(2)}) copy-start(f32[5,384,128]{2,1,0:T(8,128)S(1)} %bitcast_dynamic-update-slice_fusion.18) | copy-start | bytes 2949124
  635.1 10.6 %collective-permute-start.34 = (f32[384,128]{1,0:T(8,128)S(1)}, f32[384,128]{1,0:T(8,128)S(1)}, u32[]{:S(2)}, u32[]{:S(2)}) collective-permute-start(f32[384,128]{1,0:T(8,128)S(1)} %collective-permute-done.33), channel_id=1, source_target_pairs={{504,0},{0,8},{8,16},{16,24},{24,32},{32,40},{40,48},{48,56},{56,6... | collective-permute-start | bytes 589832 | tf_op jit(solution)/shard_map/ppermute | solution.py:12
  645.7 10.6 %collective-permute-start.35 = (f32[384,128]{1,0:T(8,128)S(1)}, f32[384,128]{1,0:T(8,128)S(1)}, u32[]{:S(2)}, u32[]{:S(2)}) collective-permute-start(f32[384,128]{1,0:T(8,128)S(1)} %collective-permute-done.34), channel_id=1, source_target_pairs={{504,0},{0,8},{8,16},{16,24},{24,32},{32,40},{40,48},{48,56},{56,6... | collective-permute-start | bytes 589832 | tf_op jit(solution)/shard_map/ppermute | solution.py:12
  656.4 10.6 %collective-permute-start.36 = (f32[384,128]{1,0:T(8,128)S(1)}, f32[384,128]{1,0:T(8,128)S(1)}, u32[]{:S(2)}, u32[]{:S(2)}) collective-permute-start(f32[384,128]{1,0:T(8,128)S(1)} %collective-permute-done.35), channel_id=1, source_target_pairs={{504,0},{0,8},{8,16},{16,24},{24,32},{32,40},{40,48},{48,56},{56,6... | collective-permute-start | bytes 589832 | tf_op jit(solution)/shard_map/ppermute | solution.py:12
  667.0 11.3 %collective-permute-start.37 = (f32[384,128]{1,0:T(8,128)S(1)}, f32[384,128]{1,0:T(8,128)S(1)}, u32[]{:S(2)}, u32[]{:S(2)}) collective-permute-start(f32[384,128]{1,0:T(8,128)S(1)} %collective-permute-done.36), channel_id=1, source_target_pairs={{504,0},{0,8},{8,16},{16,24},{24,32},{32,40},{40,48},{48,56},{56,6... | collective-permute-start | bytes 589832 | tf_op jit(solution)/shard_map/ppermute | solution.py:12
  678.3 12.4 %collective-permute-start.38 = (f32[384,128]{1,0:T(8,128)S(1)}, f32[384,128]{1,0:T(8,128)S(1)}, u32[]{:S(2)}, u32[]{:S(2)}) collective-permute-start(f32[384,128]{1,0:T(8,128)S(1)} %collective-permute-done.37), channel_id=1, source_target_pairs={{504,0},{0,8},{8,16},{16,24},{24,32},{32,40},{40,48},{48,56},{56,6... | collective-permute-start | bytes 589832 | tf_op jit(solution)/shard_map/ppermute | solution.py:12
  690.8 12.2 %collective-permute-start.39 = (f32[384,128]{1,0:T(8,128)S(1)}, f32[384,128]{1,0:T(8,128)S(1)}, u32[]{:S(2)}, u32[]{:S(2)}) collective-permute-start(f32[384,128]{1,0:T(8,128)S(1)} %collective-permute-done.38), channel_id=1, source_target_pairs={{504,0},{0,8},{8,16},{16,24},{24,32},{32,40},{40,48},{48,56},{56,6... | collective-permute-start | bytes 589832 | tf_op jit(solution)/shard_map/ppermute | solution.py:12
  707.2 5.2 copy-start.3
Sparse Core Ops, SparseCore 0:
  121.6 86.6 all-reduce.4
  323.3 79.6 all-reduce.6
  517.9 79.6 all-reduce.8
  712.6 79.6 all-reduce.10
where the time goes:
time: 803 us; the launch traced here: 801 us
  waiting for transfers between devices  626 us (78%)
  starting transfers between devices  90.4 us (11%)
  local copies, waits for them, and re-layouts  35.5 us (4%)
  matrix products  20.7 us (3%)
  other arithmetic  14 us (2%)
  between operations  13.7 us (2%)
    psum x4, waiting for transfers between devices, local(): summed = lax.psum(partial_value.reshape(row_count, feat_width), 'rep')  325 us
    ppermute x40, waiting for transfers between devices, from_behind(): return lax.ppermute(block, axis, route)  301 us
    ppermute x40, starting transfers between devices, from_behind(): return lax.ppermute(block, axis, route)  90.2 us
    dot_general x4, matrix products, local(): jnp.einsum('isab,isbc->iac', tile_values, gathered, precision=lax.Precisi...  20.7 us
    unnamed x38, local copies, waits for them, and re-layouts  16.5 us
  transfers between devices with their start and end apart: 44, of which 44 were waited for; matrix products, arithmetic and copies ran while one was open for 2% of the time, Pallas kernels for 0%

commit v1 on v0

v1 whole, which is shorter than its diff:
```python
import functools

import jax
import jax.numpy as jnp
from jax import lax
from jax.experimental import pallas as pl
from jax.experimental.pallas import tpu as pltpu
from jax.sharding import PartitionSpec as P

HOPS = 4
CHAINS = 2
HALF = 64


def send(block, place):
    cycle, groups = lax.axis_size("blk"), lax.axis_size("rep")
    route = []
    for p in range(cycle):
        for w in range(groups):
            to_p, to_w = place(p, w)
            route.append((p * groups + w, (to_p % cycle) * groups + to_w))
    return lax.ppermute(block, ("blk", "rep"), route)


def ahead(block, distance):
    return send(block, lambda p, w: (p + distance, w))


def pack(field, chain):
    blocks = field.shape[0] // 128
    half = field.reshape(blocks, 2, HALF, 2, HALF)[:, :, :, chain]
    return half.transpose(0, 2, 1, 3).reshape(blocks * HALF, 128)


def split_tiles(tiles_ref, out_ref):
    for s in range(tiles_ref.shape[1]):
        tile = tiles_ref[0, s]
        high = tile.astype(jnp.bfloat16)
        low = (tile - high.astype(jnp.float32)).astype(jnp.bfloat16)
        out_ref[0, 0:128, s * 128:(s + 1) * 128] = high
        out_ref[0, 128:256, s * 128:(s + 1) * 128] = low


def tile_parts(tile_values):
    rows, slots = tile_values.shape[:2]
    return pl.pallas_call(
        split_tiles,
        grid=(rows,),
        in_specs=[pl.BlockSpec((1, slots, 128, 128), lambda i: (i, 0, 0, 0))],
        out_specs=pl.BlockSpec((1, 256, slots * 128), lambda i: (i, 0, 0)),
        out_shape=jax.ShapeDtypeStruct((rows, 256, slots * 128), jnp.bfloat16),
        compiler_params=pltpu.CompilerParams(vmem_limit_bytes=32 * 2**20),
    )(tile_values)


def product_kernel(homes, rows, slots, index_ref, tiles_ref, scale_ref, *refs):
    units = refs[:-3]
    out_ref, source_ref, gathered_ref = refs[-3:]
    lane = lax.broadcasted_iota(jnp.int32, (HALF, 128), 1)
    left = lane < HALF
    for k, (which, first) in enumerate(homes):
        part = units[which][first:first + HALF]
        high = part.astype(jnp.bfloat16).astype(jnp.float32)
        low = part - high
        top = jnp.where(left, high, pltpu.roll(low, HALF, 1))
        bottom = jnp.where(left, pltpu.roll(high, HALF, 1), low)
        source_ref[k, 0:HALF] = top.astype(jnp.bfloat16)
        source_ref[k, HALF:128] = bottom.astype(jnp.bfloat16)
    source_ref[len(homes)] = jnp.zeros((128, 128), jnp.bfloat16)
    for i in range(rows):
        for s in range(slots):
            gathered_ref[i, s * 128:(s + 1) * 128] = source_ref[index_ref[i, s]]
    for i in range(rows):
        both = jnp.dot(tiles_ref[i], gathered_ref[i], preferred_element_type=jnp.float32)
        total = both[0:128] + both[128:256]
        total = total + pltpu.roll(total, HALF, 1)
        packed = jnp.where(left, total[0:HALF], total[HALF:128])
        out_ref[i * HALF:(i + 1) * HALF] = packed * scale_ref[i * HALF:(i + 1) * HALF]


def product(slot_index, tiles, scale, units, homes):
    rows, slots = slot_index.shape
    vmem = pl.BlockSpec(memory_space=pltpu.VMEM)
    return pl.pallas_call(
        functools.partial(product_kernel, homes, rows, slots),
        in_specs=[pl.BlockSpec(memory_space=pltpu.SMEM)] + [vmem] * (2 + len(units)),
        out_specs=vmem,
        out_shape=jax.ShapeDtypeStruct((rows * HALF, 128), jnp.float32),
        scratch_shapes=[
            pltpu.VMEM((len(homes) + 1, 128, 128), jnp.bfloat16),
            pltpu.VMEM((rows, slots * 128, 128), jnp.bfloat16),
        ],
        compiler_params=pltpu.CompilerParams(vmem_limit_bytes=32 * 2**20),
        cost_estimate=pl.CostEstimate(flops=2 * rows * slots * 256 * 128 * 128, bytes_accessed=8 * 2**20, transcendentals=0),
    )(slot_index, tiles, scale, *units)


def finish_kernel(ordered_ref, root_ref, *refs):
    out_ref = refs[-1]
    fields = refs[:-1]
    out_ref[0] = ordered_ref[...]
    lane = lax.broadcasted_iota(jnp.int32, (HALF, 128), 1)
    left = lane < HALF
    blocks = ordered_ref.shape[0] // 128
    for hop in range(HOPS):
        for b in range(blocks):
            a = fields[2 * hop][b * HALF:(b + 1) * HALF]
            c = fields[2 * hop + 1][b * HALF:(b + 1) * HALF]
            first = b * 128
            top = jnp.where(left, a, pltpu.roll(c, HALF, 1))
            bottom = jnp.where(left, pltpu.roll(a, HALF, 1), c)
            out_ref[hop + 1, first:first + HALF] = top * root_ref[first:first + HALF]
            out_ref[hop + 1, first + HALF:first + 128] = bottom * root_ref[first + HALF:first + 128]


def finish(ordered, root, fields):
    vmem = pl.BlockSpec(memory_space=pltpu.VMEM)
    return pl.pallas_call(
        finish_kernel,
        in_specs=[vmem] * (2 + len(fields)),
        out_specs=vmem,
        out_shape=jax.ShapeDtypeStruct((HOPS + 1,) + ordered.shape, jnp.float32),
        compiler_params=pltpu.CompilerParams(vmem_limit_bytes=32 * 2**20),
    )(ordered, root, *fields)


def window(own):
    two, six, four = ahead(own, 2), ahead(own, 6), ahead(own, 4)
    near = ahead(jnp.concatenate([own, six]), 1)
    far = ahead(jnp.concatenate([four, six]), -1)
    arrays = [own, two, four, six, near, far]
    places = [(0, 0), (4, 0), (1, 0), (5, 0), (2, 0), (5, 1), (3, 0), (4, 1)]
    return arrays, places


def local(features, tile_values, tile_cols, tile_counts, degrees, curve_order):
    rank_blk = lax.axis_index("blk")
    rank_rep = lax.axis_index("rep")
    cycle = lax.axis_size("blk")
    span = cycle // lax.axis_size("rep")
    rows, slots = tile_values.shape[:2]
    ordered = jnp.take(features, curve_order - rank_blk * features.shape[0], axis=0, mode="clip")
    count = degrees.astype(jnp.float32)
    inv_root = lax.rsqrt(count)[:, None]
    wide = jnp.broadcast_to(inv_root, features.shape)
    root = jnp.broadcast_to(count[:, None], features.shape) * wide
    scales = [pack(wide * wide, chain) for chain in range(CHAINS)]
    source = tile_cols // rows
    distance = jnp.clip(jnp.mod(rank_blk - rank_rep * span - source, cycle), 0, span - 1)
    live = jnp.arange(slots, dtype=jnp.int32)[None, :] < tile_counts
    slot_index = jnp.where(live, distance * rows + tile_cols % rows, span * rows)
    tiles = tile_parts(tile_values)

    def partials(owns):
        out = []
        for chain, own in enumerate(owns):
            arrays, places = window(own)
            size = rows * HALF
            homes = tuple((which, at * size + b * HALF) for which, at in places for b in range(rows))
            out.append(product(slot_index, tiles, scales[chain], arrays, homes))
        return out

    def core_pair(part):
        return part + send(part, lambda p, w: (p, w ^ 1))

    def near_chip(part):
        return part + send(part, lambda p, w: (p, w ^ 2))

    def align(pair_sum):
        same = send(pair_sum, lambda p, w: (p + span * w, w))

        def other(p, v):
            w = 6 - (v & 6) + (v & 1)
            return p + span * w, w

        return same + send(pair_sum, other)

    sent = wide * ordered
    owns = [send(pack(sent, chain), lambda p, w: (p + span * w, w)) for chain in range(CHAINS)]
    kept = []
    for hop in range(HOPS):
        parts = partials(owns)
        sums = [near_chip(core_pair(part)) for part in parts]
        if hop < HOPS - 1:
            owns = [align(s) for s in sums]
            kept += owns
    last = [s + send(s, lambda p, w: (p, w ^ 4)) for s in sums]
    size = rows * HALF
    back = send(jnp.concatenate(kept), lambda p, w: (p - span * w, w))
    fields = [back[n * size:(n + 1) * size] for n in range(len(kept))] + last
    return finish(ordered, root, fields)


def solution(mesh):
    return jax.shard_map(
        local,
        mesh=mesh,
        in_specs=(
            P("blk", None),
            P("blk", "rep", None, None),
            P("blk", "rep"),
            P("blk", "rep"),
            P("blk"),
            P("blk"),
        ),
        out_specs=P(None, "blk", None),
        check_vma=False,
    )
```

time: 803 us -> 357 us (0.44)
  waiting for transfers between devices: 626 us -> 42.3 us
  starting transfers between devices: 90.4 us -> 287 us
  local copies, waits for them, and re-layouts: 35.5 us -> 4.5 us
  matrix products: 20.7 us -> 0 us
  Pallas kernels: 0 us -> 16.6 us
  between operations: 13.7 us -> 1.32 us
  other arithmetic: 14 us -> 3.28 us
    psum x4 -> x0, waiting for transfers between devices: 325 us -> none  [local(): summed = lax.psum(partial_value.reshape(row_count, feat_width), 'rep')]
    ppermute x40 -> x73, waiting for transfers between devices: 301 us -> 42.3 us  [send(): return lax.ppermute(block, ('blk', 'rep'), route)]
    ppermute x40 -> x73, starting transfers between devices: 90.2 us -> 287 us  [send(): return lax.ppermute(block, ('blk', 'rep'), route)]
    dot_general x4 -> x0, matrix products: 20.7 us -> none  [local(): jnp.einsum('isab,isbc->iac', tile_values, gathered, precision=lax.Precisi...]
    pallas_call x0 -> x10, Pallas kernels: none -> 16.6 us  [the longest x8 14.9 us: product(): pl.pallas_call(functools.partial(product_kernel, homes, rows, slots), in_...]
    unnamed x38 -> x10, local copies, waits for them, and re-layouts: 16.5 us -> 0.23 us
    gather x5 -> x2, local copies, waits for them, and re-layouts: 16.1 us -> 1.36 us  [local(): jnp.take(features, curve_order - rank_blk * features.shape[0], axis=0, mo...]
  transfers between devices with their start and end apart: 44 -> 73, of which waited for: 44 -> 15; matrix products, arithmetic and copies ran while one was open for 2% -> 1% of each run, Pallas kernels for 0% -> 4%
where the time goes in v1:
time: 357 us; the launch traced here: 355 us
  starting transfers between devices  287 us (80%)
  waiting for transfers between devices  42.3 us (12%)
  Pallas kernels  16.6 us (5%)
  local copies, waits for them, and re-layouts  4.5 us (1%)
    ppermute x73, starting transfers between devices, send(): return lax.ppermute(block, ('blk', 'rep'), route)  287 us
    ppermute x73, waiting for transfers between devices, send(): return lax.ppermute(block, ('blk', 'rep'), route)  42.3 us
    pallas_call x8, Pallas kernels, product(): pl.pallas_call(functools.partial(product_kernel, homes, rows, slots), in_...  14.9 us
  transfers between devices with their start and end apart: 73, of which 15 were waited for; matrix products, arithmetic and copies ran while one was open for 1% of the time, Pallas kernels for 4%

profile of v1, /device:TPU:1, one launch (start us, length us, event | category | flops | bytes accessed | tf_op | source)
XLA Modules:
  0.0 354.6 jit_solution(16031381670260388281)
XLA Ops:
  3.2 4.8 %collective-permute-start.10 = (f32[192,128]{1,0:T(8,128)S(1)}, f32[192,128]{1,0:T(8,128)S(1)}, u32[]{:S(2)}, u32[]{:S(2)}) collective-permute-start(f32[192,128]{1,0:T(8,128)S(1)} %reshape.27), channel_id=1, source_target_pairs={{0,0},{1,65},{2,130},{3,195},{4,260},{5,325},{6,390},{7,455},{8,8}... | collective-permute-start | bytes 294920 | tf_op jit(solution)/shard_map/ppermute | solution.py:22
  8.1 2.2 collective-permute-start
  12.2 7.4 %collective-permute-start.12 = (f32[192,128]{1,0:T(8,128)S(1)}, f32[192,128]{1,0:T(8,128)S(1)}, u32[]{:S(2)}, u32[]{:S(2)}) collective-permute-start(f32[192,128]{1,0:T(8,128)S(1)} %collective-permute-done.10.refs_0_), channel_id=1, source_target_pairs={{0,32},{1,33},{2,34},{3,35},{4,36},{5,37},{6,38},{7,39},{8,40},{9,... | collective-permute-start | bytes 294920 | tf_op jit(solution)/shard_map/ppermute | solution.py:22
  19.6 2.2 collective-permute-start.13
  22.8 5.6 %collective-permute-start.2 = (f32[192,128]{1,0:T(8,128)S(1)}, f32[192,128]{1,0:T(8,128)S(1)}, u32[]{:S(2)}, u32[]{:S(2)}) collective-permute-start(f32[192,128]{1,0:T(8,128)S(1)} %collective-permute-done.refs_0_), channel_id=1, source_target_pairs={{0,32},{1,33},{2,34},{3,35},{4,36},{5,37},{6,38},{7,39},{8,40},{9,... | collective-permute-start | bytes 294920 | tf_op jit(solution)/shard_map/ppermute | solution.py:22
  28.4 3.8 %collective-permute-start.3 = (f32[192,128]{1,0:T(8,128)S(1)}, f32[192,128]{1,0:T(8,128)S(1)}, u32[]{:S(2)}, u32[]{:S(2)}) collective-permute-start(f32[192,128]{1,0:T(8,128)S(1)} %collective-permute-done.refs_0_), channel_id=1, source_target_pairs={{0,48},{1,49},{2,50},{3,51},{4,52},{5,53},{6,54},{7,55},{8,56},{9,... | collective-permute-start | bytes 294920 | tf_op jit(solution)/shard_map/ppermute | solution.py:22
  32.2 2.4 collective-permute-start.1
  35.4 2.3 collective-permute-start.14
  37.7 7.2 %collective-permute-start.15 = (f32[384,128]{1,0:T(8,128)}, f32[384,128]{1,0:T(8,128)}, u32[]{:S(2)}, u32[]{:S(2)}) collective-permute-start(f32[384,128]{1,0:T(8,128)} %get-tuple-element.37), channel_id=1, source_target_pairs={{0,504},{1,505},{2,506},{3,507},{4,508},{5,509},{6,510},{7,511},{8... | collective-permute-start | bytes 589832 | tf_op jit(solution)/shard_map/ppermute | solution.py:22
  47.6 7.6 %collective-permute-start.5 = (f32[384,128]{1,0:T(8,128)}, f32[384,128]{1,0:T(8,128)}, u32[]{:S(2)}, u32[]{:S(2)}) collective-permute-start(f32[384,128]{1,0:T(8,128)} %get-tuple-element.39), channel_id=1, source_target_pairs={{0,504},{1,505},{2,506},{3,507},{4,508},{5,509},{6,510},{7,511},{8... | collective-permute-start | bytes 589832 | tf_op jit(solution)/shard_map/ppermute | solution.py:22
  58.8 2.2 shard_map.65
  61.0 1.9 collective-permute-start.6
  63.0 3.9 %collective-permute-done.11.refs_1_ = f32[192,128]{1,0:T(8,128)S(1)} collective-permute-done((f32[192,128]{1,0:T(8,128)S(1)}, f32[192,128]{1,0:T(8,128)S(1)}, u32[]{:S(2)}, u32[]{:S(2)}) %collective-permute-start.11) | collective-permute-done | bytes 98336 | tf_op jit(solution)/shard_map/ppermute | solution.py:22
  66.9 2.2 shard_map.66
  69.1 1.9 collective-permute-start.16
  71.1 10.4 %collective-permute-start.7 = (f32[192,128]{1,0:T(8,128)S(1)}, f32[192,128]{1,0:T(8,128)S(1)}, u32[]{:S(2)}, u32[]{:S(2)}) collective-permute-start(f32[192,128]{1,0:T(8,128)S(1)} %add.89), channel_id=1, source_target_pairs={{0,2},{1,3},{2,0},{3,1},{4,6},{5,7},{6,4},{7,5},{8,10},{9,11},{10,... | collective-permute-start | bytes 294920 | tf_op jit(solution)/shard_map/ppermute | solution.py:22
  81.5 1.9 collective-permute-start.17
  83.5 3.3 collective-permute-done.7
  86.8 1.9 collective-permute-start.8
  88.7 6.5 %collective-permute-start.9 = (f32[192,128]{1,0:T(8,128)S(1)}, f32[192,128]{1,0:T(8,128)S(1)}, u32[]{:S(2)}, u32[]{:S(2)}) collective-permute-start(f32[192,128]{1,0:T(8,128)S(1)} %add.90), channel_id=1, source_target_pairs={{0,390},{1,455},{2,260},{3,325},{4,130},{5,195},{6,0},{7,65},{8,39... | collective-permute-start | bytes 294920 | tf_op jit(solution)/shard_map/ppermute | solution.py:22
  95.3 4.0 %collective-permute-start.18 = (f32[192,128]{1,0:T(8,128)S(1)}, f32[192,128]{1,0:T(8,128)S(1)}, u32[]{:S(2)}, u32[]{:S(2)}) collective-permute-start(f32[192,128]{1,0:T(8,128)S(1)} %add.93), channel_id=1, source_target_pairs={{0,0},{1,65},{2,130},{3,195},{4,260},{5,325},{6,390},{7,455},{8,8}... | collective-permute-start | bytes 294920 | tf_op jit(solution)/shard_map/ppermute | solution.py:22
  99.2 2.4 collective-permute-start.19
  103.6 5.2 %collective-permute-start.22 = (f32[192,128]{1,0:T(8,128)S(1)}, f32[192,128]{1,0:T(8,128)S(1)}, u32[]{:S(2)}, u32[]{:S(2)}) collective-permute-start(f32[192,128]{1,0:T(8,128)S(1)} %get-tuple-element.16.refs_0_), channel_id=1, source_target_pairs={{0,48},{1,49},{2,50},{3,51},{4,52},{5,53},{6,54},{7,55},{8,56},{9,... | collective-permute-start | bytes 294920 | tf_op jit(solution)/shard_map/ppermute | solution.py:22
  109.0 6.8 %collective-permute-start.30 = (f32[192,128]{1,0:T(8,128)S(1)}, f32[192,128]{1,0:T(8,128)S(1)}, u32[]{:S(2)}, u32[]{:S(2)}) collective-permute-start(f32[192,128]{1,0:T(8,128)S(1)} %get-tuple-element.14.refs_0_), channel_id=1, source_target_pairs={{0,32},{1,33},{2,34},{3,35},{4,36},{5,37},{6,38},{7,39},{8,40},{9,... | collective-permute-start | bytes 294920 | tf_op jit(solution)/shard_map/ppermute | solution.py:22
  117.8 5.4 %collective-permute-start.20 = (f32[192,128]{1,0:T(8,128)S(1)}, f32[192,128]{1,0:T(8,128)S(1)}, u32[]{:S(2)}, u32[]{:S(2)}) collective-permute-start(f32[192,128]{1,0:T(8,128)S(1)} %get-tuple-element.16.refs_0_), channel_id=1, source_target_pairs={{0,16},{1,17},{2,18},{3,19},{4,20},{5,21},{6,22},{7,23},{8,24},{9,... | collective-permute-start | bytes 294920 | tf_op jit(solution)/shard_map/ppermute | solution.py:22
  123.3 2.6 collective-permute-start.23
  125.8 7.0 %collective-permute-start.24 = (f32[384,128]{1,0:T(8,128)S(1)}, f32[384,128]{1,0:T(8,128)S(1)}, u32[]{:S(2)}, u32[]{:S(2)}) collective-permute-start(f32[384,128]{1,0:T(8,128)S(1)} %get-tuple-element.35), channel_id=1, source_target_pairs={{0,504},{1,505},{2,506},{3,507},{4,508},{5,509},{6,510},{7,511},{8... | collective-permute-start | bytes 589832 | tf_op jit(solution)/shard_map/ppermute | solution.py:22
  134.8 7.6 %collective-permute-start.33 = (f32[384,128]{1,0:T(8,128)S(1)}, f32[384,128]{1,0:T(8,128)S(1)}, u32[]{:S(2)}, u32[]{:S(2)}) collective-permute-start(f32[384,128]{1,0:T(8,128)S(1)} %get-tuple-element.33), channel_id=1, source_target_pairs={{0,504},{1,505},{2,506},{3,507},{4,508},{5,509},{6,510},{7,511},{8... | collective-permute-start | bytes 589832 | tf_op jit(solution)/shard_map/ppermute | solution.py:22
  148.0 5.9 %collective-permute-done.29.refs_1_ = f32[192,128]{1,0:T(8,128)S(1)} collective-permute-done((f32[192,128]{1,0:T(8,128)S(1)}, f32[192,128]{1,0:T(8,128)S(1)}, u32[]{:S(2)}, u32[]{:S(2)}) %collective-permute-start.29) | collective-permute-done | bytes 98336 | tf_op jit(solution)/shard_map/ppermute | solution.py:22
  155.6 2.6 collective-permute-start.34
  158.3 5.3 %collective-permute-start.26 = (f32[192,128]{1,0:T(8,128)S(1)}, f32[192,128]{1,0:T(8,128)S(1)}, u32[]{:S(2)}, u32[]{:S(2)}) collective-permute-start(f32[192,128]{1,0:T(8,128)S(1)} %add.95), channel_id=1, source_target_pairs={{0,2},{1,3},{2,0},{3,1},{4,6},{5,7},{6,4},{7,5},{8,10},{9,11},{10,... | collective-permute-start | bytes 294920 | tf_op jit(solution)/shard_map/ppermute | solution.py:22
  165.5 2.9 collective-permute-done.26
  170.4 4.4 %collective-permute-start.28 = (f32[192,128]{1,0:T(8,128)S(1)}, f32[192,128]{1,0:T(8,128)S(1)}, u32[]{:S(2)}, u32[]{:S(2)}) collective-permute-start(f32[192,128]{1,0:T(8,128)S(1)} %add.96), channel_id=1, source_target_pairs={{0,390},{1,455},{2,260},{3,325},{4,130},{5,195},{6,0},{7,65},{8,39... | collective-permute-start | bytes 294920 | tf_op jit(solution)/shard_map/ppermute | solution.py:22
  174.9 3.4 collective-permute-start.36
  178.3 5.0 %collective-permute-start.37 = (f32[192,128]{1,0:T(8,128)S(1)}, f32[192,128]{1,0:T(8,128)S(1)}, u32[]{:S(2)}, u32[]{:S(2)}) collective-permute-start(f32[192,128]{1,0:T(8,128)S(1)} %add.99), channel_id=1, source_target_pairs={{0,390},{1,455},{2,260},{3,325},{4,130},{5,195},{6,0},{7,65},{8,39... | collective-permute-start | bytes 294920 | tf_op jit(solution)/shard_map/ppermute | solution.py:22
  185.3 2.4 collective-permute-start.40
  188.1 6.6 %collective-permute-start.48 = (f32[192,128]{1,0:T(8,128)S(1)}, f32[192,128]{1,0:T(8,128)S(1)}, u32[]{:S(2)}, u32[]{:S(2)}) collective-permute-start(f32[192,128]{1,0:T(8,128)S(1)} %get-tuple-element.10.refs_0_), channel_id=1, source_target_pairs={{0,32},{1,33},{2,34},{3,35},{4,36},{5,37},{6,38},{7,39},{8,40},{9,... | collective-permute-start | bytes 294920 | tf_op jit(solution)/shard_map/ppermute | solution.py:22
  196.6 5.4 %collective-permute-start.38 = (f32[192,128]{1,0:T(8,128)S(1)}, f32[192,128]{1,0:T(8,128)S(1)}, u32[]{:S(2)}, u32[]{:S(2)}) collective-permute-start(f32[192,128]{1,0:T(8,128)S(1)} %get-tuple-element.12.refs_0_), channel_id=1, source_target_pairs={{0,16},{1,17},{2,18},{3,19},{4,20},{5,21},{6,22},{7,23},{8,24},{9,... | collective-permute-start | bytes 294920 | tf_op jit(solution)/shard_map/ppermute | solution.py:22
  204.1 7.6 %collective-permute-start.42 = (f32[384,128]{1,0:T(8,128)S(1)}, f32[384,128]{1,0:T(8,128)S(1)}, u32[]{:S(2)}, u32[]{:S(2)}) collective-permute-start(f32[384,128]{1,0:T(8,128)S(1)} %get-tuple-element.31), channel_id=1, source_target_pairs={{0,504},{1,505},{2,506},{3,507},{4,508},{5,509},{6,510},{7,511},{8... | collective-permute-start | bytes 589832 | tf_op jit(solution)/shard_map/ppermute | solution.py:22
  211.7 1.9 collective-permute-start.50
  213.6 7.6 %collective-permute-start.51 = (f32[384,128]{1,0:T(8,128)S(1)}, f32[384,128]{1,0:T(8,128)S(1)}, u32[]{:S(2)}, u32[]{:S(2)}) collective-permute-start(f32[384,128]{1,0:T(8,128)S(1)} %get-tuple-element.29), channel_id=1, source_target_pairs={{0,504},{1,505},{2,506},{3,507},{4,508},{5,509},{6,510},{7,511},{8... | collective-permute-start | bytes 589832 | tf_op jit(solution)/shard_map/ppermute | solution.py:22
  224.9 2.2 collective-permute-start.43
  227.2 5.3 %collective-permute-done.47.refs_1_ = f32[192,128]{1,0:T(8,128)S(1)} collective-permute-done((f32[192,128]{1,0:T(8,128)S(1)}, f32[192,128]{1,0:T(8,128)S(1)}, u32[]{:S(2)}, u32[]{:S(2)}) %collective-permute-start.47) | collective-permute-done | bytes 98336 | tf_op jit(solution)/shard_map/ppermute | solution.py:22
  234.3 2.9 collective-permute-start.52
  237.2 6.1 %collective-permute-start.44 = (f32[192,128]{1,0:T(8,128)S(1)}, f32[192,128]{1,0:T(8,128)S(1)}, u32[]{:S(2)}, u32[]{:S(2)}) collective-permute-start(f32[192,128]{1,0:T(8,128)S(1)} %add.101), channel_id=1, source_target_pairs={{0,2},{1,3},{2,0},{3,1},{4,6},{5,7},{6,4},{7,5},{8,10},{9,11},{10,... | collective-permute-start | bytes 294920 | tf_op jit(solution)/shard_map/ppermute | solution.py:22
  245.2 3.3 collective-permute-done.44
  250.4 2.8 collective-permute-start.46
  253.3 4.1 %collective-permute-start.54 = (f32[192,128]{1,0:T(8,128)S(1)}, f32[192,128]{1,0:T(8,128)S(1)}, u32[]{:S(2)}, u32[]{:S(2)}) collective-permute-start(f32[192,128]{1,0:T(8,128)S(1)} %add.105), channel_id=1, source_target_pairs={{0,0},{1,65},{2,130},{3,195},{4,260},{5,325},{6,390},{7,455},{8,8}... | collective-permute-start | bytes 294920 | tf_op jit(solution)/shard_map/ppermute | solution.py:22
  257.4 5.9 %collective-permute-start.55 = (f32[192,128]{1,0:T(8,128)S(1)}, f32[192,128]{1,0:T(8,128)S(1)}, u32[]{:S(2)}, u32[]{:S(2)}) collective-permute-start(f32[192,128]{1,0:T(8,128)S(1)} %add.105), channel_id=1, source_target_pairs={{0,390},{1,455},{2,260},{3,325},{4,130},{5,195},{6,0},{7,65},{8,39... | collective-permute-start | bytes 294920 | tf_op jit(solution)/shard_map/ppermute | solution.py:22
  263.4 3.6 %collective-permute-done.55 = f32[192,128]{1,0:T(8,128)S(1)} collective-permute-done((f32[192,128]{1,0:T(8,128)S(1)}, f32[192,128]{1,0:T(8,128)S(1)}, u32[]{:S(2)}, u32[]{:S(2)}) %collective-permute-start.55) | collective-permute-done | bytes 98336 | tf_op jit(solution)/shard_map/ppermute | solution.py:22
  269.0 2.7 collective-permute-start.67
  271.7 3.9 %collective-permute-start.65 = (f32[192,128]{1,0:T(8,128)S(1)}, f32[192,128]{1,0:T(8,128)S(1)}, u32[]{:S(2)}, u32[]{:S(2)}) collective-permute-start(f32[192,128]{1,0:T(8,128)S(1)} %get-tuple-element.6.refs_0_), channel_id=1, source_target_pairs={{0,16},{1,17},{2,18},{3,19},{4,20},{5,21},{6,22},{7,23},{8,24},{9,... | collective-permute-start | bytes 294920 | tf_op jit(solution)/shard_map/ppermute | solution.py:22
  275.6 6.1 %collective-permute-start.58 = (f32[192,128]{1,0:T(8,128)S(1)}, f32[192,128]{1,0:T(8,128)S(1)}, u32[]{:S(2)}, u32[]{:S(2)}) collective-permute-start(f32[192,128]{1,0:T(8,128)S(1)} %get-tuple-element.8.refs_0_), channel_id=1, source_target_pairs={{0,32},{1,33},{2,34},{3,35},{4,36},{5,37},{6,38},{7,39},{8,40},{9,... | collective-permute-start | bytes 294920 | tf_op jit(solution)/shard_map/ppermute | solution.py:22
  281.7 3.1 collective-permute-start.59
  284.8 5.9 %collective-permute-start.56 = (f32[1152,128]{1,0:T(8,128)S(1)}, f32[1152,128]{1,0:T(8,128)S(1)}, u32[]{:S(2)}, u32[]{:S(2)}) collective-permute-start(f32[1152,128]{1,0:T(8,128)S(1)} %get-tuple-element.5), channel_id=1, source_target_pairs={{0,0},{1,449},{2,386},{3,323},{4,260},{5,197},{6,134},{7,71},{8,8}... | collective-permute-start | bytes 1769480 | tf_op jit(solution)/shard_map/ppermute | solution.py:22
  290.8 2.0 collective-permute-start.68
  292.8 7.5 %collective-permute-start.69 = (f32[384,128]{1,0:T(8,128)S(1)}, f32[384,128]{1,0:T(8,128)S(1)}, u32[]{:S(2)}, u32[]{:S(2)}) collective-permute-start(f32[384,128]{1,0:T(8,128)S(1)} %get-tuple-element.25), channel_id=1, source_target_pairs={{0,504},{1,505},{2,506},{3,507},{4,508},{5,509},{6,510},{7,511},{8... | collective-permute-start | bytes 589832 | tf_op jit(solution)/shard_map/ppermute | solution.py:22
  300.4 1.9 collective-permute-start.60
  302.3 7.6 %collective-permute-start.61 = (f32[384,128]{1,0:T(8,128)S(1)}, f32[384,128]{1,0:T(8,128)S(1)}, u32[]{:S(2)}, u32[]{:S(2)}) collective-permute-start(f32[384,128]{1,0:T(8,128)S(1)} %get-tuple-element.27), channel_id=1, source_target_pairs={{0,504},{1,505},{2,506},{3,507},{4,508},{5,509},{6,510},{7,511},{8... | collective-permute-start | bytes 589832 | tf_op jit(solution)/shard_map/ppermute | solution.py:22
  315.5 4.9 %collective-permute-done.57.refs_1_ = f32[192,128]{1,0:T(8,128)S(1)} collective-permute-done((f32[192,128]{1,0:T(8,128)S(1)}, f32[192,128]{1,0:T(8,128)S(1)}, u32[]{:S(2)}, u32[]{:S(2)}) %collective-permute-start.57) | collective-permute-done | bytes 98336 | tf_op jit(solution)/shard_map/ppermute | solution.py:22
  324.1 11.8 %collective-permute-start.71 = (f32[192,128]{1,0:T(8,128)S(1)}, f32[192,128]{1,0:T(8,128)S(1)}, u32[]{:S(2)}, u32[]{:S(2)}) collective-permute-start(f32[192,128]{1,0:T(8,128)S(1)} %add.110), channel_id=1, source_target_pairs={{0,2},{1,3},{2,0},{3,1},{4,6},{5,7},{6,4},{7,5},{8,10},{9,11},{10,... | collective-permute-start | bytes 294920 | tf_op jit(solution)/shard_map/ppermute | solution.py:22
  339.1 3.8 %collective-permute-start.72 = (f32[192,128]{1,0:T(8,128)S(1)}, f32[192,128]{1,0:T(8,128)S(1)}, u32[]{:S(2)}, u32[]{:S(2)}) collective-permute-start(f32[192,128]{1,0:T(8,128)S(1)} %add.111), channel_id=1, source_target_pairs={{0,4},{1,5},{2,6},{3,7},{4,0},{5,1},{6,2},{7,3},{8,12},{9,13},{10,... | collective-permute-start | bytes 294920 | tf_op jit(solution)/shard_map/ppermute | solution.py:22
  343.9 4.5 %collective-permute-start.64 = (f32[192,128]{1,0:T(8,128)S(1)}, f32[192,128]{1,0:T(8,128)S(1)}, u32[]{:S(2)}, u32[]{:S(2)}) collective-permute-start(f32[192,128]{1,0:T(8,128)S(1)} %add.108), channel_id=1, source_target_pairs={{0,4},{1,5},{2,6},{3,7},{4,0},{5,1},{6,2},{7,3},{8,12},{9,13},{10,... | collective-permute-start | bytes 294920 | tf_op jit(solution)/shard_map/ppermute | solution.py:22
  348.4 2.9 collective-permute-done.72
  (152 shorter events, 64.6 us)
Async XLA Ops:
  8.1 14.6 %collective-permute-start = (f32[192,128]{1,0:T(8,128)S(1)}, f32[192,128]{1,0:T(8,128)S(1)}, u32[]{:S(2)}, u32[]{:S(2)}) collective-permute-start(f32[192,128]{1,0:T(8,128)S(1)} %reshape.26), channel_id=1, source_target_pairs={{0,0},{1,65},{2,130},{3,195},{4,260},{5,325},{6,390},{7,455},{8,8}... | collective-permute-start | bytes 294920 | tf_op jit(solution)/shard_map/ppermute | solution.py:22
  12.2 22.4 %collective-permute-start.12 = (f32[192,128]{1,0:T(8,128)S(1)}, f32[192,128]{1,0:T(8,128)S(1)}, u32[]{:S(2)}, u32[]{:S(2)}) collective-permute-start(f32[192,128]{1,0:T(8,128)S(1)} %collective-permute-done.10.refs_0_), channel_id=1, source_target_pairs={{0,32},{1,33},{2,34},{3,35},{4,36},{5,37},{6,38},{7,39},{8,40},{9,... | collective-permute-start | bytes 294920 | tf_op jit(solution)/shard_map/ppermute | solution.py:22
  19.6 15.0 %collective-permute-start.13 = (f32[192,128]{1,0:T(8,128)S(1)}, f32[192,128]{1,0:T(8,128)S(1)}, u32[]{:S(2)}, u32[]{:S(2)}) collective-permute-start(f32[192,128]{1,0:T(8,128)S(1)} %collective-permute-done.10.refs_0_), channel_id=1, source_target_pairs={{0,48},{1,49},{2,50},{3,51},{4,52},{5,53},{6,54},{7,55},{8,56},{9,... | collective-permute-start | bytes 294920 | tf_op jit(solution)/shard_map/ppermute | solution.py:22
  22.8 22.2 %collective-permute-start.2 = (f32[192,128]{1,0:T(8,128)S(1)}, f32[192,128]{1,0:T(8,128)S(1)}, u32[]{:S(2)}, u32[]{:S(2)}) collective-permute-start(f32[192,128]{1,0:T(8,128)S(1)} %collective-permute-done.refs_0_), channel_id=1, source_target_pairs={{0,32},{1,33},{2,34},{3,35},{4,36},{5,37},{6,38},{7,39},{8,40},{9,... | collective-permute-start | bytes 294920 | tf_op jit(solution)/shard_map/ppermute | solution.py:22
  28.4 16.5 %collective-permute-start.3 = (f32[192,128]{1,0:T(8,128)S(1)}, f32[192,128]{1,0:T(8,128)S(1)}, u32[]{:S(2)}, u32[]{:S(2)}) collective-permute-start(f32[192,128]{1,0:T(8,128)S(1)} %collective-permute-done.refs_0_), channel_id=1, source_target_pairs={{0,48},{1,49},{2,50},{3,51},{4,52},{5,53},{6,54},{7,55},{8,56},{9,... | collective-permute-start | bytes 294920 | tf_op jit(solution)/shard_map/ppermute | solution.py:22
  32.2 24.2 %collective-permute-start.1 = (f32[192,128]{1,0:T(8,128)S(1)}, f32[192,128]{1,0:T(8,128)S(1)}, u32[]{:S(2)}, u32[]{:S(2)}) collective-permute-start(f32[192,128]{1,0:T(8,128)S(1)} %collective-permute-done.refs_0_), channel_id=1, source_target_pairs={{0,16},{1,17},{2,18},{3,19},{4,20},{5,21},{6,22},{7,23},{8,24},{9,... | collective-permute-start | bytes 294920 | tf_op jit(solution)/shard_map/ppermute | solution.py:22
  35.4 31.5 %collective-permute-start.14 = (f32[384,128]{1,0:T(8,128)}, f32[384,128]{1,0:T(8,128)}, u32[]{:S(2)}, u32[]{:S(2)}) collective-permute-start(f32[384,128]{1,0:T(8,128)} %get-tuple-element.38), channel_id=1, source_target_pairs={{0,8},{1,9},{2,10},{3,11},{4,12},{5,13},{6,14},{7,15},{8,16},{9,17... | collective-permute-start | bytes 589832 | tf_op jit(solution)/shard_map/ppermute | solution.py:22
  37.7 29.2 %collective-permute-start.15 = (f32[384,128]{1,0:T(8,128)}, f32[384,128]{1,0:T(8,128)}, u32[]{:S(2)}, u32[]{:S(2)}) collective-permute-start(f32[384,128]{1,0:T(8,128)} %get-tuple-element.37), channel_id=1, source_target_pairs={{0,504},{1,505},{2,506},{3,507},{4,508},{5,509},{6,510},{7,511},{8... | collective-permute-start | bytes 589832 | tf_op jit(solution)/shard_map/ppermute | solution.py:22
  45.7 13.1 %collective-permute-start.4 = (f32[384,128]{1,0:T(8,128)}, f32[384,128]{1,0:T(8,128)}, u32[]{:S(2)}, u32[]{:S(2)}) collective-permute-start(f32[384,128]{1,0:T(8,128)} %get-tuple-element.40), channel_id=1, source_target_pairs={{0,8},{1,9},{2,10},{3,11},{4,12},{5,13},{6,14},{7,15},{8,16},{9,17... | collective-permute-start | bytes 589832 | tf_op jit(solution)/shard_map/ppermute | solution.py:22
  47.6 11.2 %collective-permute-start.5 = (f32[384,128]{1,0:T(8,128)}, f32[384,128]{1,0:T(8,128)}, u32[]{:S(2)}, u32[]{:S(2)}) collective-permute-start(f32[384,128]{1,0:T(8,128)} %get-tuple-element.39), channel_id=1, source_target_pairs={{0,504},{1,505},{2,506},{3,507},{4,508},{5,509},{6,510},{7,511},{8... | collective-permute-start | bytes 589832 | tf_op jit(solution)/shard_map/ppermute | solution.py:22
  56.4 10.5 %collective-permute-start.11 = (f32[192,128]{1,0:T(8,128)S(1)}, f32[192,128]{1,0:T(8,128)S(1)}, u32[]{:S(2)}, u32[]{:S(2)}) collective-permute-start(f32[192,128]{1,0:T(8,128)S(1)} %collective-permute-done.10.refs_0_), channel_id=1, source_target_pairs={{0,16},{1,17},{2,18},{3,19},{4,20},{5,21},{6,22},{7,23},{8,24},{9,... | collective-permute-start | bytes 294920 | tf_op jit(solution)/shard_map/ppermute | solution.py:22
  61.0 10.0 %collective-permute-start.6 = (f32[192,128]{1,0:T(8,128)S(1)}, f32[192,128]{1,0:T(8,128)S(1)}, u32[]{:S(2)}, u32[]{:S(2)}) collective-permute-start(f32[192,128]{1,0:T(8,128)S(1)} %shard_map.65), channel_id=1, source_target_pairs={{0,1},{1,0},{2,3},{3,2},{4,5},{5,4},{6,7},{7,6},{8,9},{9,8},{10,11... | collective-permute-start | bytes 294920 | tf_op jit(solution)/shard_map/ppermute | solution.py:22
  69.1 12.4 %collective-permute-start.16 = (f32[192,128]{1,0:T(8,128)S(1)}, f32[192,128]{1,0:T(8,128)S(1)}, u32[]{:S(2)}, u32[]{:S(2)}) collective-permute-start(f32[192,128]{1,0:T(8,128)S(1)} %shard_map.66), channel_id=1, source_target_pairs={{0,1},{1,0},{2,3},{3,2},{4,5},{5,4},{6,7},{7,6},{8,9},{9,8},{10,11... | collective-permute-start | bytes 294920 | tf_op jit(solution)/shard_map/ppermute | solution.py:22
  71.1 15.7 %collective-permute-start.7 = (f32[192,128]{1,0:T(8,128)S(1)}, f32[192,128]{1,0:T(8,128)S(1)}, u32[]{:S(2)}, u32[]{:S(2)}) collective-permute-start(f32[192,128]{1,0:T(8,128)S(1)} %add.89), channel_id=1, source_target_pairs={{0,2},{1,3},{2,0},{3,1},{4,6},{5,7},{6,4},{7,5},{8,10},{9,11},{10,... | collective-permute-start | bytes 294920 | tf_op jit(solution)/shard_map/ppermute | solution.py:22
  81.5 13.7 %collective-permute-start.17 = (f32[192,128]{1,0:T(8,128)S(1)}, f32[192,128]{1,0:T(8,128)S(1)}, u32[]{:S(2)}, u32[]{:S(2)}) collective-permute-start(f32[192,128]{1,0:T(8,128)S(1)} %add.92), channel_id=1, source_target_pairs={{0,2},{1,3},{2,0},{3,1},{4,6},{5,7},{6,4},{7,5},{8,10},{9,11},{10,... | collective-permute-start | bytes 294920 | tf_op jit(solution)/shard_map/ppermute | solution.py:22
  86.8 14.8 %collective-permute-start.8 = (f32[192,128]{1,0:T(8,128)S(1)}, f32[192,128]{1,0:T(8,128)S(1)}, u32[]{:S(2)}, u32[]{:S(2)}) collective-permute-start(f32[192,128]{1,0:T(8,128)S(1)} %add.90), channel_id=1, source_target_pairs={{0,0},{1,65},{2,130},{3,195},{4,260},{5,325},{6,390},{7,455},{8,8}... | collective-permute-start | bytes 294920 | tf_op jit(solution)/shard_map/ppermute | solution.py:22
  88.7 12.9 %collective-permute-start.9 = (f32[192,128]{1,0:T(8,128)S(1)}, f32[192,128]{1,0:T(8,128)S(1)}, u32[]{:S(2)}, u32[]{:S(2)}) collective-permute-start(f32[192,128]{1,0:T(8,128)S(1)} %add.90), channel_id=1, source_target_pairs={{0,390},{1,455},{2,260},{3,325},{4,130},{5,195},{6,0},{7,65},{8,39... | collective-permute-start | bytes 294920 | tf_op jit(solution)/shard_map/ppermute | solution.py:22
  95.3 13.5 %collective-permute-start.18 = (f32[192,128]{1,0:T(8,128)S(1)}, f32[192,128]{1,0:T(8,128)S(1)}, u32[]{:S(2)}, u32[]{:S(2)}) collective-permute-start(f32[192,128]{1,0:T(8,128)S(1)} %add.93), channel_id=1, source_target_pairs={{0,0},{1,65},{2,130},{3,195},{4,260},{5,325},{6,390},{7,455},{8,8}... | collective-permute-start | bytes 294920 | tf_op jit(solution)/shard_map/ppermute | solution.py:22
  101.7 21.5 %collective-permute-start.21 = (f32[192,128]{1,0:T(8,128)S(1)}, f32[192,128]{1,0:T(8,128)S(1)}, u32[]{:S(2)}, u32[]{:S(2)}) collective-permute-start(f32[192,128]{1,0:T(8,128)S(1)} %get-tuple-element.16.refs_0_), channel_id=1, source_target_pairs={{0,32},{1,33},{2,34},{3,35},{4,36},{5,37},{6,38},{7,39},{8,40},{9,... | collective-permute-start | bytes 294920 | tf_op jit(solution)/shard_map/ppermute | solution.py:22
  103.6 19.6 %collective-permute-start.22 = (f32[192,128]{1,0:T(8,128)S(1)}, f32[192,128]{1,0:T(8,128)S(1)}, u32[]{:S(2)}, u32[]{:S(2)}) collective-permute-start(f32[192,128]{1,0:T(8,128)S(1)} %get-tuple-element.16.refs_0_), channel_id=1, source_target_pairs={{0,48},{1,49},{2,50},{3,51},{4,52},{5,53},{6,54},{7,55},{8,56},{9,... | collective-permute-start | bytes 294920 | tf_op jit(solution)/shard_map/ppermute | solution.py:22
  109.0 23.8 %collective-permute-start.30 = (f32[192,128]{1,0:T(8,128)S(1)}, f32[192,128]{1,0:T(8,128)S(1)}, u32[]{:S(2)}, u32[]{:S(2)}) collective-permute-start(f32[192,128]{1,0:T(8,128)S(1)} %get-tuple-element.14.refs_0_), channel_id=1, source_target_pairs={{0,32},{1,33},{2,34},{3,35},{4,36},{5,37},{6,38},{7,39},{8,40},{9,... | collective-permute-start | bytes 294920 | tf_op jit(solution)/shard_map/ppermute | solution.py:22
  115.8 17.0 %collective-permute-start.31 = (f32[192,128]{1,0:T(8,128)S(1)}, f32[192,128]{1,0:T(8,128)S(1)}, u32[]{:S(2)}, u32[]{:S(2)}) collective-permute-start(f32[192,128]{1,0:T(8,128)S(1)} %get-tuple-element.14.refs_0_), channel_id=1, source_target_pairs={{0,48},{1,49},{2,50},{3,51},{4,52},{5,53},{6,54},{7,55},{8,56},{9,... | collective-permute-start | bytes 294920 | tf_op jit(solution)/shard_map/ppermute | solution.py:22
  117.8 24.6 %collective-permute-start.20 = (f32[192,128]{1,0:T(8,128)S(1)}, f32[192,128]{1,0:T(8,128)S(1)}, u32[]{:S(2)}, u32[]{:S(2)}) collective-permute-start(f32[192,128]{1,0:T(8,128)S(1)} %get-tuple-element.16.refs_0_), channel_id=1, source_target_pairs={{0,16},{1,17},{2,18},{3,19},{4,20},{5,21},{6,22},{7,23},{8,24},{9,... | collective-permute-start | bytes 294920 | tf_op jit(solution)/shard_map/ppermute | solution.py:22
  123.3 21.0 %collective-permute-start.23 = (f32[384,128]{1,0:T(8,128)S(1)}, f32[384,128]{1,0:T(8,128)S(1)}, u32[]{:S(2)}, u32[]{:S(2)}) collective-permute-start(f32[384,128]{1,0:T(8,128)S(1)} %get-tuple-element.36), channel_id=1, source_target_pairs={{0,8},{1,9},{2,10},{3,11},{4,12},{5,13},{6,14},{7,15},{8,16},{9,17... | collective-permute-start | bytes 589832 | tf_op jit(solution)/shard_map/ppermute | solution.py:22
  125.8 18.5 %collective-permute-start.24 = (f32[384,128]{1,0:T(8,128)S(1)}, f32[384,128]{1,0:T(8,128)S(1)}, u32[]{:S(2)}, u32[]{:S(2)}) collective-permute-start(f32[384,128]{1,0:T(8,128)S(1)} %get-tuple-element.35), channel_id=1, source_target_pairs={{0,504},{1,505},{2,506},{3,507},{4,508},{5,509},{6,510},{7,511},{8... | collective-permute-start | bytes 589832 | tf_op jit(solution)/shard_map/ppermute | solution.py:22
  132.8 21.1 %collective-permute-start.32 = (f32[384,128]{1,0:T(8,128)S(1)}, f32[384,128]{1,0:T(8,128)S(1)}, u32[]{:S(2)}, u32[]{:S(2)}) collective-permute-start(f32[384,128]{1,0:T(8,128)S(1)} %get-tuple-element.34), channel_id=1, source_target_pairs={{0,8},{1,9},{2,10},{3,11},{4,12},{5,13},{6,14},{7,15},{8,16},{9,17... | collective-permute-start | bytes 589832 | tf_op jit(solution)/shard_map/ppermute | solution.py:22
  134.8 19.1 %collective-permute-start.33 = (f32[384,128]{1,0:T(8,128)S(1)}, f32[384,128]{1,0:T(8,128)S(1)}, u32[]{:S(2)}, u32[]{:S(2)}) collective-permute-start(f32[384,128]{1,0:T(8,128)S(1)} %get-tuple-element.33), channel_id=1, source_target_pairs={{0,504},{1,505},{2,506},{3,507},{4,508},{5,509},{6,510},{7,511},{8... | collective-permute-start | bytes 589832 | tf_op jit(solution)/shard_map/ppermute | solution.py:22
  142.4 11.5 %collective-permute-start.29 = (f32[192,128]{1,0:T(8,128)S(1)}, f32[192,128]{1,0:T(8,128)S(1)}, u32[]{:S(2)}, u32[]{:S(2)}) collective-permute-start(f32[192,128]{1,0:T(8,128)S(1)} %get-tuple-element.14.refs_0_), channel_id=1, source_target_pairs={{0,16},{1,17},{2,18},{3,19},{4,20},{5,21},{6,22},{7,23},{8,24},{9,... | collective-permute-start | bytes 294920 | tf_op jit(solution)/shard_map/ppermute | solution.py:22
  146.1 12.2 %collective-permute-start.25 = (f32[192,128]{1,0:T(8,128)S(1)}, f32[192,128]{1,0:T(8,128)S(1)}, u32[]{:S(2)}, u32[]{:S(2)}) collective-permute-start(f32[192,128]{1,0:T(8,128)S(1)} %shard_map.67), channel_id=1, source_target_pairs={{0,1},{1,0},{2,3},{3,2},{4,5},{5,4},{6,7},{7,6},{8,9},{9,8},{10,11... | collective-permute-start | bytes 294920 | tf_op jit(solution)/shard_map/ppermute | solution.py:22
  158.3 10.2 %collective-permute-start.26 = (f32[192,128]{1,0:T(8,128)S(1)}, f32[192,128]{1,0:T(8,128)S(1)}, u32[]{:S(2)}, u32[]{:S(2)}) collective-permute-start(f32[192,128]{1,0:T(8,128)S(1)} %add.95), channel_id=1, source_target_pairs={{0,2},{1,3},{2,0},{3,1},{4,6},{5,7},{6,4},{7,5},{8,10},{9,11},{10,... | collective-permute-start | bytes 294920 | tf_op jit(solution)/shard_map/ppermute | solution.py:22
  163.6 11.3 %collective-permute-start.35 = (f32[192,128]{1,0:T(8,128)S(1)}, f32[192,128]{1,0:T(8,128)S(1)}, u32[]{:S(2)}, u32[]{:S(2)}) collective-permute-start(f32[192,128]{1,0:T(8,128)S(1)} %add.98), channel_id=1, source_target_pairs={{0,2},{1,3},{2,0},{3,1},{4,6},{5,7},{6,4},{7,5},{8,10},{9,11},{10,... | collective-permute-start | bytes 294920 | tf_op jit(solution)/shard_map/ppermute | solution.py:22
  168.5 14.8 %collective-permute-start.27 = (f32[192,128]{1,0:T(8,128)S(1)}, f32[192,128]{1,0:T(8,128)S(1)}, u32[]{:S(2)}, u32[]{:S(2)}) collective-permute-start(f32[192,128]{1,0:T(8,128)S(1)} %add.96), channel_id=1, source_target_pairs={{0,0},{1,65},{2,130},{3,195},{4,260},{5,325},{6,390},{7,455},{8,8}... | collective-permute-start | bytes 294920 | tf_op jit(solution)/shard_map/ppermute | solution.py:22
  170.4 12.9 %collective-permute-start.28 = (f32[192,128]{1,0:T(8,128)S(1)}, f32[192,128]{1,0:T(8,128)S(1)}, u32[]{:S(2)}, u32[]{:S(2)}) collective-permute-start(f32[192,128]{1,0:T(8,128)S(1)} %add.96), channel_id=1, source_target_pairs={{0,390},{1,455},{2,260},{3,325},{4,130},{5,195},{6,0},{7,65},{8,39... | collective-permute-start | bytes 294920 | tf_op jit(solution)/shard_map/ppermute | solution.py:22
  174.9 12.8 %collective-permute-start.36 = (f32[192,128]{1,0:T(8,128)S(1)}, f32[192,128]{1,0:T(8,128)S(1)}, u32[]{:S(2)}, u32[]{:S(2)}) collective-permute-start(f32[192,128]{1,0:T(8,128)S(1)} %add.99), channel_id=1, source_target_pairs={{0,0},{1,65},{2,130},{3,195},{4,260},{5,325},{6,390},{7,455},{8,8}... | collective-permute-start | bytes 294920 | tf_op jit(solution)/shard_map/ppermute | solution.py:22
  183.4 18.7 %collective-permute-start.39 = (f32[192,128]{1,0:T(8,128)S(1)}, f32[192,128]{1,0:T(8,128)S(1)}, u32[]{:S(2)}, u32[]{:S(2)}) collective-permute-start(f32[192,128]{1,0:T(8,128)S(1)} %get-tuple-element.12.refs_0_), channel_id=1, source_target_pairs={{0,32},{1,33},{2,34},{3,35},{4,36},{5,37},{6,38},{7,39},{8,40},{9,... | collective-permute-start | bytes 294920 | tf_op jit(solution)/shard_map/ppermute | solution.py:22
  185.3 16.8 %collective-permute-start.40 = (f32[192,128]{1,0:T(8,128)S(1)}, f32[192,128]{1,0:T(8,128)S(1)}, u32[]{:S(2)}, u32[]{:S(2)}) collective-permute-start(f32[192,128]{1,0:T(8,128)S(1)} %get-tuple-element.12.refs_0_), channel_id=1, source_target_pairs={{0,48},{1,49},{2,50},{3,51},{4,52},{5,53},{6,54},{7,55},{8,56},{9,... | collective-permute-start | bytes 294920 | tf_op jit(solution)/shard_map/ppermute | solution.py:22
  188.1 23.6 %collective-permute-start.48 = (f32[192,128]{1,0:T(8,128)S(1)}, f32[192,128]{1,0:T(8,128)S(1)}, u32[]{:S(2)}, u32[]{:S(2)}) collective-permute-start(f32[192,128]{1,0:T(8,128)S(1)} %get-tuple-element.10.refs_0_), channel_id=1, source_target_pairs={{0,32},{1,33},{2,34},{3,35},{4,36},{5,37},{6,38},{7,39},{8,40},{9,... | collective-permute-start | bytes 294920 | tf_op jit(solution)/shard_map/ppermute | solution.py:22
  194.7 17.0 %collective-permute-start.49 = (f32[192,128]{1,0:T(8,128)S(1)}, f32[192,128]{1,0:T(8,128)S(1)}, u32[]{:S(2)}, u32[]{:S(2)}) collective-permute-start(f32[192,128]{1,0:T(8,128)S(1)} %get-tuple-element.10.refs_0_), channel_id=1, source_target_pairs={{0,48},{1,49},{2,50},{3,51},{4,52},{5,53},{6,54},{7,55},{8,56},{9,... | collective-permute-start | bytes 294920 | tf_op jit(solution)/shard_map/ppermute | solution.py:22
  196.6 24.6 %collective-permute-start.38 = (f32[192,128]{1,0:T(8,128)S(1)}, f32[192,128]{1,0:T(8,128)S(1)}, u32[]{:S(2)}, u32[]{:S(2)}) collective-permute-start(f32[192,128]{1,0:T(8,128)S(1)} %get-tuple-element.12.refs_0_), channel_id=1, source_target_pairs={{0,16},{1,17},{2,18},{3,19},{4,20},{5,21},{6,22},{7,23},{8,24},{9,... | collective-permute-start | bytes 294920 | tf_op jit(solution)/shard_map/ppermute | solution.py:22
  202.1 21.0 %collective-permute-start.41 = (f32[384,128]{1,0:T(8,128)S(1)}, f32[384,128]{1,0:T(8,128)S(1)}, u32[]{:S(2)}, u32[]{:S(2)}) collective-permute-start(f32[384,128]{1,0:T(8,128)S(1)} %get-tuple-element.32), channel_id=1, source_target_pairs={{0,8},{1,9},{2,10},{3,11},{4,12},{5,13},{6,14},{7,15},{8,16},{9,17... | collective-permute-start | bytes 589832 | tf_op jit(solution)/shard_map/ppermute | solution.py:22
  204.1 19.1 %collective-permute-start.42 = (f32[384,128]{1,0:T(8,128)S(1)}, f32[384,128]{1,0:T(8,128)S(1)}, u32[]{:S(2)}, u32[]{:S(2)}) collective-permute-start(f32[384,128]{1,0:T(8,128)S(1)} %get-tuple-element.31), channel_id=1, source_target_pairs={{0,504},{1,505},{2,506},{3,507},{4,508},{5,509},{6,510},{7,511},{8... | collective-permute-start | bytes 589832 | tf_op jit(solution)/shard_map/ppermute | solution.py:22
  211.7 20.8 %collective-permute-start.50 = (f32[384,128]{1,0:T(8,128)S(1)}, f32[384,128]{1,0:T(8,128)S(1)}, u32[]{:S(2)}, u32[]{:S(2)}) collective-permute-start(f32[384,128]{1,0:T(8,128)S(1)} %get-tuple-element.30), channel_id=1, source_target_pairs={{0,8},{1,9},{2,10},{3,11},{4,12},{5,13},{6,14},{7,15},{8,16},{9,17... | collective-permute-start | bytes 589832 | tf_op jit(solution)/shard_map/ppermute | solution.py:22
  213.6 18.9 %collective-permute-start.51 = (f32[384,128]{1,0:T(8,128)S(1)}, f32[384,128]{1,0:T(8,128)S(1)}, u32[]{:S(2)}, u32[]{:S(2)}) collective-permute-start(f32[384,128]{1,0:T(8,128)S(1)} %get-tuple-element.29), channel_id=1, source_target_pairs={{0,504},{1,505},{2,506},{3,507},{4,508},{5,509},{6,510},{7,511},{8... | collective-permute-start | bytes 589832 | tf_op jit(solution)/shard_map/ppermute | solution.py:22
  221.2 11.3 %collective-permute-start.47 = (f32[192,128]{1,0:T(8,128)S(1)}, f32[192,128]{1,0:T(8,128)S(1)}, u32[]{:S(2)}, u32[]{:S(2)}) collective-permute-start(f32[192,128]{1,0:T(8,128)S(1)} %get-tuple-element.10.refs_0_), channel_id=1, source_target_pairs={{0,16},{1,17},{2,18},{3,19},{4,20},{5,21},{6,22},{7,23},{8,24},{9,... | collective-permute-start | bytes 294920 | tf_op jit(solution)/shard_map/ppermute | solution.py:22
  224.9 12.2 %collective-permute-start.43 = (f32[192,128]{1,0:T(8,128)S(1)}, f32[192,128]{1,0:T(8,128)S(1)}, u32[]{:S(2)}, u32[]{:S(2)}) collective-permute-start(f32[192,128]{1,0:T(8,128)S(1)} %shard_map.69), channel_id=1, source_target_pairs={{0,1},{1,0},{2,3},{3,2},{4,5},{5,4},{6,7},{7,6},{8,9},{9,8},{10,11... | collective-permute-start | bytes 294920 | tf_op jit(solution)/shard_map/ppermute | solution.py:22
  237.2 11.3 %collective-permute-start.44 = (f32[192,128]{1,0:T(8,128)S(1)}, f32[192,128]{1,0:T(8,128)S(1)}, u32[]{:S(2)}, u32[]{:S(2)}) collective-permute-start(f32[192,128]{1,0:T(8,128)S(1)} %add.101), channel_id=1, source_target_pairs={{0,2},{1,3},{2,0},{3,1},{4,6},{5,7},{6,4},{7,5},{8,10},{9,11},{10,... | collective-permute-start | bytes 294920 | tf_op jit(solution)/shard_map/ppermute | solution.py:22
  248.5 14.8 %collective-permute-start.45 = (f32[192,128]{1,0:T(8,128)S(1)}, f32[192,128]{1,0:T(8,128)S(1)}, u32[]{:S(2)}, u32[]{:S(2)}) collective-permute-start(f32[192,128]{1,0:T(8,128)S(1)} %add.102), channel_id=1, source_target_pairs={{0,0},{1,65},{2,130},{3,195},{4,260},{5,325},{6,390},{7,455},{8,8}... | collective-permute-start | bytes 294920 | tf_op jit(solution)/shard_map/ppermute | solution.py:22
  250.4 12.9 %collective-permute-start.46 = (f32[192,128]{1,0:T(8,128)S(1)}, f32[192,128]{1,0:T(8,128)S(1)}, u32[]{:S(2)}, u32[]{:S(2)}) collective-permute-start(f32[192,128]{1,0:T(8,128)S(1)} %add.102), channel_id=1, source_target_pairs={{0,390},{1,455},{2,260},{3,325},{4,130},{5,195},{6,0},{7,65},{8,39... | collective-permute-start | bytes 294920 | tf_op jit(solution)/shard_map/ppermute | solution.py:22
  253.3 10.1 %collective-permute-start.54 = (f32[192,128]{1,0:T(8,128)S(1)}, f32[192,128]{1,0:T(8,128)S(1)}, u32[]{:S(2)}, u32[]{:S(2)}) collective-permute-start(f32[192,128]{1,0:T(8,128)S(1)} %add.105), channel_id=1, source_target_pairs={{0,0},{1,65},{2,130},{3,195},{4,260},{5,325},{6,390},{7,455},{8,8}... | collective-permute-start | bytes 294920 | tf_op jit(solution)/shard_map/ppermute | solution.py:22
  267.0 17.8 %collective-permute-start.66 = (f32[192,128]{1,0:T(8,128)S(1)}, f32[192,128]{1,0:T(8,128)S(1)}, u32[]{:S(2)}, u32[]{:S(2)}) collective-permute-start(f32[192,128]{1,0:T(8,128)S(1)} %get-tuple-element.6.refs_0_), channel_id=1, source_target_pairs={{0,32},{1,33},{2,34},{3,35},{4,36},{5,37},{6,38},{7,39},{8,40},{9,... | collective-permute-start | bytes 294920 | tf_op jit(solution)/shard_map/ppermute | solution.py:22
  269.0 21.8 %collective-permute-start.67 = (f32[192,128]{1,0:T(8,128)S(1)}, f32[192,128]{1,0:T(8,128)S(1)}, u32[]{:S(2)}, u32[]{:S(2)}) collective-permute-start(f32[192,128]{1,0:T(8,128)S(1)} %get-tuple-element.6.refs_0_), channel_id=1, source_target_pairs={{0,48},{1,49},{2,50},{3,51},{4,52},{5,53},{6,54},{7,55},{8,56},{9,... | collective-permute-start | bytes 294920 | tf_op jit(solution)/shard_map/ppermute | solution.py:22
  271.7 30.6 %collective-permute-start.65 = (f32[192,128]{1,0:T(8,128)S(1)}, f32[192,128]{1,0:T(8,128)S(1)}, u32[]{:S(2)}, u32[]{:S(2)}) collective-permute-start(f32[192,128]{1,0:T(8,128)S(1)} %get-tuple-element.6.refs_0_), channel_id=1, source_target_pairs={{0,16},{1,17},{2,18},{3,19},{4,20},{5,21},{6,22},{7,23},{8,24},{9,... | collective-permute-start | bytes 294920 | tf_op jit(solution)/shard_map/ppermute | solution.py:22
  275.6 17.1 %collective-permute-start.58 = (f32[192,128]{1,0:T(8,128)S(1)}, f32[192,128]{1,0:T(8,128)S(1)}, u32[]{:S(2)}, u32[]{:S(2)}) collective-permute-start(f32[192,128]{1,0:T(8,128)S(1)} %get-tuple-element.8.refs_0_), channel_id=1, source_target_pairs={{0,32},{1,33},{2,34},{3,35},{4,36},{5,37},{6,38},{7,39},{8,40},{9,... | collective-permute-start | bytes 294920 | tf_op jit(solution)/shard_map/ppermute | solution.py:22
  281.7 18.6 %collective-permute-start.59 = (f32[192,128]{1,0:T(8,128)S(1)}, f32[192,128]{1,0:T(8,128)S(1)}, u32[]{:S(2)}, u32[]{:S(2)}) collective-permute-start(f32[192,128]{1,0:T(8,128)S(1)} %get-tuple-element.8.refs_0_), channel_id=1, source_target_pairs={{0,48},{1,49},{2,50},{3,51},{4,52},{5,53},{6,54},{7,55},{8,56},{9,... | collective-permute-start | bytes 294920 | tf_op jit(solution)/shard_map/ppermute | solution.py:22
  284.8 63.5 %collective-permute-start.56 = (f32[1152,128]{1,0:T(8,128)S(1)}, f32[1152,128]{1,0:T(8,128)S(1)}, u32[]{:S(2)}, u32[]{:S(2)}) collective-permute-start(f32[1152,128]{1,0:T(8,128)S(1)} %get-tuple-element.5), channel_id=1, source_target_pairs={{0,0},{1,449},{2,386},{3,323},{4,260},{5,197},{6,134},{7,71},{8,8}... | collective-permute-start | bytes 1769480 | tf_op jit(solution)/shard_map/ppermute | solution.py:22
  290.8 19.1 %collective-permute-start.68 = (f32[384,128]{1,0:T(8,128)S(1)}, f32[384,128]{1,0:T(8,128)S(1)}, u32[]{:S(2)}, u32[]{:S(2)}) collective-permute-start(f32[384,128]{1,0:T(8,128)S(1)} %get-tuple-element.26), channel_id=1, source_target_pairs={{0,8},{1,9},{2,10},{3,11},{4,12},{5,13},{6,14},{7,15},{8,16},{9,17... | collective-permute-start | bytes 589832 | tf_op jit(solution)/shard_map/ppermute | solution.py:22
  292.8 19.1 %collective-permute-start.69 = (f32[384,128]{1,0:T(8,128)S(1)}, f32[384,128]{1,0:T(8,128)S(1)}, u32[]{:S(2)}, u32[]{:S(2)}) collective-permute-start(f32[384,128]{1,0:T(8,128)S(1)} %get-tuple-element.25), channel_id=1, source_target_pairs={{0,504},{1,505},{2,506},{3,507},{4,508},{5,509},{6,510},{7,511},{8... | collective-permute-start | bytes 589832 | tf_op jit(solution)/shard_map/ppermute | solution.py:22
  300.4 20.0 %collective-permute-start.60 = (f32[384,128]{1,0:T(8,128)S(1)}, f32[384,128]{1,0:T(8,128)S(1)}, u32[]{:S(2)}, u32[]{:S(2)}) collective-permute-start(f32[384,128]{1,0:T(8,128)S(1)} %get-tuple-element.28), channel_id=1, source_target_pairs={{0,8},{1,9},{2,10},{3,11},{4,12},{5,13},{6,14},{7,15},{8,16},{9,17... | collective-permute-start | bytes 589832 | tf_op jit(solution)/shard_map/ppermute | solution.py:22
  302.3 18.1 %collective-permute-start.61 = (f32[384,128]{1,0:T(8,128)S(1)}, f32[384,128]{1,0:T(8,128)S(1)}, u32[]{:S(2)}, u32[]{:S(2)}) collective-permute-start(f32[384,128]{1,0:T(8,128)S(1)} %get-tuple-element.27), channel_id=1, source_target_pairs={{0,504},{1,505},{2,506},{3,507},{4,508},{5,509},{6,510},{7,511},{8... | collective-permute-start | bytes 589832 | tf_op jit(solution)/shard_map/ppermute | solution.py:22
  309.9 10.5 %collective-permute-start.57 = (f32[192,128]{1,0:T(8,128)S(1)}, f32[192,128]{1,0:T(8,128)S(1)}, u32[]{:S(2)}, u32[]{:S(2)}) collective-permute-start(f32[192,128]{1,0:T(8,128)S(1)} %get-tuple-element.8.refs_0_), channel_id=1, source_target_pairs={{0,16},{1,17},{2,18},{3,19},{4,20},{5,21},{6,22},{7,23},{8,24},{9,... | collective-permute-start | bytes 294920 | tf_op jit(solution)/shard_map/ppermute | solution.py:22
  313.6 10.5 %collective-permute-start.70 = (f32[192,128]{1,0:T(8,128)S(1)}, f32[192,128]{1,0:T(8,128)S(1)}, u32[]{:S(2)}, u32[]{:S(2)}) collective-permute-start(f32[192,128]{1,0:T(8,128)S(1)} %shard_map.72), channel_id=1, source_target_pairs={{0,1},{1,0},{2,3},{3,2},{4,5},{5,4},{6,7},{7,6},{8,9},{9,8},{10,11... | collective-permute-start | bytes 294920 | tf_op jit(solution)/shard_map/ppermute | solution.py:22
  322.1 13.8 %collective-permute-start.62 = (f32[192,128]{1,0:T(8,128)S(1)}, f32[192,128]{1,0:T(8,128)S(1)}, u32[]{:S(2)}, u32[]{:S(2)}) collective-permute-start(f32[192,128]{1,0:T(8,128)S(1)} %shard_map.71), channel_id=1, source_target_pairs={{0,1},{1,0},{2,3},{3,2},{4,5},{5,4},{6,7},{7,6},{8,9},{9,8},{10,11... | collective-permute-start | bytes 294920 | tf_op jit(solution)/shard_map/ppermute | solution.py:22
  324.1 15.0 %collective-permute-start.71 = (f32[192,128]{1,0:T(8,128)S(1)}, f32[192,128]{1,0:T(8,128)S(1)}, u32[]{:S(2)}, u32[]{:S(2)}) collective-permute-start(f32[192,128]{1,0:T(8,128)S(1)} %add.110), channel_id=1, source_target_pairs={{0,2},{1,3},{2,0},{3,1},{4,6},{5,7},{6,4},{7,5},{8,10},{9,11},{10,... | collective-permute-start | bytes 294920 | tf_op jit(solution)/shard_map/ppermute | solution.py:22
  339.1 12.2 %collective-permute-start.72 = (f32[192,128]{1,0:T(8,128)S(1)}, f32[192,128]{1,0:T(8,128)S(1)}, u32[]{:S(2)}, u32[]{:S(2)}) collective-permute-start(f32[192,128]{1,0:T(8,128)S(1)} %add.111), channel_id=1, source_target_pairs={{0,4},{1,5},{2,6},{3,7},{4,0},{5,1},{6,2},{7,3},{8,12},{9,13},{10,... | collective-permute-start | bytes 294920 | tf_op jit(solution)/shard_map/ppermute | solution.py:22
  (14 other events, 247.8 us)

commit v2 on v0

v2 whole, which is shorter than its diff:
```python
import functools

import jax
import jax.numpy as jnp
from jax import lax
from jax.experimental import pallas as pl
from jax.experimental.pallas import tpu as pltpu
from jax.sharding import PartitionSpec as P

HOPS = 4
HALF = 64
VMEM_BYTES = 16 * 2**20


def send(block, place):
    cycle, groups = lax.axis_size("blk"), lax.axis_size("rep")
    route = []
    for p in range(cycle):
        for w in range(groups):
            to_p, to_w = place(p, w)
            route.append((p * groups + w, (to_p % cycle) * groups + to_w))
    return lax.ppermute(block, ("blk", "rep"), route)


def swap_cores(block):
    return send(block, lambda p, w: (p, w ^ 1))


def pack(field, half):
    blocks = field.shape[0] // 128
    part = field.reshape(blocks, 2, HALF, 2, HALF)[:, :, :, half]
    return part.transpose(0, 2, 1, 3).reshape(blocks * HALF, 128)


def split_tiles(first_slots, second_slots, core_ref, mine_ref, other_ref, out_ref):
    for s, (at_first, at_second) in enumerate(zip(first_slots, second_slots)):
        def read(at):
            held, place = at
            return (mine_ref if held == "mine" else other_ref)[place * 128:(place + 1) * 128]
        tile = jnp.where(core_ref[0] == 0, read(at_first), read(at_second))
        high = tile.astype(jnp.bfloat16)
        low = (tile - high.astype(jnp.float32)).astype(jnp.bfloat16)
        out_ref[0, 0:128, s * 128:(s + 1) * 128] = high
        out_ref[0, 128:256, s * 128:(s + 1) * 128] = low


def tile_parts(core, mine, other, rows, first_slots, second_slots):
    slots = len(first_slots)
    held = 1 + max(place for _, place in first_slots)
    block = pl.BlockSpec((held * 128, 128), lambda i, core: (i, 0))
    return pl.pallas_call(
        functools.partial(split_tiles, first_slots, second_slots),
        grid_spec=pltpu.PrefetchScalarGridSpec(
            num_scalar_prefetch=1,
            grid=(rows,),
            in_specs=[block, block],
            out_specs=pl.BlockSpec((1, 256, slots * 128), lambda i, core: (i, 0, 0)),
        ),
        out_shape=jax.ShapeDtypeStruct((rows, 256, slots * 128), jnp.bfloat16),
        compiler_params=pltpu.CompilerParams(vmem_limit_bytes=VMEM_BYTES),
    )(core, mine, other)


def multiply(index_ref, tiles_ref, scale_ref, source_ref, gathered_ref, out_ref):
    rows, slots = index_ref.shape
    left = lax.broadcasted_iota(jnp.int32, (HALF, 128), 1) < HALF
    for i in range(rows):
        for s in range(slots):
            gathered_ref[i, s * 128:(s + 1) * 128] = source_ref[index_ref[i, s]]
    for i in range(rows):
        both = jnp.dot(tiles_ref[i], gathered_ref[i], preferred_element_type=jnp.float32)
        total = both[0:128] + both[128:256]
        total = total + pltpu.roll(total, HALF, 1)
        at = slice(i * HALF, (i + 1) * HALF)
        out_ref[at] = jnp.where(left, total[0:HALF], total[HALF:128]) * scale_ref[at]


def near_kernel(index_ref, tiles_ref, scale_ref, units_ref, near_ref, source_ref, gathered_ref):
    left = lax.broadcasted_iota(jnp.int32, (HALF, 128), 1) < HALF
    count = units_ref.shape[0] // HALF
    for k in range(count):
        part = units_ref[k * HALF:(k + 1) * HALF]
        high = part.astype(jnp.bfloat16).astype(jnp.float32)
        low = part - high
        top = jnp.where(left, high, pltpu.roll(low, HALF, 1))
        bottom = jnp.where(left, pltpu.roll(high, HALF, 1), low)
        source_ref[k, 0:HALF] = top.astype(jnp.bfloat16)
        source_ref[k, HALF:128] = bottom.astype(jnp.bfloat16)
    source_ref[count] = jnp.zeros((128, 128), jnp.bfloat16)
    multiply(index_ref, tiles_ref, scale_ref, source_ref, gathered_ref, near_ref)


def far_kernel(members, index_ref, tiles_ref, scale_ref, source_ref, near_ref, out_ref, gathered_ref, far_ref):
    multiply(index_ref, tiles_ref, scale_ref, source_ref, gathered_ref, far_ref)
    piece = near_ref.shape[0] // members
    for m in range(members):
        at = slice(m * piece, (m + 1) * piece)
        out_ref[2 * m * piece:(2 * m + 1) * piece] = near_ref[at]
        out_ref[(2 * m + 1) * piece:(2 * m + 2) * piece] = far_ref[at]


def product_call(kernel, inputs, rows, slots, out_shape, more_scratch=()):
    vmem = pl.BlockSpec(memory_space=pltpu.VMEM)
    smem = pl.BlockSpec(memory_space=pltpu.SMEM)
    return pl.pallas_call(
        kernel,
        in_specs=[smem] + [vmem] * (inputs - 1),
        out_specs=jax.tree.map(lambda _: vmem, out_shape),
        out_shape=out_shape,
        scratch_shapes=[pltpu.VMEM((rows, slots * 128, 128), jnp.bfloat16), *more_scratch],
        compiler_params=pltpu.CompilerParams(vmem_limit_bytes=VMEM_BYTES),
        cost_estimate=pl.CostEstimate(flops=2 * rows * slots * 256 * 128 * 128, bytes_accessed=4 * 2**20, transcendentals=0),
    )


def near_product(index, tiles, scale, units):
    rows, slots = index.shape
    sums = jax.ShapeDtypeStruct((rows * HALF, 128), jnp.float32)
    source = jax.ShapeDtypeStruct((units.shape[0] // HALF + 1, 128, 128), jnp.bfloat16)
    return product_call(near_kernel, 4, rows, slots, [sums, source])(index, tiles, scale, units)


def far_product(index, tiles, scale, source, near, members):
    rows, slots = index.shape
    both = jax.ShapeDtypeStruct((2 * rows * HALF, 128), jnp.float32)
    scratch = [pltpu.VMEM((rows * HALF, 128), jnp.float32)]
    return product_call(functools.partial(far_kernel, members), 5, rows, slots, both, scratch)(index, tiles, scale, source, near)


def piece_sums(came_ref, lines, pairs):
    piece = came_ref.shape[0] // (2 * lines * pairs)

    def read(line, pair, which):
        first = (2 * (line * pairs + pair) + which) * piece
        return came_ref[first:first + piece]

    sums = []
    for line in range(lines):
        terms = [read(line, pair, 0) for pair in range(pairs)]
        terms += [read((line - 1) % lines, pair, 1) for pair in range(pairs)]
        while len(terms) > 1:
            terms = [a + b for a, b in zip(terms[::2], terms[1::2])]
        sums.append(terms[0])
    return sums


def hand_on_kernel(lines, pairs, came_ref, out_ref):
    sums = piece_sums(came_ref, lines, pairs)
    piece = sums[0].shape[0]
    for line in range(lines):
        for pair in range(pairs):
            first = 2 * (line * pairs + pair) * piece
            out_ref[first:first + piece] = sums[(line - 2 * pair) % lines]
            out_ref[first + piece:first + 2 * piece] = sums[(line - 2 * pair - 1) % lines]


def hand_out_kernel(lines, pairs, came_ref, out_ref):
    sums = piece_sums(came_ref, lines, pairs)
    piece = sums[0].shape[0]
    for line in range(lines):
        for member in range(2 * pairs):
            first = (line * 2 * pairs + member) * piece
            out_ref[first:first + piece] = sums[line]


def hand(kernel, came, lines, pairs):
    vmem = pl.BlockSpec(memory_space=pltpu.VMEM)
    return pl.pallas_call(
        functools.partial(kernel, lines, pairs),
        in_specs=[vmem],
        out_specs=vmem,
        out_shape=jax.ShapeDtypeStruct(came.shape, jnp.float32),
        compiler_params=pltpu.CompilerParams(vmem_limit_bytes=VMEM_BYTES),
    )(came)


def choose_kernel(members, span, rank_ref, came_ref, chunks_ref, own_ref, behind_ref):
    piece = came_ref.shape[0] // (2 * members)
    for m in range(members):
        at = slice(m * piece, (m + 1) * piece)
        own_ref[at] = came_ref[2 * m * piece:(2 * m + 1) * piece]
        behind_ref[at] = came_ref[(2 * m + 1) * piece:(2 * m + 2) * piece]
    for y in range(span):
        chunks_ref[y] = jnp.where(y >= rank_ref[0], own_ref[...], behind_ref[...])


def choose(rank_y, came, members, span):
    vmem = pl.BlockSpec(memory_space=pltpu.VMEM)
    unit = (came.shape[0] // 2, came.shape[1])
    return pl.pallas_call(
        functools.partial(choose_kernel, members, span),
        in_specs=[pl.BlockSpec(memory_space=pltpu.SMEM), vmem],
        out_specs=[vmem, vmem],
        out_shape=[jax.ShapeDtypeStruct((span, *unit), jnp.float32), jax.ShapeDtypeStruct(unit, jnp.float32)],
        scratch_shapes=[pltpu.VMEM(unit, jnp.float32)],
        compiler_params=pltpu.CompilerParams(vmem_limit_bytes=VMEM_BYTES),
    )(rank_y, came)


def finish_kernel(members, core_ref, ordered_ref, root_ref, mine_ref, other_ref, last_ref, out_ref, halves_ref):
    out_ref[0] = ordered_ref[...]
    left = lax.broadcasted_iota(jnp.int32, (HALF, 128), 1) < HALF
    first_core = core_ref[0] == 0
    blocks = ordered_ref.shape[0] // 128
    size = blocks * HALF
    piece = size // members
    for m in range(members):
        for half in range(2):
            first = (2 * m + half) * piece
            halves_ref[half, m * piece:(m + 1) * piece] = last_ref[first:first + piece]
    for hop in range(HOPS):
        for b in range(blocks):
            if hop < HOPS - 1:
                at = slice(hop * size + b * HALF, hop * size + (b + 1) * HALF)
                a = jnp.where(first_core, mine_ref[at], other_ref[at])
                c = jnp.where(first_core, other_ref[at], mine_ref[at])
            else:
                at = slice(b * HALF, (b + 1) * HALF)
                a, c = halves_ref[0, at], halves_ref[1, at]
            first = b * 128
            top = jnp.where(left, a, pltpu.roll(c, HALF, 1))
            bottom = jnp.where(left, pltpu.roll(a, HALF, 1), c)
            out_ref[hop + 1, first:first + HALF] = top * root_ref[first:first + HALF]
            out_ref[hop + 1, first + HALF:first + 128] = bottom * root_ref[first + HALF:first + 128]


def finish(core, ordered, root, mine, other, last, members):
    vmem = pl.BlockSpec(memory_space=pltpu.VMEM)
    return pl.pallas_call(
        functools.partial(finish_kernel, members),
        in_specs=[pl.BlockSpec(memory_space=pltpu.SMEM)] + [vmem] * 5,
        out_specs=vmem,
        out_shape=jax.ShapeDtypeStruct((HOPS + 1,) + ordered.shape, jnp.float32),
        scratch_shapes=[pltpu.VMEM((2, ordered.shape[0] // 2, 128), jnp.float32)],
        compiler_params=pltpu.CompilerParams(vmem_limit_bytes=VMEM_BYTES),
    )(core, ordered, root, mine, other, last)


def ring_exchange(chunks):
    span = chunks.shape[0]
    rings = [[first + at for at in range(span)] for first in range(0, lax.axis_size("blk"), span)]
    return lax.all_to_all(chunks, "blk", 0, 0, axis_index_groups=rings)


def plane_exchange(block, span, cores):
    cycle, groups = lax.axis_size("blk"), lax.axis_size("rep")
    planes = []
    for y in range(span):
        for core in range(0, 2, cores):
            starts = range(core, groups, 2) if cores == 1 else range(groups)
            planes.append([p * groups + w for p in range(y, cycle, span) for w in starts])
    pieces = block.reshape(len(planes[0]), 1, -1)
    moved = lax.all_to_all(pieces, ("blk", "rep"), 0, 0, axis_index_groups=planes)
    return moved.reshape(block.shape)


def local(features, tile_values, tile_cols, tile_counts, degrees, curve_order):
    rank_blk = lax.axis_index("blk")
    rank_rep = lax.axis_index("rep")
    span = lax.axis_size("blk") // lax.axis_size("rep")
    rows, slots = tile_values.shape[:2]
    mid = slots // 2
    core = rank_rep % 2
    first_core = core == 0
    core_ref = core.reshape(1)

    swapped = swap_cores(tile_values)
    live = jnp.arange(slots, dtype=jnp.int32)[None, :] < tile_counts
    index = jnp.where(live, tile_cols % (span * rows), span * rows)
    swapped_index = swap_cores(index)
    near_index = jnp.where(first_core, index, swapped_index)
    leaving = jnp.where(first_core, swapped[:, :mid], tile_values[:, mid:]).reshape(-1, 128)
    leaving_index = jnp.where(first_core, swapped_index, index).astype(jnp.float32)
    index_rows = jnp.pad(leaving_index, ((0, 8 - rows), (0, 128 - slots)))
    leaving = jnp.concatenate([leaving, index_rows])

    ordered = jnp.take(features, curve_order - rank_blk * features.shape[0], axis=0, mode="clip")
    count = degrees.astype(jnp.float32)
    inv_root = lax.rsqrt(count)[:, None]
    wide = jnp.broadcast_to(inv_root, features.shape)
    root = jnp.broadcast_to(count[:, None], features.shape) * wide
    scale = pack(wide * wide, 0)
    sent = wide * ordered
    start = jnp.where(first_core, pack(sent, 0), pack(sent, 1))

    def aligned(p, w):
        return p + 2 * span * (w // 2), w

    def behind_aligned(p, w):
        return p + 2 * span * (w // 2) + span, w

    rank_y = rank_blk % span
    lines = lax.axis_size("blk") // span
    pairs = lax.axis_size("rep") // 2
    members = lines * pairs
    own, behind = send(start, aligned), send(start, behind_aligned)
    far_scale = send(scale, lambda p, w: (p - span, w))
    every = [("mine", s) for s in range(slots)], [("other", s) for s in range(slots)]
    flat = tile_values.reshape(-1, 128), swapped.reshape(-1, 128)
    near_tiles = tile_parts(core_ref, *flat, rows, *every)
    own, behind, leaving, far_scale = lax.optimization_barrier((own, behind, leaving, far_scale))
    came = send(leaving, lambda p, w: (p - span, w))
    ring = jnp.arange(span, dtype=jnp.int32)[:, None, None]
    chunks = jnp.where(ring >= rank_y, own[None], behind[None])
    kept = []
    for hop in range(HOPS):
        units = ring_exchange(chunks).reshape(-1, 128)
        if hop == 0:
            units, came = lax.optimization_barrier((units, came))
        near, source = near_product(near_index, near_tiles, scale, units)
        if hop == 0:
            rest = swap_cores(came)
            low_slots = [("mine", s) for s in range(mid)] + [("other", s) for s in range(mid)]
            high_slots = [("other", s) for s in range(mid)] + [("mine", s) for s in range(mid)]
            far_index = came[rows * mid * 128:][:rows, :slots].astype(jnp.int32)
            far_tiles = tile_parts(core_ref, came, rest, rows, low_slots, high_slots)
        sums = far_product(far_index, far_tiles, far_scale, source, near, members)
        pieces = plane_exchange(sums, span, 1)
        if hop < HOPS - 1:
            came_units = plane_exchange(hand(hand_on_kernel, pieces, lines, pairs), span, 1)
            chunks, own = choose(rank_y.reshape(1), came_units, members, span)
            kept.append(own)
    last = plane_exchange(hand(hand_out_kernel, pieces, lines, pairs), span, 2)
    mine = send(jnp.concatenate(kept), lambda p, w: (p - 2 * span * (w // 2), w))
    return finish(core_ref, ordered, root, mine, swap_cores(mine), last, members)


def solution(mesh):
    return jax.shard_map(
        local,
        mesh=mesh,
        in_specs=(
            P("blk", None),
            P("blk", "rep", None, None),
            P("blk", "rep"),
            P("blk", "rep"),
            P("blk"),
            P("blk"),
        ),
        out_specs=P(None, "blk", None),
        check_vma=False,
    )
```

time: 803 us -> 287 us (0.36)
  waiting for transfers between devices: 626 us -> 42.8 us
  blocking collectives: 0 us -> 159 us
  starting transfers between devices: 90.4 us -> 55.3 us
  local copies, waits for them, and re-layouts: 35.5 us -> 2.75 us
  Pallas kernels: 0 us -> 20.8 us
  matrix products: 20.7 us -> 0 us
  between operations: 13.7 us -> 0.38 us
  other arithmetic: 14 us -> 5.57 us
    psum x4 -> x0, waiting for transfers between devices: 325 us -> none  [local(): summed = lax.psum(partial_value.reshape(row_count, feat_width), 'rep')]
    ppermute x40 -> x9, waiting for transfers between devices: 301 us -> 25.8 us  [send(): return lax.ppermute(block, ('blk', 'rep'), route)]
    all_to_all x0 -> x9, blocking collectives: none -> 159 us  [the longest x6 93.3 us: plane_exchange(): lax.all_to_all(pieces, ('blk', 'rep'), 0, 0, axis_index_groups=planes)]
    ppermute x40 -> x9, starting transfers between devices: 90.2 us -> 31.7 us  [send(): return lax.ppermute(block, ('blk', 'rep'), route)]
    all_to_all x0 -> x3, starting transfers between devices: none -> 23.6 us  [the longest x2 20.1 us: plane_exchange(): lax.all_to_all(pieces, ('blk', 'rep'), 0, 0, axis_index_groups=planes)]
    pallas_call x0 -> x18, Pallas kernels: none -> 20.8 us  [the longest x4 6.91 us: near_product(): product_call(near_kernel, 4, rows, slots, [sums, source])]
    dot_general x4 -> x0, matrix products: 20.7 us -> none  [local(): jnp.einsum('isab,isbc->iac', tile_values, gathered, precision=lax.Precisi...]
    all_to_all x0 -> x3, waiting for transfers between devices: none -> 16.9 us  [the longest x2 16.9 us: plane_exchange(): lax.all_to_all(pieces, ('blk', 'rep'), 0, 0, axis_index_groups=planes)]
  transfers between devices with their start and end apart: 44 -> 12, of which waited for: 44 -> 4; matrix products, arithmetic and copies ran while one was open for 2% -> 2% of each run, Pallas kernels for 0% -> 2%
where the time goes in v2:
time: 287 us; the launch traced here: 286 us
  blocking collectives  159 us (55%)
  starting transfers between devices  55.3 us (19%)
  waiting for transfers between devices  42.8 us (15%)
  Pallas kernels  20.8 us (7%)
  other arithmetic  5.57 us (2%)
    all_to_all x6, blocking collectives, plane_exchange(): lax.all_to_all(pieces, ('blk', 'rep'), 0, 0, axis_index_groups=planes)  93.3 us
    all_to_all x3, blocking collectives, ring_exchange(): return lax.all_to_all(chunks, 'blk', 0, 0, axis_index_groups=rings)  65.3 us
    ppermute x9, starting transfers between devices, send(): return lax.ppermute(block, ('blk', 'rep'), route)  31.7 us
    ppermute x9, waiting for transfers between devices, send(): return lax.ppermute(block, ('blk', 'rep'), route)  25.8 us
    all_to_all x2, starting transfers between devices, plane_exchange(): lax.all_to_all(pieces, ('blk', 'rep'), 0, 0, axis_index_groups=planes)  20.1 us
    all_to_all x2, waiting for transfers between devices, plane_exchange(): lax.all_to_all(pieces, ('blk', 'rep'), 0, 0, axis_index_groups=planes)  16.9 us
    pallas_call x4, Pallas kernels, near_product(): product_call(near_kernel, 4, rows, slots, [sums, source])  6.91 us
    pallas_call x4, Pallas kernels, far_product(): product_call(functools.partial(far_kernel, members), 5, rows, slots, both...  6.58 us
  transfers between devices with their start and end apart: 12, of which 4 were waited for; matrix products, arithmetic and copies ran while one was open for 2% of the time, Pallas kernels for 2%

profile of v2, /device:TPU:1, one launch (start us, length us, event | category | flops | bytes accessed | tf_op | source)
XLA Modules:
  0.0 286.1 jit_solution(4354243045468220048)
XLA Ops:
  0.0 8.9 %collective-permute-start.2 = (f32[3,12,128,128]{3,2,1,0:T(8,128)}, f32[3,12,128,128]{3,2,1,0:T(8,128)}, u32[]{:S(2)}, u32[]{:S(2)}) collective-permute-start(f32[3,12,128,128]{3,2,1,0:T(8,128)} %param.7), channel_id=1, source_target_pairs={{0,1},{1,0},{2,3},{3,2},{4,5},{5,4},{6,7},{7,6},{8,9},{9,8},{10,11... | collective-permute-start | bytes 7077896 | tf_op jit(solution)/shard_map/ppermute | solution.py:22
  8.9 0.7 broadcast_subtract_fusion
  9.6 1.1 gather_fusion
  10.8 0.0 copy-start.4
  10.8 0.0 copy-start.5
  10.8 0.2 gather.7
  11.1 0.1 broadcast_in_dim.53
  11.2 0.3 copy-done.2
  11.4 0.1 copy.12
  11.6 0.4 copy_multiply_fusion
  12.0 0.1 fusion
  12.1 0.2 select_n.68
  12.2 0.8 collective-permute-start
  13.0 1.9 collective-permute-start.1
  15.0 0.1 fusion.1
  15.0 1.9 collective-permute-start.3
  17.0 0.1 broadcast_in_dim.55
  17.0 0.1 copy.14
  17.2 0.3 broadcast_bitcast_fusion
  17.4 0.2 reshape.110.scale_ref
  17.6 5.7 %collective-permute-start.4 = (f32[192,128]{1,0:T(8,128)S(1)}, f32[192,128]{1,0:T(8,128)S(1)}, u32[]{:S(2)}, u32[]{:S(2)}) collective-permute-start(f32[192,128]{1,0:T(8,128)S(1)} %reshape.110.scale_ref), channel_id=1, source_target_pairs={{0,448},{1,449},{2,450},{3,451},{4,452},{5,453},{6,454},{7,455},{8... | collective-permute-start | bytes 294920 | tf_op jit(solution)/shard_map/ppermute | solution.py:22
  23.4 0.1 broadcast_select_fusion.1
  23.5 1.4 slice_select_fusion
  24.9 1.1 select_maximum_fusion
  26.0 0.0 collective-permute-done
  26.0 0.0 collective-permute-done.1
  26.0 1.0 broadcast_select_fusion
  27.0 3.5 %all-to-all-start = ((f32[8,192,128]{2,1,0:T(8,128)}), f32[8,192,128]{2,1,0:T(8,128)S(1)}, u32[]{:S(2)}, u32[]{:S(2)}) async-start(f32[8,192,128]{2,1,0:T(8,128)} %broadcast_select_fusion), calls=%async_computation | async-start | bytes 1572864 | tf_op jit(solution)/shard_map/all_to_all | solution.py:242
  30.6 5.5 %collective-permute-start.5 = (f32[2312,128]{1,0:T(8,128)}, f32[2312,128]{1,0:T(8,128)}, u32[]{:S(2)}, u32[]{:S(2)}) collective-permute-start(f32[2312,128]{1,0:T(8,128)} %select_maximum_fusion), channel_id=1, source_target_pairs={{0,448},{1,449},{2,450},{3,451},{4,452},{5,453},{6,454},{7,455},{8... | collective-permute-start | bytes 3551240 | tf_op jit(solution)/shard_map/ppermute | solution.py:22
  36.1 24.6 %collective-permute-done.5.mine_ref = f32[2312,128]{1,0:T(8,128)} collective-permute-done((f32[2312,128]{1,0:T(8,128)}, f32[2312,128]{1,0:T(8,128)}, u32[]{:S(2)}, u32[]{:S(2)}) %collective-permute-start.5) | collective-permute-done | bytes 1183776 | tf_op jit(solution)/shard_map/ppermute | solution.py:22
  60.7 3.8 %collective-permute-start.6 = (f32[2312,128]{1,0:T(8,128)}, f32[2312,128]{1,0:T(8,128)S(1)}, u32[]{:S(2)}, u32[]{:S(2)}) collective-permute-start(f32[2312,128]{1,0:T(8,128)} %collective-permute-done.5.mine_ref), channel_id=1, source_target_pairs={{0,1},{1,0},{2,3},{3,2},{4,5},{5,4},{6,7},{7,6},{8,9},{9,8},{10,11... | collective-permute-start | bytes 3551240 | tf_op jit(solution)/shard_map/ppermute | solution.py:22
  64.6 2.7 shard_map.65.tiles_ref
  67.2 1.7 shard_map.66
  69.0 0.7 slice_convert_fusion.index_ref
  69.6 2.4 shard_map.64.tiles_ref
  72.1 1.5 shard_map.67
  73.5 22.6 %all_to_all.60 = f32[32,1,1536]{2,1,0:T(1,128)S(1)} all-to-all(f32[32,1,1536]{2,1,0:T(1,128)S(1)} %bitcast.38), channel_id=1, replica_groups={{0,2,4,6,64,66,68,70,128,130,132,134,192,194,196,198,256,258,260,262,32..., dimensions={0} | all-to-all | bytes 393216 | tf_op jit(solution)/shard_map/all_to_all | solution.py:253
  96.2 15.1 %all_to_all.61 = f32[32,1,1536]{2,1,0:T(1,128)S(1)} all-to-all(f32[32,1,1536]{2,1,0:T(1,128)S(1)} %bitcast.46), channel_id=1, replica_groups={{0,2,4,6,64,66,68,70,128,130,132,134,192,194,196,198,256,258,260,262,32..., dimensions={0} | all-to-all | bytes 393216 | tf_op jit(solution)/shard_map/all_to_all | solution.py:253
  111.3 0.1 shard_map.69
  111.4 26.4 %all_to_all.62 = f32[8,192,128]{2,1,0:T(8,128)S(1)} all-to-all(f32[8,192,128]{2,1,0:T(8,128)S(1)} %get-tuple-element.34), channel_id=1, replica_groups={{0,8,16,24,32,40,48,56},{64,72,80,88,96,104,112,120},{128,136,144,152,1..., dimensions={0} | all-to-all | bytes 1572864 | tf_op jit(solution)/shard_map/all_to_all | solution.py:242
  137.8 1.7 shard_map.70
  139.5 1.5 shard_map.71
  141.0 15.5 %all_to_all.63 = f32[32,1,1536]{2,1,0:T(1,128)S(1)} all-to-all(f32[32,1,1536]{2,1,0:T(1,128)S(1)} %bitcast.39), channel_id=1, replica_groups={{0,2,4,6,64,66,68,70,128,130,132,134,192,194,196,198,256,258,260,262,32..., dimensions={0} | all-to-all | bytes 393216 | tf_op jit(solution)/shard_map/all_to_all | solution.py:253
  156.6 13.4 %all_to_all.64 = f32[32,1,1536]{2,1,0:T(1,128)S(1)} all-to-all(f32[32,1,1536]{2,1,0:T(1,128)S(1)} %bitcast.48), channel_id=1, replica_groups={{0,2,4,6,64,66,68,70,128,130,132,134,192,194,196,198,256,258,260,262,32..., dimensions={0} | all-to-all | bytes 393216 | tf_op jit(solution)/shard_map/all_to_all | solution.py:253
  170.0 0.1 shard_map.73
  170.1 20.3 %all_to_all.65 = f32[8,192,128]{2,1,0:T(8,128)S(1)} all-to-all(f32[8,192,128]{2,1,0:T(8,128)S(1)} %get-tuple-element.38), channel_id=1, replica_groups={{0,8,16,24,32,40,48,56},{64,72,80,88,96,104,112,120},{128,136,144,152,1..., dimensions={0} | all-to-all | bytes 1572864 | tf_op jit(solution)/shard_map/all_to_all | solution.py:242
  190.3 1.7 shard_map.74
  192.0 1.5 shard_map.75
  193.5 13.5 %all_to_all.66 = f32[32,1,1536]{2,1,0:T(1,128)S(1)} all-to-all(f32[32,1,1536]{2,1,0:T(1,128)S(1)} %bitcast.40), channel_id=1, replica_groups={{0,2,4,6,64,66,68,70,128,130,132,134,192,194,196,198,256,258,260,262,32..., dimensions={0} | all-to-all | bytes 393216 | tf_op jit(solution)/shard_map/all_to_all | solution.py:253
  207.1 13.1 %all_to_all.67 = f32[32,1,1536]{2,1,0:T(1,128)S(1)} all-to-all(f32[32,1,1536]{2,1,0:T(1,128)S(1)} %bitcast.50), channel_id=1, replica_groups={{0,2,4,6,64,66,68,70,128,130,132,134,192,194,196,198,256,258,260,262,32..., dimensions={0} | all-to-all | bytes 393216 | tf_op jit(solution)/shard_map/all_to_all | solution.py:253
  220.2 0.1 shard_map.77
  220.3 18.6 %all_to_all.68 = f32[8,192,128]{2,1,0:T(8,128)S(1)} all-to-all(f32[8,192,128]{2,1,0:T(8,128)S(1)} %get-tuple-element.42), channel_id=1, replica_groups={{0,8,16,24,32,40,48,56},{64,72,80,88,96,104,112,120},{128,136,144,152,1..., dimensions={0} | all-to-all | bytes 1572864 | tf_op jit(solution)/shard_map/all_to_all | solution.py:242
  238.9 1.7 shard_map.78
  240.6 2.2 shard_map.79
  242.8 4.5 %all-to-all-start.10 = ((f32[32,1,1536]{2,1,0:T(1,128)}), f32[32,1,1536]{2,1,0:T(1,128)S(1)}, u32[]{:S(2)}, u32[]{:S(2)}) async-start(f32[32,1,1536]{2,1,0:T(1,128)} %bitcast.25), calls=%async_computation.10 | async-start | bytes 393216 | tf_op jit(solution)/shard_map/all_to_all | solution.py:253
  247.3 0.7 collective-permute-start.7
  247.9 8.3 %all-to-all-done.10 = f32[32,1,1536]{2,1,0:T(1,128)S(1)} async-done(((f32[32,1,1536]{2,1,0:T(1,128)}), f32[32,1,1536]{2,1,0:T(1,128)S(1)}, u32[]{:S(2)}, u32[]{:S(2)}) %all-to-all-start.10) | async-done | bytes 196640 | tf_op jit(solution)/shard_map/all_to_all | solution.py:253
  256.2 0.7 shard_map.80
  256.9 15.7 %all-to-all-start.11 = ((f32[64,1,768]{2,1,0:T(1,128)}), f32[64,1,768]{2,1,0:T(1,128)S(1)}, u32[]{:S(2)}, u32[]{:S(2)}) async-start(f32[64,1,768]{2,1,0:T(1,128)} %bitcast.27), calls=%async_computation.11 | async-start | bytes 393216 | tf_op jit(solution)/shard_map/all_to_all | solution.py:253
  272.6 2.4 collective-permute-start.8
  275.0 1.2 collective-permute-done.8.other_ref
  276.2 8.6 %all-to-all-done.11 = f32[64,1,768]{2,1,0:T(1,128)S(1)} async-done(((f32[64,1,768]{2,1,0:T(1,128)}), f32[64,1,768]{2,1,0:T(1,128)S(1)}, u32[]{:S(2)}, u32[]{:S(2)}) %all-to-all-start.11) | async-done | bytes 196640 | tf_op jit(solution)/shard_map/all_to_all | solution.py:253
  284.8 0.1 broadcast_in_dim.51.root_ref
  284.9 1.2 shard_map.81
  (24 shorter events, 0.2 us)
Async XLA Ops:
  0.0 9.6 %copy-start = (f32[384,128]{1,0:T(8,128)S(1)}, f32[384,128]{1,0:T(8,128)}, u32[]{:S(2)}) copy-start(f32[384,128]{1,0:T(8,128)} %param.6) | copy-start | bytes 589828
  0.0 23.4 %collective-permute-start.2 = (f32[3,12,128,128]{3,2,1,0:T(8,128)}, f32[3,12,128,128]{3,2,1,0:T(8,128)}, u32[]{:S(2)}, u32[]{:S(2)}) collective-permute-start(f32[3,12,128,128]{3,2,1,0:T(8,128)} %param.7), channel_id=1, source_target_pairs={{0,1},{1,0},{2,3},{3,2},{4,5},{5,4},{6,7},{7,6},{8,9},{9,8},{10,11... | collective-permute-start | bytes 7077896 | tf_op jit(solution)/shard_map/ppermute | solution.py:22
  9.6 1.4 copy-start.6
  10.8 0.7 copy-start.2
  10.8 4.2 %copy-start.4 = (s32[3,12]{1,0:T(4,128)S(1)}, s32[3,12]{1,0:T(4,128)}, u32[]{:S(2)}) copy-start(s32[3,12]{1,0:T(4,128)} %param.8) | copy-start | bytes 436
  10.8 4.2 %copy-start.5 = (s32[3,1]{0,1:T(1,128)S(1)}, s32[3,1]{0,1:T(1,128)}, u32[]{:S(2)}) copy-start(s32[3,1]{0,1:T(1,128)} %param.9) | copy-start | bytes 40
  11.6 11.9 %copy-start.1 = (f32[3,12,128,128]{3,2,1,0:T(8,128)S(1)}, f32[3,12,128,128]{3,2,1,0:T(8,128)}, u32[]{:S(2)}) copy-start(f32[3,12,128,128]{3,2,1,0:T(8,128)} %param.7) | copy-start | bytes 7077892
  12.2 13.8 %collective-permute-start = (f32[192,128]{1,0:T(8,128)S(1)}, f32[192,128]{1,0:T(8,128)S(1)}, u32[]{:S(2)}, u32[]{:S(2)}) collective-permute-start(f32[192,128]{1,0:T(8,128)S(1)} %select_n.68), channel_id=1, source_target_pairs={{0,0},{1,1},{2,130},{3,131},{4,260},{5,261},{6,390},{7,391},{8,8},... | collective-permute-start | bytes 294920 | tf_op jit(solution)/shard_map/ppermute | solution.py:22
  13.0 13.0 %collective-permute-start.1 = (f32[192,128]{1,0:T(8,128)S(1)}, f32[192,128]{1,0:T(8,128)S(1)}, u32[]{:S(2)}, u32[]{:S(2)}) collective-permute-start(f32[192,128]{1,0:T(8,128)S(1)} %select_n.68), channel_id=1, source_target_pairs={{0,64},{1,65},{2,194},{3,195},{4,324},{5,325},{6,454},{7,455},{8,7... | collective-permute-start | bytes 294920 | tf_op jit(solution)/shard_map/ppermute | solution.py:22
  15.0 8.3 %collective-permute-start.3 = (s32[3,12]{1,0:T(4,128)S(1)}, s32[3,12]{1,0:T(4,128)S(1)}, u32[]{:S(2)}, u32[]{:S(2)}) collective-permute-start(s32[3,12]{1,0:T(4,128)S(1)} %fusion.1), channel_id=1, source_target_pairs={{0,1},{1,0},{2,3},{3,2},{4,5},{5,4},{6,7},{7,6},{8,9},{9,8},{10,11... | collective-permute-start | bytes 440 | tf_op jit(solution)/shard_map/ppermute | solution.py:22
  17.6 8.4 %collective-permute-start.4 = (f32[192,128]{1,0:T(8,128)S(1)}, f32[192,128]{1,0:T(8,128)S(1)}, u32[]{:S(2)}, u32[]{:S(2)}) collective-permute-start(f32[192,128]{1,0:T(8,128)S(1)} %reshape.110.scale_ref), channel_id=1, source_target_pairs={{0,448},{1,449},{2,450},{3,451},{4,452},{5,453},{6,454},{7,455},{8... | collective-permute-start | bytes 294920 | tf_op jit(solution)/shard_map/ppermute | solution.py:22
  27.0 33.7 %all-to-all-start = ((f32[8,192,128]{2,1,0:T(8,128)}), f32[8,192,128]{2,1,0:T(8,128)S(1)}, u32[]{:S(2)}, u32[]{:S(2)}) async-start(f32[8,192,128]{2,1,0:T(8,128)} %broadcast_select_fusion), calls=%async_computation | async-start | bytes 1572864 | tf_op jit(solution)/shard_map/all_to_all | solution.py:242
  30.6 30.1 %collective-permute-start.5 = (f32[2312,128]{1,0:T(8,128)}, f32[2312,128]{1,0:T(8,128)}, u32[]{:S(2)}, u32[]{:S(2)}) collective-permute-start(f32[2312,128]{1,0:T(8,128)} %select_maximum_fusion), channel_id=1, source_target_pairs={{0,448},{1,449},{2,450},{3,451},{4,452},{5,453},{6,454},{7,455},{8... | collective-permute-start | bytes 3551240 | tf_op jit(solution)/shard_map/ppermute | solution.py:22
  60.7 8.9 %collective-permute-start.6 = (f32[2312,128]{1,0:T(8,128)}, f32[2312,128]{1,0:T(8,128)S(1)}, u32[]{:S(2)}, u32[]{:S(2)}) collective-permute-start(f32[2312,128]{1,0:T(8,128)} %collective-permute-done.5.mine_ref), channel_id=1, source_target_pairs={{0,1},{1,0},{2,3},{3,2},{4,5},{5,4},{6,7},{7,6},{8,9},{9,8},{10,11... | collective-permute-start | bytes 3551240 | tf_op jit(solution)/shard_map/ppermute | solution.py:22
  242.8 42.2 %copy-start.3 = (f32[384,128]{1,0:T(8,128)S(1)}, f32[384,128]{1,0:T(8,128)}, u32[]{:S(2)}) copy-start(f32[384,128]{1,0:T(8,128)} %copy-done.2) | copy-start | bytes 589828
  242.8 13.5 %all-to-all-start.10 = ((f32[32,1,1536]{2,1,0:T(1,128)}), f32[32,1,1536]{2,1,0:T(1,128)S(1)}, u32[]{:S(2)}, u32[]{:S(2)}) async-start(f32[32,1,1536]{2,1,0:T(1,128)} %bitcast.25), calls=%async_computation.10 | async-start | bytes 393216 | tf_op jit(solution)/shard_map/all_to_all | solution.py:253
  247.3 25.3 %collective-permute-start.7 = (f32[576,128]{1,0:T(8,128)S(1)}, f32[576,128]{1,0:T(8,128)S(1)}, u32[]{:S(2)}, u32[]{:S(2)}) collective-permute-start(f32[576,128]{1,0:T(8,128)S(1)} %pad_maximum_fusion), channel_id=1, source_target_pairs={{0,0},{1,1},{2,386},{3,387},{4,260},{5,261},{6,134},{7,135},{8,8},... | collective-permute-start | bytes 884744 | tf_op jit(solution)/shard_map/ppermute | solution.py:22
  256.9 27.9 %all-to-all-start.11 = ((f32[64,1,768]{2,1,0:T(1,128)}), f32[64,1,768]{2,1,0:T(1,128)S(1)}, u32[]{:S(2)}, u32[]{:S(2)}) async-start(f32[64,1,768]{2,1,0:T(1,128)} %bitcast.27), calls=%async_computation.11 | async-start | bytes 393216 | tf_op jit(solution)/shard_map/all_to_all | solution.py:253
  272.6 3.6 %collective-permute-start.8 = (f32[576,128]{1,0:T(8,128)S(1)}, f32[576,128]{1,0:T(8,128)S(1)}, u32[]{:S(2)}, u32[]{:S(2)}) collective-permute-start(f32[576,128]{1,0:T(8,128)S(1)} %collective-permute-done.7.mine_ref), channel_id=1, source_target_pairs={{0,1},{1,0},{2,3},{3,2},{4,5},{5,4},{6,7},{7,6},{8,9},{9,8},{10,11... | collective-permute-start | bytes 884744 | tf_op jit(solution)/shard_map/ppermute | solution.py:22

commit v3 on v2

--- a/solution.py
+++ b/solution.py
@@ -90,6 +90,10 @@
     multiply(index_ref, tiles_ref, scale_ref, source_ref, gathered_ref, near_ref)
 
 
+def last_kernel(index_ref, tiles_ref, scale_ref, source_ref, out_ref, gathered_ref):
+    multiply(index_ref, tiles_ref, scale_ref, source_ref, gathered_ref, out_ref)
+
+
 def far_kernel(members, index_ref, tiles_ref, scale_ref, source_ref, near_ref, out_ref, gathered_ref, far_ref):
     multiply(index_ref, tiles_ref, scale_ref, source_ref, gathered_ref, far_ref)
     piece = near_ref.shape[0] // members
@@ -125,6 +129,12 @@
     both = jax.ShapeDtypeStruct((2 * rows * HALF, 128), jnp.float32)
     scratch = [pltpu.VMEM((rows * HALF, 128), jnp.float32)]
     return product_call(functools.partial(far_kernel, members), 5, rows, slots, both, scratch)(index, tiles, scale, source, near)
+
+
+def last_product(index, tiles, scale, source):
+    rows, slots = index.shape
+    sums = jax.ShapeDtypeStruct((rows * HALF, 128), jnp.float32)
+    return product_call(last_kernel, 4, rows, slots, sums)(index, tiles, scale, source)
 
 
 def piece_sums(came_ref, lines, pairs):
@@ -154,19 +164,10 @@
             out_ref[first + piece:first + 2 * piece] = sums[(line - 2 * pair - 1) % lines]
 
 
-def hand_out_kernel(lines, pairs, came_ref, out_ref):
-    sums = piece_sums(came_ref, lines, pairs)
-    piece = sums[0].shape[0]
-    for line in range(lines):
-        for member in range(2 * pairs):
-            first = (line * 2 * pairs + member) * piece
-            out_ref[first:first + piece] = sums[line]
-
-
-def hand(kernel, came, lines, pairs):
+def hand_on(came, lines, pairs):
     vmem = pl.BlockSpec(memory_space=pltpu.VMEM)
     return pl.pallas_call(
-        functools.partial(kernel, lines, pairs),
+        functools.partial(hand_on_kernel, lines, pairs),
         in_specs=[vmem],
         out_specs=vmem,
         out_shape=jax.ShapeDtypeStruct(came.shape, jnp.float32),
@@ -197,26 +198,19 @@
     )(rank_y, came)
 
 
-def finish_kernel(members, core_ref, ordered_ref, root_ref, mine_ref, other_ref, last_ref, out_ref, halves_ref):
+def finish_kernel(core_ref, ordered_ref, root_ref, mine_ref, mine_last_ref, other_ref, other_last_ref, out_ref):
     out_ref[0] = ordered_ref[...]
     left = lax.broadcasted_iota(jnp.int32, (HALF, 128), 1) < HALF
     first_core = core_ref[0] == 0
     blocks = ordered_ref.shape[0] // 128
     size = blocks * HALF
-    piece = size // members
-    for m in range(members):
-        for half in range(2):
-            first = (2 * m + half) * piece
-            halves_ref[half, m * piece:(m + 1) * piece] = last_ref[first:first + piece]
     for hop in range(HOPS):
         for b in range(blocks):
-            if hop < HOPS - 1:
-                at = slice(hop * size + b * HALF, hop * size + (b + 1) * HALF)
-                a = jnp.where(first_core, mine_ref[at], other_ref[at])
-                c = jnp.where(first_core, other_ref[at], mine_ref[at])
-            else:
-                at = slice(b * HALF, (b + 1) * HALF)
-                a, c = halves_ref[0, at], halves_ref[1, at]
+            at = b * HALF if hop == HOPS - 1 else hop * size + b * HALF
+            mine = (mine_last_ref if hop == HOPS - 1 else mine_ref)[at:at + HALF]
+            other = (other_last_ref if hop == HOPS - 1 else other_ref)[at:at + HALF]
+            a = jnp.where(first_core, mine, other)
+            c = jnp.where(first_core, other, mine)
             first = b * 128
             top = jnp.where(left, a, pltpu.roll(c, HALF, 1))
             bottom = jnp.where(left, pltpu.roll(a, HALF, 1), c)
@@ -224,16 +218,15 @@
             out_ref[hop + 1, first + HALF:first + 128] = bottom * root_ref[first + HALF:first + 128]
 
 
-def finish(core, ordered, root, mine, other, last, members):
+def finish(core, ordered, root, fields):
     vmem = pl.BlockSpec(memory_space=pltpu.VMEM)
     return pl.pallas_call(
-        functools.partial(finish_kernel, members),
-        in_specs=[pl.BlockSpec(memory_space=pltpu.SMEM)] + [vmem] * 5,
+        finish_kernel,
+        in_specs=[pl.BlockSpec(memory_space=pltpu.SMEM)] + [vmem] * (2 + len(fields)),
         out_specs=vmem,
         out_shape=jax.ShapeDtypeStruct((HOPS + 1,) + ordered.shape, jnp.float32),
-        scratch_shapes=[pltpu.VMEM((2, ordered.shape[0] // 2, 128), jnp.float32)],
-        compiler_params=pltpu.CompilerParams(vmem_limit_bytes=VMEM_BYTES),
-    )(core, ordered, root, mine, other, last)
+        compiler_params=pltpu.CompilerParams(vmem_limit_bytes=VMEM_BYTES),
+    )(core, ordered, root, *fields)
 
 
 def ring_exchange(chunks):
@@ -242,13 +235,19 @@
     return lax.all_to_all(chunks, "blk", 0, 0, axis_index_groups=rings)
 
 
-def plane_exchange(block, span, cores):
+def pair_exchange(block, pairs):
     cycle, groups = lax.axis_size("blk"), lax.axis_size("rep")
-    planes = []
-    for y in range(span):
-        for core in range(0, 2, cores):
-            starts = range(core, groups, 2) if cores == 1 else range(groups)
-            planes.append([p * groups + w for p in range(y, cycle, span) for w in starts])
+    sets = [[p * groups + w for w in range(core, groups, 2)] for p in range(cycle) for core in range(2)]
+    copies = jnp.broadcast_to(block[None], (pairs, *block.shape))
+    return lax.all_to_all(copies, ("blk", "rep"), 0, 0, axis_index_groups=sets)
+
+
+def plane_exchange(block, span):
+    cycle, groups = lax.axis_size("blk"), lax.axis_size("rep")
+    planes = [
+        [p * groups + w for p in range(y, cycle, span) for w in range(core, groups, 2)]
+        for y in range(span) for core in range(2)
+    ]
     pieces = block.reshape(len(planes[0]), 1, -1)
     moved = lax.all_to_all(pieces, ("blk", "rep"), 0, 0, axis_index_groups=planes)
     return moved.reshape(block.shape)
@@ -270,9 +269,6 @@
     swapped_index = swap_cores(index)
     near_index = jnp.where(first_core, index, swapped_index)
     leaving = jnp.where(first_core, swapped[:, :mid], tile_values[:, mid:]).reshape(-1, 128)
-    leaving_index = jnp.where(first_core, swapped_index, index).astype(jnp.float32)
-    index_rows = jnp.pad(leaving_index, ((0, 8 - rows), (0, 128 - slots)))
-    leaving = jnp.concatenate([leaving, index_rows])
 
     ordered = jnp.take(features, curve_order - rank_blk * features.shape[0], axis=0, mode="clip")
     count = degrees.astype(jnp.float32)
@@ -294,35 +290,41 @@
     pairs = lax.axis_size("rep") // 2
     members = lines * pairs
     own, behind = send(start, aligned), send(start, behind_aligned)
-    far_scale = send(scale, lambda p, w: (p - span, w))
+    leaving_index = jnp.where(first_core, swapped_index, index).astype(jnp.float32)
+    index_rows = jnp.pad(leaving_index, ((0, 8 - rows), (0, 128 - slots)))
+    far_parts = send(jnp.concatenate([scale, index_rows]), lambda p, w: (p - span, w))
+    own, behind, far_parts, leaving = lax.optimization_barrier((own, behind, far_parts, leaving))
+    came = send(leaving, lambda p, w: (p - span, w))
+    far_scale = far_parts[:rows * HALF]
+    far_index = far_parts[rows * HALF:][:rows, :slots].astype(jnp.int32)
     every = [("mine", s) for s in range(slots)], [("other", s) for s in range(slots)]
     flat = tile_values.reshape(-1, 128), swapped.reshape(-1, 128)
     near_tiles = tile_parts(core_ref, *flat, rows, *every)
-    own, behind, leaving, far_scale = lax.optimization_barrier((own, behind, leaving, far_scale))
-    came = send(leaving, lambda p, w: (p - span, w))
     ring = jnp.arange(span, dtype=jnp.int32)[:, None, None]
     chunks = jnp.where(ring >= rank_y, own[None], behind[None])
     kept = []
-    for hop in range(HOPS):
+    for hop in range(HOPS - 1):
         units = ring_exchange(chunks).reshape(-1, 128)
         if hop == 0:
-            units, came = lax.optimization_barrier((units, came))
+            came, near_tiles = lax.optimization_barrier((came, near_tiles))
         near, source = near_product(near_index, near_tiles, scale, units)
         if hop == 0:
             rest = swap_cores(came)
             low_slots = [("mine", s) for s in range(mid)] + [("other", s) for s in range(mid)]
             high_slots = [("other", s) for s in range(mid)] + [("mine", s) for s in range(mid)]
-            far_index = came[rows * mid * 128:][:rows, :slots].astype(jnp.int32)
             far_tiles = tile_parts(core_ref, came, rest, rows, low_slots, high_slots)
         sums = far_product(far_index, far_tiles, far_scale, source, near, members)
-        pieces = plane_exchange(sums, span, 1)
-        if hop < HOPS - 1:
-            came_units = plane_exchange(hand(hand_on_kernel, pieces, lines, pairs), span, 1)
-            chunks, own = choose(rank_y.reshape(1), came_units, members, span)
-            kept.append(own)
-    last = plane_exchange(hand(hand_out_kernel, pieces, lines, pairs), span, 2)
+        pieces = plane_exchange(sums, span)
+        came_units = plane_exchange(hand_on(pieces, lines, pairs), span)
+        chunks, own = choose(rank_y.reshape(1), came_units, members, span)
+        kept.append(own)
     mine = send(jnp.concatenate(kept), lambda p, w: (p - 2 * span * (w // 2), w))
-    return finish(core_ref, ordered, root, mine, swap_cores(mine), last, members)
+    units = ring_exchange(chunks).reshape(-1, 128)
+    near, source = near_product(near_index, near_tiles, scale, units)
+    far = last_product(far_index, far_tiles, far_scale, source)
+    chip = near + send(far, lambda p, w: (p + span, w))
+    last = pair_exchange(chip, pairs).sum(axis=0)
+    return finish(core_ref, ordered, root, [mine, last, swap_cores(mine), swap_cores(last)])
 
 
 def solution(mesh):

time: 287 us -> 271 us (0.944)
  waiting for transfers between devices: 42.8 us -> 22 us
  starting transfers between devices: 55.3 us -> 63.7 us
  blocking collectives: 159 us -> 155 us
    ppermute x9 -> x11, starting transfers between devices: 31.7 us -> 56.7 us  [send(): return lax.ppermute(block, ('blk', 'rep'), route)]
    all_to_all x2 -> x1, waiting for transfers between devices: 16.9 us -> 0.01 us  [pair_exchange(): return lax.all_to_all(copies, ('blk', 'rep'), 0, 0, axis_index_groups=sets)]
    all_to_all x2 -> x1, starting transfers between devices: 20.1 us -> 3.46 us  [pair_exchange(): return lax.all_to_all(copies, ('blk', 'rep'), 0, 0, axis_index_groups=sets)]
    all_to_all x6, blocking collectives: 93.3 us -> 89.1 us  [plane_exchange(): lax.all_to_all(pieces, ('blk', 'rep'), 0, 0, axis_index_groups=planes)]
    ppermute x9 -> x11, waiting for transfers between devices: 25.8 us -> 22 us  [send(): return lax.ppermute(block, ('blk', 'rep'), route)]
    pallas_call x4 -> x3, Pallas kernels: 6.58 us -> 4.46 us  [far_product(): product_call(functools.partial(far_kernel, members), 5, rows, slots, both...]
  transfers between devices with their start and end apart: 12 -> 13, of which waited for: 4 -> 5; matrix products, arithmetic and copies ran while one was open for 2% -> 3% of each run, Pallas kernels for 2% -> 2%
where the time goes in v3:
time: 271 us; the launch traced here: 270 us
  blocking collectives  155 us (57%)
  starting transfers between devices  63.7 us (24%)
  waiting for transfers between devices  22 us (8%)
  Pallas kernels  19.6 us (7%)
  local copies, waits for them, and re-layouts  4.92 us (2%)
  other arithmetic  4.84 us (2%)
    all_to_all x6, blocking collectives, plane_exchange(): lax.all_to_all(pieces, ('blk', 'rep'), 0, 0, axis_index_groups=planes)  89.1 us
    all_to_all x3, blocking collectives, ring_exchange(): return lax.all_to_all(chunks, 'blk', 0, 0, axis_index_groups=rings)  65.5 us
    ppermute x11, starting transfers between devices, send(): return lax.ppermute(block, ('blk', 'rep'), route)  56.7 us
    ppermute x11, waiting for transfers between devices, send(): return lax.ppermute(block, ('blk', 'rep'), route)  22 us
    pallas_call x4, Pallas kernels, near_product(): product_call(near_kernel, 4, rows, slots, [sums, source])  6.87 us
  transfers between devices with their start and end apart: 13, of which 5 were waited for; matrix products, arithmetic and copies ran while one was open for 3% of the time, Pallas kernels for 2%

profile of v3, /device:TPU:1, one launch (start us, length us, event | category | flops | bytes accessed | tf_op | source)
XLA Modules:
  0.0 270.1 jit_solution(10154157424023266722)
XLA Ops:
  0.0 8.9 %collective-permute-start.4 = (f32[3,12,128,128]{3,2,1,0:T(8,128)}, f32[3,12,128,128]{3,2,1,0:T(8,128)}, u32[]{:S(2)}, u32[]{:S(2)}) collective-permute-start(f32[3,12,128,128]{3,2,1,0:T(8,128)} %param.7), channel_id=1, source_target_pairs={{0,1},{1,0},{2,3},{3,2},{4,5},{5,4},{6,7},{7,6},{8,9},{9,8},{10,11... | collective-permute-start | bytes 7077896 | tf_op jit(solution)/shard_map/ppermute | solution.py:22
  9.0 0.7 broadcast_subtract_fusion
  9.6 0.0 copy-start.1
  9.7 1.1 gather_fusion
  10.8 0.2 gather.7
  11.1 0.1 broadcast_in_dim.58
  11.2 0.1 copy.21
  11.3 0.4 copy_multiply_fusion
  11.7 0.1 fusion
  11.8 0.2 select_n.68
  11.9 0.7 collective-permute-start
  12.6 1.9 collective-permute-start.1
  14.6 0.1 fusion.1
  14.6 1.9 collective-permute-start.2
  16.5 0.1 broadcast_in_dim.60
  16.6 0.1 copy.23
  16.8 0.3 broadcast_bitcast_fusion
  17.0 0.2 reshape.98.scale_ref
  17.2 0.5 collective-permute-done.2
  17.7 0.1 broadcast_select_fusion.1
  17.8 5.5 %collective-permute-start.3 = (f32[200,128]{1,0:T(8,128)S(1)}, f32[200,128]{1,0:T(8,128)S(1)}, u32[]{:S(2)}, u32[]{:S(2)}) collective-permute-start(f32[200,128]{1,0:T(8,128)S(1)} %select_maximum_fusion), channel_id=1, source_target_pairs={{0,448},{1,449},{2,450},{3,451},{4,452},{5,453},{6,454},{7,455},{8... | collective-permute-start | bytes 307208 | tf_op jit(solution)/shard_map/ppermute | solution.py:22
  23.2 0.0 collective-permute-done.4
  23.3 2.4 slice_select_fusion
  25.7 0.0 collective-permute-done
  25.7 5.7 %collective-permute-start.5 = (f32[2304,128]{1,0:T(8,128)}, f32[2304,128]{1,0:T(8,128)}, u32[]{:S(2)}, u32[]{:S(2)}) collective-permute-start(f32[2304,128]{1,0:T(8,128)} %bitcast.6), channel_id=1, source_target_pairs={{0,448},{1,449},{2,450},{3,451},{4,452},{5,453},{6,454},{7,455},{8... | collective-permute-start | bytes 3538952 | tf_op jit(solution)/shard_map/ppermute | solution.py:22
  31.4 1.0 broadcast_select_fusion
  32.4 3.5 %all-to-all-start = ((f32[8,192,128]{2,1,0:T(8,128)}), f32[8,192,128]{2,1,0:T(8,128)S(1)}, u32[]{:S(2)}, u32[]{:S(2)}) async-start(f32[8,192,128]{2,1,0:T(8,128)} %broadcast_select_fusion), calls=%async_computation | async-start | bytes 1572864 | tf_op jit(solution)/shard_map/all_to_all | solution.py:235
  36.0 0.0 copy-start.2
  36.0 1.7 copy-done.2
  37.7 2.7 shard_map.64.tiles_ref
  40.4 15.5 %collective-permute-done.5.mine_ref = f32[2304,128]{1,0:T(8,128)} collective-permute-done((f32[2304,128]{1,0:T(8,128)}, f32[2304,128]{1,0:T(8,128)}, u32[]{:S(2)}, u32[]{:S(2)}) %collective-permute-start.5) | collective-permute-done | bytes 1179680 | tf_op jit(solution)/shard_map/ppermute | solution.py:22
  55.9 3.9 %collective-permute-start.6 = (f32[2304,128]{1,0:T(8,128)}, f32[2304,128]{1,0:T(8,128)}, u32[]{:S(2)}, u32[]{:S(2)}) collective-permute-start(f32[2304,128]{1,0:T(8,128)} %collective-permute-done.5.mine_ref), channel_id=1, source_target_pairs={{0,1},{1,0},{2,3},{3,2},{4,5},{5,4},{6,7},{7,6},{8,9},{9,8},{10,11... | collective-permute-start | bytes 3538952 | tf_op jit(solution)/shard_map/ppermute | solution.py:22
  59.8 1.7 shard_map.66
  61.6 1.0 collective-permute-done.6.other_ref
  62.6 2.6 shard_map.65.tiles_ref
  65.2 1.5 shard_map.67
  66.7 19.3 %all_to_all.55 = f32[32,1,1536]{2,1,0:T(1,128)S(1)} all-to-all(f32[32,1,1536]{2,1,0:T(1,128)S(1)} %bitcast.33), channel_id=1, replica_groups={{0,2,4,6,64,66,68,70,128,130,132,134,192,194,196,198,256,258,260,262,32..., dimensions={0} | all-to-all | bytes 393216 | tf_op jit(solution)/shard_map/all_to_all | solution.py:252
  86.0 14.7 %all_to_all.56 = f32[32,1,1536]{2,1,0:T(1,128)S(1)} all-to-all(f32[32,1,1536]{2,1,0:T(1,128)S(1)} %bitcast.40), channel_id=1, replica_groups={{0,2,4,6,64,66,68,70,128,130,132,134,192,194,196,198,256,258,260,262,32..., dimensions={0} | all-to-all | bytes 393216 | tf_op jit(solution)/shard_map/all_to_all | solution.py:252
  100.7 0.1 shard_map.69
  100.8 26.2 %all_to_all.57 = f32[8,192,128]{2,1,0:T(8,128)S(1)} all-to-all(f32[8,192,128]{2,1,0:T(8,128)S(1)} %get-tuple-element.34), channel_id=1, replica_groups={{0,8,16,24,32,40,48,56},{64,72,80,88,96,104,112,120},{128,136,144,152,1..., dimensions={0} | all-to-all | bytes 1572864 | tf_op jit(solution)/shard_map/all_to_all | solution.py:235
  127.0 1.7 shard_map.70
  128.7 1.5 shard_map.71
  130.2 15.2 %all_to_all.58 = f32[32,1,1536]{2,1,0:T(1,128)S(1)} all-to-all(f32[32,1,1536]{2,1,0:T(1,128)S(1)} %bitcast.34), channel_id=1, replica_groups={{0,2,4,6,64,66,68,70,128,130,132,134,192,194,196,198,256,258,260,262,32..., dimensions={0} | all-to-all | bytes 393216 | tf_op jit(solution)/shard_map/all_to_all | solution.py:252
  145.4 13.2 %all_to_all.59 = f32[32,1,1536]{2,1,0:T(1,128)S(1)} all-to-all(f32[32,1,1536]{2,1,0:T(1,128)S(1)} %bitcast.42), channel_id=1, replica_groups={{0,2,4,6,64,66,68,70,128,130,132,134,192,194,196,198,256,258,260,262,32..., dimensions={0} | all-to-all | bytes 393216 | tf_op jit(solution)/shard_map/all_to_all | solution.py:252
  158.7 0.1 shard_map.73
  158.8 20.8 %all_to_all.60 = f32[8,192,128]{2,1,0:T(8,128)S(1)} all-to-all(f32[8,192,128]{2,1,0:T(8,128)S(1)} %get-tuple-element.38), channel_id=1, replica_groups={{0,8,16,24,32,40,48,56},{64,72,80,88,96,104,112,120},{128,136,144,152,1..., dimensions={0} | all-to-all | bytes 1572864 | tf_op jit(solution)/shard_map/all_to_all | solution.py:235
  179.5 1.7 shard_map.74
  181.2 1.5 shard_map.75
  182.7 13.5 %all_to_all.61 = f32[32,1,1536]{2,1,0:T(1,128)S(1)} all-to-all(f32[32,1,1536]{2,1,0:T(1,128)S(1)} %bitcast.35), channel_id=1, replica_groups={{0,2,4,6,64,66,68,70,128,130,132,134,192,194,196,198,256,258,260,262,32..., dimensions={0} | all-to-all | bytes 393216 | tf_op jit(solution)/shard_map/all_to_all | solution.py:252
  196.2 13.1 %all_to_all.62 = f32[32,1,1536]{2,1,0:T(1,128)S(1)} all-to-all(f32[32,1,1536]{2,1,0:T(1,128)S(1)} %bitcast.44), channel_id=1, replica_groups={{0,2,4,6,64,66,68,70,128,130,132,134,192,194,196,198,256,258,260,262,32..., dimensions={0} | all-to-all | bytes 393216 | tf_op jit(solution)/shard_map/all_to_all | solution.py:252
  209.4 0.1 shard_map.77
  209.4 18.5 %all_to_all.63 = f32[8,192,128]{2,1,0:T(8,128)S(1)} all-to-all(f32[8,192,128]{2,1,0:T(8,128)S(1)} %get-tuple-element.42), channel_id=1, replica_groups={{0,8,16,24,32,40,48,56},{64,72,80,88,96,104,112,120},{128,136,144,152,1..., dimensions={0} | all-to-all | bytes 1572864 | tf_op jit(solution)/shard_map/all_to_all | solution.py:235
  228.0 1.7 shard_map.78
  229.7 1.5 shard_map.79
  231.2 3.4 %collective-permute-start.8 = (f32[192,128]{1,0:T(8,128)S(1)}, f32[192,128]{1,0:T(8,128)S(1)}, u32[]{:S(2)}, u32[]{:S(2)}) collective-permute-start(f32[192,128]{1,0:T(8,128)S(1)} %shard_map.79), channel_id=1, source_target_pairs={{0,64},{1,65},{2,66},{3,67},{4,68},{5,69},{6,70},{7,71},{8,72},{9,... | collective-permute-start | bytes 294920 | tf_op jit(solution)/shard_map/ppermute | solution.py:22
  234.5 4.1 %collective-permute-done.8 = f32[192,128]{1,0:T(8,128)S(1)} collective-permute-done((f32[192,128]{1,0:T(8,128)S(1)}, f32[192,128]{1,0:T(8,128)S(1)}, u32[]{:S(2)}, u32[]{:S(2)}) %collective-permute-start.8) | collective-permute-done | bytes 98336 | tf_op jit(solution)/shard_map/ppermute | solution.py:22
  238.7 0.8 broadcast_in_dim.64
  239.4 3.5 %all-to-all-start.10 = ((f32[4,192,128]{2,1,0:T(8,128)}), f32[4,192,128]{2,1,0:T(8,128)S(1)}, u32[]{:S(2)}, u32[]{:S(2)}) async-start(f32[4,192,128]{2,1,0:T(8,128)} %broadcast_in_dim.64), calls=%async_computation.10 | async-start | bytes 786432 | tf_op jit(solution)/shard_map/all_to_all | solution.py:242
  242.9 0.7 collective-permute-start.7
  243.6 14.5 %collective-permute-start.9 = (f32[576,128]{1,0:T(8,128)S(1)}, f32[576,128]{1,0:T(8,128)S(1)}, u32[]{:S(2)}, u32[]{:S(2)}) collective-permute-start(f32[576,128]{1,0:T(8,128)S(1)} %collective-permute-done.7.mine_ref), channel_id=1, source_target_pairs={{0,1},{1,0},{2,3},{3,2},{4,5},{5,4},{6,7},{7,6},{8,9},{9,8},{10,11... | collective-permute-start | bytes 884744 | tf_op jit(solution)/shard_map/ppermute | solution.py:22
  258.2 9.6 %collective-permute-start.10 = (f32[192,128]{1,0:T(8,128)S(1)}, f32[192,128]{1,0:T(8,128)S(1)}, u32[]{:S(2)}, u32[]{:S(2)}) collective-permute-start(f32[192,128]{1,0:T(8,128)S(1)} %reduce_sum.9.mine_last_ref), channel_id=1, source_target_pairs={{0,1},{1,0},{2,3},{3,2},{4,5},{5,4},{6,7},{7,6},{8,9},{9,8},{10,11... | collective-permute-start | bytes 294920 | tf_op jit(solution)/shard_map/ppermute | solution.py:22
  267.9 0.9 collective-permute-done.10.other_last_ref
  268.8 0.1 broadcast_in_dim.57.root_ref
  268.9 1.2 shard_map.80
  (35 shorter events, 0.2 us)
Async XLA Ops:
  0.0 9.6 %copy-start = (f32[384,128]{1,0:T(8,128)S(1)}, f32[384,128]{1,0:T(8,128)}, u32[]{:S(2)}) copy-start(f32[384,128]{1,0:T(8,128)} %param.6) | copy-start | bytes 589828
  0.0 11.1 %copy-start.9 = (s32[384]{0:T(512)S(1)}, s32[384]{0:T(512)}, u32[]{:S(2)}) copy-start(s32[384]{0:T(512)} %param.10) | copy-start | bytes 4612
  0.0 14.5 %copy-start.7 = (s32[3,12]{1,0:T(4,128)S(1)}, s32[3,12]{1,0:T(4,128)}, u32[]{:S(2)}) copy-start(s32[3,12]{1,0:T(4,128)} %param.8) | copy-start | bytes 436
  0.0 14.5 %copy-start.8 = (s32[3,1]{0,1:T(1,128)S(1)}, s32[3,1]{0,1:T(1,128)}, u32[]{:S(2)}) copy-start(s32[3,1]{0,1:T(1,128)} %param.9) | copy-start | bytes 40
  0.0 23.2 %collective-permute-start.4 = (f32[3,12,128,128]{3,2,1,0:T(8,128)}, f32[3,12,128,128]{3,2,1,0:T(8,128)}, u32[]{:S(2)}, u32[]{:S(2)}) collective-permute-start(f32[3,12,128,128]{3,2,1,0:T(8,128)} %param.7), channel_id=1, source_target_pairs={{0,1},{1,0},{2,3},{3,2},{4,5},{5,4},{6,7},{7,6},{8,9},{9,8},{10,11... | collective-permute-start | bytes 7077896 | tf_op jit(solution)/shard_map/ppermute | solution.py:22
  9.6 13.6 %copy-start.1 = (f32[3,12,128,128]{3,2,1,0:T(8,128)S(1)}, f32[3,12,128,128]{3,2,1,0:T(8,128)}, u32[]{:S(2)}) copy-start(f32[3,12,128,128]{3,2,1,0:T(8,128)} %param.7) | copy-start | bytes 7077892
  10.8 6.0 %copy-start.3 = (f32[384,128]{1,0:T(8,128)}, f32[384,128]{1,0:T(8,128)S(1)}, u32[]{:S(2)}) copy-start(f32[384,128]{1,0:T(8,128)S(1)} %gather_fusion) | copy-start | bytes 589828
  11.9 13.7 %collective-permute-start = (f32[192,128]{1,0:T(8,128)S(1)}, f32[192,128]{1,0:T(8,128)S(1)}, u32[]{:S(2)}, u32[]{:S(2)}) collective-permute-start(f32[192,128]{1,0:T(8,128)S(1)} %select_n.68), channel_id=1, source_target_pairs={{0,0},{1,1},{2,130},{3,131},{4,260},{5,261},{6,390},{7,391},{8,8},... | collective-permute-start | bytes 294920 | tf_op jit(solution)/shard_map/ppermute | solution.py:22
  12.6 13.1 %collective-permute-start.1 = (f32[192,128]{1,0:T(8,128)S(1)}, f32[192,128]{1,0:T(8,128)S(1)}, u32[]{:S(2)}, u32[]{:S(2)}) collective-permute-start(f32[192,128]{1,0:T(8,128)S(1)} %select_n.68), channel_id=1, source_target_pairs={{0,64},{1,65},{2,194},{3,195},{4,324},{5,325},{6,454},{7,455},{8,7... | collective-permute-start | bytes 294920 | tf_op jit(solution)/shard_map/ppermute | solution.py:22
  14.6 3.0 %collective-permute-start.2 = (s32[3,12]{1,0:T(4,128)S(1)}, s32[3,12]{1,0:T(4,128)S(1)}, u32[]{:S(2)}, u32[]{:S(2)}) collective-permute-start(s32[3,12]{1,0:T(4,128)S(1)} %fusion.1), channel_id=1, source_target_pairs={{0,1},{1,0},{2,3},{3,2},{4,5},{5,4},{6,7},{7,6},{8,9},{9,8},{10,11... | collective-permute-start | bytes 440 | tf_op jit(solution)/shard_map/ppermute | solution.py:22
  17.8 7.9 %collective-permute-start.3 = (f32[200,128]{1,0:T(8,128)S(1)}, f32[200,128]{1,0:T(8,128)S(1)}, u32[]{:S(2)}, u32[]{:S(2)}) collective-permute-start(f32[200,128]{1,0:T(8,128)S(1)} %select_maximum_fusion), channel_id=1, source_target_pairs={{0,448},{1,449},{2,450},{3,451},{4,452},{5,453},{6,454},{7,455},{8... | collective-permute-start | bytes 307208 | tf_op jit(solution)/shard_map/ppermute | solution.py:22
  25.7 6.7 %copy-start.5 = (f32[200,128]{1,0:T(8,128)}, f32[200,128]{1,0:T(8,128)S(1)}, u32[]{:S(2)}) copy-start(f32[200,128]{1,0:T(8,128)S(1)} %collective-permute-done.3) | copy-start | bytes 307204
  25.7 30.1 %collective-permute-start.5 = (f32[2304,128]{1,0:T(8,128)}, f32[2304,128]{1,0:T(8,128)}, u32[]{:S(2)}, u32[]{:S(2)}) collective-permute-start(f32[2304,128]{1,0:T(8,128)} %bitcast.6), channel_id=1, source_target_pairs={{0,448},{1,449},{2,450},{3,451},{4,452},{5,453},{6,454},{7,455},{8... | collective-permute-start | bytes 3538952 | tf_op jit(solution)/shard_map/ppermute | solution.py:22
  32.4 27.4 %all-to-all-start = ((f32[8,192,128]{2,1,0:T(8,128)}), f32[8,192,128]{2,1,0:T(8,128)S(1)}, u32[]{:S(2)}, u32[]{:S(2)}) async-start(f32[8,192,128]{2,1,0:T(8,128)} %broadcast_select_fusion), calls=%async_computation | async-start | bytes 1572864 | tf_op jit(solution)/shard_map/all_to_all | solution.py:235
  36.0 1.7 copy-start.2
  37.7 22.1 %copy-start.6 = (f32[200,128]{1,0:T(8,128)S(1)}, f32[200,128]{1,0:T(8,128)}, u32[]{:S(2)}) copy-start(f32[200,128]{1,0:T(8,128)} %copy-done.5) | copy-start | bytes 307204
  55.9 6.7 %collective-permute-start.6 = (f32[2304,128]{1,0:T(8,128)}, f32[2304,128]{1,0:T(8,128)}, u32[]{:S(2)}, u32[]{:S(2)}) collective-permute-start(f32[2304,128]{1,0:T(8,128)} %collective-permute-done.5.mine_ref), channel_id=1, source_target_pairs={{0,1},{1,0},{2,3},{3,2},{4,5},{5,4},{6,7},{7,6},{8,9},{9,8},{10,11... | collective-permute-start | bytes 3538952 | tf_op jit(solution)/shard_map/ppermute | solution.py:22
  229.7 39.2 %copy-start.4 = (f32[384,128]{1,0:T(8,128)S(1)}, f32[384,128]{1,0:T(8,128)}, u32[]{:S(2)}) copy-start(f32[384,128]{1,0:T(8,128)} %copy-done.3) | copy-start | bytes 589828
  231.2 7.5 %collective-permute-start.8 = (f32[192,128]{1,0:T(8,128)S(1)}, f32[192,128]{1,0:T(8,128)S(1)}, u32[]{:S(2)}, u32[]{:S(2)}) collective-permute-start(f32[192,128]{1,0:T(8,128)S(1)} %shard_map.79), channel_id=1, source_target_pairs={{0,64},{1,65},{2,66},{3,67},{4,68},{5,69},{6,70},{7,71},{8,72},{9,... | collective-permute-start | bytes 294920 | tf_op jit(solution)/shard_map/ppermute | solution.py:22
  239.4 18.7 %all-to-all-start.10 = ((f32[4,192,128]{2,1,0:T(8,128)}), f32[4,192,128]{2,1,0:T(8,128)S(1)}, u32[]{:S(2)}, u32[]{:S(2)}) async-start(f32[4,192,128]{2,1,0:T(8,128)} %broadcast_in_dim.64), calls=%async_computation.10 | async-start | bytes 786432 | tf_op jit(solution)/shard_map/all_to_all | solution.py:242
  242.9 0.7 collective-permute-start.7
  243.6 24.2 %collective-permute-start.9 = (f32[576,128]{1,0:T(8,128)S(1)}, f32[576,128]{1,0:T(8,128)S(1)}, u32[]{:S(2)}, u32[]{:S(2)}) collective-permute-start(f32[576,128]{1,0:T(8,128)S(1)} %collective-permute-done.7.mine_ref), channel_id=1, source_target_pairs={{0,1},{1,0},{2,3},{3,2},{4,5},{5,4},{6,7},{7,6},{8,9},{9,8},{10,11... | collective-permute-start | bytes 884744 | tf_op jit(solution)/shard_map/ppermute | solution.py:22
  258.2 10.6 %collective-permute-start.10 = (f32[192,128]{1,0:T(8,128)S(1)}, f32[192,128]{1,0:T(8,128)S(1)}, u32[]{:S(2)}, u32[]{:S(2)}) collective-permute-start(f32[192,128]{1,0:T(8,128)S(1)} %reduce_sum.9.mine_last_ref), channel_id=1, source_target_pairs={{0,1},{1,0},{2,3},{3,2},{4,5},{5,4},{6,7},{7,6},{8,9},{9,8},{10,11... | collective-permute-start | bytes 294920 | tf_op jit(solution)/shard_map/ppermute | solution.py:22

commit v4 on v3

--- a/solution.py
+++ b/solution.py
@@ -292,21 +292,23 @@
     own, behind = send(start, aligned), send(start, behind_aligned)
     leaving_index = jnp.where(first_core, swapped_index, index).astype(jnp.float32)
     index_rows = jnp.pad(leaving_index, ((0, 8 - rows), (0, 128 - slots)))
-    far_parts = send(jnp.concatenate([scale, index_rows]), lambda p, w: (p - span, w))
-    own, behind, far_parts, leaving = lax.optimization_barrier((own, behind, far_parts, leaving))
+    far_rows = jnp.concatenate([scale, index_rows])
+    own, behind, leaving = lax.optimization_barrier((own, behind, leaving))
     came = send(leaving, lambda p, w: (p - span, w))
-    far_scale = far_parts[:rows * HALF]
-    far_index = far_parts[rows * HALF:][:rows, :slots].astype(jnp.int32)
     every = [("mine", s) for s in range(slots)], [("other", s) for s in range(slots)]
     flat = tile_values.reshape(-1, 128), swapped.reshape(-1, 128)
     near_tiles = tile_parts(core_ref, *flat, rows, *every)
+    near_tiles, far_rows = lax.optimization_barrier((near_tiles, far_rows))
+    far_parts = send(far_rows, lambda p, w: (p - span, w))
     ring = jnp.arange(span, dtype=jnp.int32)[:, None, None]
     chunks = jnp.where(ring >= rank_y, own[None], behind[None])
     kept = []
     for hop in range(HOPS - 1):
         units = ring_exchange(chunks).reshape(-1, 128)
         if hop == 0:
-            came, near_tiles = lax.optimization_barrier((came, near_tiles))
+            came, near_tiles, far_parts = lax.optimization_barrier((came, near_tiles, far_parts))
+            far_scale = far_parts[:rows * HALF]
+            far_index = far_parts[rows * HALF:][:rows, :slots].astype(jnp.int32)
         near, source = near_product(near_index, near_tiles, scale, units)
         if hop == 0:
             rest = swap_cores(came)
@@ -320,8 +322,8 @@
         kept.append(own)
     mine = send(jnp.concatenate(kept), lambda p, w: (p - 2 * span * (w // 2), w))
     units = ring_exchange(chunks).reshape(-1, 128)
-    near, source = near_product(near_index, near_tiles, scale, units)
-    far = last_product(far_index, far_tiles, far_scale, source)
+    far, source = near_product(far_index, far_tiles, far_scale, units)
+    near = last_product(near_index, near_tiles, scale, source)
     chip = near + send(far, lambda p, w: (p + span, w))
     last = pair_exchange(chip, pairs).sum(axis=0)
     return finish(core_ref, ordered, root, [mine, last, swap_cores(mine), swap_cores(last)])

time: 271 us -> 267 us (0.985)
  starting transfers between devices: 63.7 us -> 57.7 us
    ppermute x11, starting transfers between devices: 56.7 us -> 50.4 us  [send(): return lax.ppermute(block, ('blk', 'rep'), route)]
    all_to_all x6, blocking collectives: 89.1 us -> 92.2 us  [plane_exchange(): lax.all_to_all(pieces, ('blk', 'rep'), 0, 0, axis_index_groups=planes)]
where the time goes in v4:
time: 267 us; the launch traced here: 266 us
  blocking collectives  156 us (58%)
  starting transfers between devices  57.7 us (22%)
  waiting for transfers between devices  22.9 us (9%)
  Pallas kernels  19.6 us (7%)
  local copies, waits for them, and re-layouts  4.92 us (2%)
  other arithmetic  4.85 us (2%)
    all_to_all x6, blocking collectives, plane_exchange(): lax.all_to_all(pieces, ('blk', 'rep'), 0, 0, axis_index_groups=planes)  92.2 us
    all_to_all x3, blocking collectives, ring_exchange(): return lax.all_to_all(chunks, 'blk', 0, 0, axis_index_groups=rings)  63.7 us
    ppermute x11, starting transfers between devices, send(): return lax.ppermute(block, ('blk', 'rep'), route)  50.4 us
    ppermute x11, waiting for transfers between devices, send(): return lax.ppermute(block, ('blk', 'rep'), route)  22.9 us
    pallas_call x4, Pallas kernels, near_product(): product_call(near_kernel, 4, rows, slots, [sums, source])  6.91 us
  transfers between devices with their start and end apart: 13, of which 5 were waited for; matrix products, arithmetic and copies ran while one was open for 3% of the time, Pallas kernels for 2%

profile of v4, /device:TPU:1, one launch (start us, length us, event | category | flops | bytes accessed | tf_op | source)
XLA Modules:
  0.0 266.3 jit_solution(3421075692358942306)
XLA Ops:
  0.0 9.0 %collective-permute-start.2 = (f32[3,12,128,128]{3,2,1,0:T(8,128)}, f32[3,12,128,128]{3,2,1,0:T(8,128)}, u32[]{:S(2)}, u32[]{:S(2)}) collective-permute-start(f32[3,12,128,128]{3,2,1,0:T(8,128)} %param.7), channel_id=1, source_target_pairs={{0,1},{1,0},{2,3},{3,2},{4,5},{5,4},{6,7},{7,6},{8,9},{9,8},{10,11... | collective-permute-start | bytes 7077896 | tf_op jit(solution)/shard_map/ppermute | solution.py:22
  9.1 0.7 broadcast_subtract_fusion
  9.8 1.1 gather_fusion
  10.9 0.2 gather.7
  11.2 0.1 broadcast_in_dim.58
  11.3 0.1 copy.21
  11.4 0.4 copy_multiply_fusion
  11.8 0.0 copy-start.5
  11.8 0.0 copy-start.6
  11.8 0.1 fusion
  11.9 0.2 select_n.68
  12.1 0.7 collective-permute-start
  12.7 1.9 collective-permute-start.1
  14.7 0.0 collective-permute-done.2
  14.7 2.4 slice_select_fusion
  17.1 4.0 %collective-permute-done.1 = f32[192,128]{1,0:T(8,128)S(1)} collective-permute-done((f32[192,128]{1,0:T(8,128)S(1)}, f32[192,128]{1,0:T(8,128)S(1)}, u32[]{:S(2)}, u32[]{:S(2)}) %collective-permute-start.1) | collective-permute-done | bytes 98336 | tf_op jit(solution)/shard_map/ppermute | solution.py:22
  21.2 1.9 collective-permute-start.3
  23.1 0.1 fusion.1
  23.2 2.7 %collective-permute-start.4 = (s32[3,12]{1,0:T(4,128)S(1)}, s32[3,12]{1,0:T(4,128)S(1)}, u32[]{:S(2)}, u32[]{:S(2)}) collective-permute-start(s32[3,12]{1,0:T(4,128)S(1)} %fusion.1), channel_id=1, source_target_pairs={{0,1},{1,0},{2,3},{3,2},{4,5},{5,4},{6,7},{7,6},{8,9},{9,8},{10,11... | collective-permute-start | bytes 440 | tf_op jit(solution)/shard_map/ppermute | solution.py:22
  25.9 0.1 broadcast_in_dim.60
  26.0 0.1 copy.23
  26.1 0.3 broadcast_bitcast_fusion
  26.3 0.2 reshape.101.scale_ref
  26.5 1.0 broadcast_select_fusion
  27.5 3.9 %all-to-all-start = ((f32[8,192,128]{2,1,0:T(8,128)}), f32[8,192,128]{2,1,0:T(8,128)S(1)}, u32[]{:S(2)}, u32[]{:S(2)}) async-start(f32[8,192,128]{2,1,0:T(8,128)} %broadcast_select_fusion), calls=%async_computation | async-start | bytes 1572864 | tf_op jit(solution)/shard_map/all_to_all | solution.py:235
  31.4 0.1 broadcast_select_fusion.1
  31.5 0.0 copy-start.2
  31.5 1.7 copy-done.2
  33.2 2.6 shard_map.64.tiles_ref
  35.8 2.2 collective-permute-start.5
  38.0 14.2 %collective-permute-done.5 = f32[200,128]{1,0:T(8,128)S(1)} collective-permute-done((f32[200,128]{1,0:T(8,128)S(1)}, f32[200,128]{1,0:T(8,128)S(1)}, u32[]{:S(2)}, u32[]{:S(2)}) %collective-permute-start.5) | collective-permute-done | bytes 102432 | tf_op jit(solution)/shard_map/ppermute | solution.py:22
  52.2 3.5 %collective-permute-start.6 = (f32[2304,128]{1,0:T(8,128)}, f32[2304,128]{1,0:T(8,128)}, u32[]{:S(2)}, u32[]{:S(2)}) collective-permute-start(f32[2304,128]{1,0:T(8,128)} %collective-permute-done.3.mine_ref), channel_id=1, source_target_pairs={{0,1},{1,0},{2,3},{3,2},{4,5},{5,4},{6,7},{7,6},{8,9},{9,8},{10,11... | collective-permute-start | bytes 3538952 | tf_op jit(solution)/shard_map/ppermute | solution.py:22
  55.8 1.7 shard_map.66
  57.5 1.0 collective-permute-done.6.other_ref
  58.5 2.6 shard_map.65.tiles_ref
  61.1 1.5 shard_map.67
  62.6 22.3 %all_to_all.55 = f32[32,1,1536]{2,1,0:T(1,128)S(1)} all-to-all(f32[32,1,1536]{2,1,0:T(1,128)S(1)} %bitcast.33), channel_id=1, replica_groups={{0,2,4,6,64,66,68,70,128,130,132,134,192,194,196,198,256,258,260,262,32..., dimensions={0} | all-to-all | bytes 393216 | tf_op jit(solution)/shard_map/all_to_all | solution.py:252
  85.0 14.8 %all_to_all.56 = f32[32,1,1536]{2,1,0:T(1,128)S(1)} all-to-all(f32[32,1,1536]{2,1,0:T(1,128)S(1)} %bitcast.40), channel_id=1, replica_groups={{0,2,4,6,64,66,68,70,128,130,132,134,192,194,196,198,256,258,260,262,32..., dimensions={0} | all-to-all | bytes 393216 | tf_op jit(solution)/shard_map/all_to_all | solution.py:252
  99.8 0.1 shard_map.69
  99.9 24.4 %all_to_all.57 = f32[8,192,128]{2,1,0:T(8,128)S(1)} all-to-all(f32[8,192,128]{2,1,0:T(8,128)S(1)} %get-tuple-element.38), channel_id=1, replica_groups={{0,8,16,24,32,40,48,56},{64,72,80,88,96,104,112,120},{128,136,144,152,1..., dimensions={0} | all-to-all | bytes 1572864 | tf_op jit(solution)/shard_map/all_to_all | solution.py:235
  124.3 1.7 shard_map.70
  126.0 1.5 shard_map.71
  127.5 15.2 %all_to_all.58 = f32[32,1,1536]{2,1,0:T(1,128)S(1)} all-to-all(f32[32,1,1536]{2,1,0:T(1,128)S(1)} %bitcast.34), channel_id=1, replica_groups={{0,2,4,6,64,66,68,70,128,130,132,134,192,194,196,198,256,258,260,262,32..., dimensions={0} | all-to-all | bytes 393216 | tf_op jit(solution)/shard_map/all_to_all | solution.py:252
  142.7 13.2 %all_to_all.59 = f32[32,1,1536]{2,1,0:T(1,128)S(1)} all-to-all(f32[32,1,1536]{2,1,0:T(1,128)S(1)} %bitcast.42), channel_id=1, replica_groups={{0,2,4,6,64,66,68,70,128,130,132,134,192,194,196,198,256,258,260,262,32..., dimensions={0} | all-to-all | bytes 393216 | tf_op jit(solution)/shard_map/all_to_all | solution.py:252
  156.0 0.1 shard_map.73
  156.0 20.8 %all_to_all.60 = f32[8,192,128]{2,1,0:T(8,128)S(1)} all-to-all(f32[8,192,128]{2,1,0:T(8,128)S(1)} %get-tuple-element.42), channel_id=1, replica_groups={{0,8,16,24,32,40,48,56},{64,72,80,88,96,104,112,120},{128,136,144,152,1..., dimensions={0} | all-to-all | bytes 1572864 | tf_op jit(solution)/shard_map/all_to_all | solution.py:235
  176.8 1.7 shard_map.74
  178.5 1.5 shard_map.75
  180.0 13.5 %all_to_all.61 = f32[32,1,1536]{2,1,0:T(1,128)S(1)} all-to-all(f32[32,1,1536]{2,1,0:T(1,128)S(1)} %bitcast.35), channel_id=1, replica_groups={{0,2,4,6,64,66,68,70,128,130,132,134,192,194,196,198,256,258,260,262,32..., dimensions={0} | all-to-all | bytes 393216 | tf_op jit(solution)/shard_map/all_to_all | solution.py:252
  193.5 13.1 %all_to_all.62 = f32[32,1,1536]{2,1,0:T(1,128)S(1)} all-to-all(f32[32,1,1536]{2,1,0:T(1,128)S(1)} %bitcast.44), channel_id=1, replica_groups={{0,2,4,6,64,66,68,70,128,130,132,134,192,194,196,198,256,258,260,262,32..., dimensions={0} | all-to-all | bytes 393216 | tf_op jit(solution)/shard_map/all_to_all | solution.py:252
  206.7 0.1 shard_map.77
  206.7 18.5 %all_to_all.63 = f32[8,192,128]{2,1,0:T(8,128)S(1)} all-to-all(f32[8,192,128]{2,1,0:T(8,128)S(1)} %get-tuple-element.46), channel_id=1, replica_groups={{0,8,16,24,32,40,48,56},{64,72,80,88,96,104,112,120},{128,136,144,152,1..., dimensions={0} | all-to-all | bytes 1572864 | tf_op jit(solution)/shard_map/all_to_all | solution.py:235
  225.3 1.7 shard_map.78
  227.0 3.3 %collective-permute-start.8 = (f32[192,128]{1,0:T(8,128)S(1)}, f32[192,128]{1,0:T(8,128)S(1)}, u32[]{:S(2)}, u32[]{:S(2)}) collective-permute-start(f32[192,128]{1,0:T(8,128)S(1)} %get-tuple-element.48), channel_id=1, source_target_pairs={{0,64},{1,65},{2,66},{3,67},{4,68},{5,69},{6,70},{7,71},{8,72},{9,... | collective-permute-start | bytes 294920 | tf_op jit(solution)/shard_map/ppermute | solution.py:22
  230.4 1.4 shard_map.79
  231.8 2.7 %collective-permute-done.8 = f32[192,128]{1,0:T(8,128)S(1)} collective-permute-done((f32[192,128]{1,0:T(8,128)S(1)}, f32[192,128]{1,0:T(8,128)S(1)}, u32[]{:S(2)}, u32[]{:S(2)}) %collective-permute-start.8) | collective-permute-done | bytes 98336 | tf_op jit(solution)/shard_map/ppermute | solution.py:22
  234.5 0.8 broadcast_in_dim.64
  235.3 3.5 %all-to-all-start.10 = ((f32[4,192,128]{2,1,0:T(8,128)}), f32[4,192,128]{2,1,0:T(8,128)S(1)}, u32[]{:S(2)}, u32[]{:S(2)}) async-start(f32[4,192,128]{2,1,0:T(8,128)} %broadcast_in_dim.64), calls=%async_computation.10 | async-start | bytes 786432 | tf_op jit(solution)/shard_map/all_to_all | solution.py:242
  238.8 0.7 collective-permute-start.7
  239.5 14.8 %collective-permute-start.9 = (f32[576,128]{1,0:T(8,128)S(1)}, f32[576,128]{1,0:T(8,128)S(1)}, u32[]{:S(2)}, u32[]{:S(2)}) collective-permute-start(f32[576,128]{1,0:T(8,128)S(1)} %collective-permute-done.7.mine_ref), channel_id=1, source_target_pairs={{0,1},{1,0},{2,3},{3,2},{4,5},{5,4},{6,7},{7,6},{8,9},{9,8},{10,11... | collective-permute-start | bytes 884744 | tf_op jit(solution)/shard_map/ppermute | solution.py:22
  254.4 9.6 %collective-permute-start.10 = (f32[192,128]{1,0:T(8,128)S(1)}, f32[192,128]{1,0:T(8,128)S(1)}, u32[]{:S(2)}, u32[]{:S(2)}) collective-permute-start(f32[192,128]{1,0:T(8,128)S(1)} %reduce_sum.9.mine_last_ref), channel_id=1, source_target_pairs={{0,1},{1,0},{2,3},{3,2},{4,5},{5,4},{6,7},{7,6},{8,9},{9,8},{10,11... | collective-permute-start | bytes 294920 | tf_op jit(solution)/shard_map/ppermute | solution.py:22
  264.0 0.9 collective-permute-done.10.other_last_ref
  264.9 0.1 broadcast_in_dim.57.root_ref
  265.1 1.2 shard_map.80
  (31 shorter events, 0.2 us)
Async XLA Ops:
  0.0 9.8 %copy-start = (f32[384,128]{1,0:T(8,128)S(1)}, f32[384,128]{1,0:T(8,128)}, u32[]{:S(2)}) copy-start(f32[384,128]{1,0:T(8,128)} %param.6) | copy-start | bytes 589828
  0.0 14.7 %copy-start.1 = (f32[3,12,128,128]{3,2,1,0:T(8,128)S(1)}, f32[3,12,128,128]{3,2,1,0:T(8,128)}, u32[]{:S(2)}) copy-start(f32[3,12,128,128]{3,2,1,0:T(8,128)} %param.7) | copy-start | bytes 7077892
  0.0 11.2 %copy-start.7 = (s32[384]{0:T(512)S(1)}, s32[384]{0:T(512)}, u32[]{:S(2)}) copy-start(s32[384]{0:T(512)} %param.10) | copy-start | bytes 4612
  0.0 14.7 %collective-permute-start.2 = (f32[3,12,128,128]{3,2,1,0:T(8,128)}, f32[3,12,128,128]{3,2,1,0:T(8,128)}, u32[]{:S(2)}, u32[]{:S(2)}) collective-permute-start(f32[3,12,128,128]{3,2,1,0:T(8,128)} %param.7), channel_id=1, source_target_pairs={{0,1},{1,0},{2,3},{3,2},{4,5},{5,4},{6,7},{7,6},{8,9},{9,8},{10,11... | collective-permute-start | bytes 7077896 | tf_op jit(solution)/shard_map/ppermute | solution.py:22
  10.9 6.2 %copy-start.3 = (f32[384,128]{1,0:T(8,128)}, f32[384,128]{1,0:T(8,128)S(1)}, u32[]{:S(2)}) copy-start(f32[384,128]{1,0:T(8,128)S(1)} %gather_fusion) | copy-start | bytes 589828
  11.8 11.3 %copy-start.5 = (s32[3,12]{1,0:T(4,128)S(1)}, s32[3,12]{1,0:T(4,128)}, u32[]{:S(2)}) copy-start(s32[3,12]{1,0:T(4,128)} %param.8) | copy-start | bytes 436
  11.8 11.3 %copy-start.6 = (s32[3,1]{0,1:T(1,128)S(1)}, s32[3,1]{0,1:T(1,128)}, u32[]{:S(2)}) copy-start(s32[3,1]{0,1:T(1,128)} %param.9) | copy-start | bytes 40
  12.1 5.1 %collective-permute-start = (f32[192,128]{1,0:T(8,128)S(1)}, f32[192,128]{1,0:T(8,128)S(1)}, u32[]{:S(2)}, u32[]{:S(2)}) collective-permute-start(f32[192,128]{1,0:T(8,128)S(1)} %select_n.68), channel_id=1, source_target_pairs={{0,0},{1,1},{2,130},{3,131},{4,260},{5,261},{6,390},{7,391},{8,8},... | collective-permute-start | bytes 294920 | tf_op jit(solution)/shard_map/ppermute | solution.py:22
  12.7 8.4 %collective-permute-start.1 = (f32[192,128]{1,0:T(8,128)S(1)}, f32[192,128]{1,0:T(8,128)S(1)}, u32[]{:S(2)}, u32[]{:S(2)}) collective-permute-start(f32[192,128]{1,0:T(8,128)S(1)} %select_n.68), channel_id=1, source_target_pairs={{0,64},{1,65},{2,194},{3,195},{4,324},{5,325},{6,454},{7,455},{8,7... | collective-permute-start | bytes 294920 | tf_op jit(solution)/shard_map/ppermute | solution.py:22
  21.2 31.1 %collective-permute-start.3 = (f32[2304,128]{1,0:T(8,128)}, f32[2304,128]{1,0:T(8,128)}, u32[]{:S(2)}, u32[]{:S(2)}) collective-permute-start(f32[2304,128]{1,0:T(8,128)} %bitcast.4), channel_id=1, source_target_pairs={{0,448},{1,449},{2,450},{3,451},{4,452},{5,453},{6,454},{7,455},{8... | collective-permute-start | bytes 3538952 | tf_op jit(solution)/shard_map/ppermute | solution.py:22
  23.2 8.3 %collective-permute-start.4 = (s32[3,12]{1,0:T(4,128)S(1)}, s32[3,12]{1,0:T(4,128)S(1)}, u32[]{:S(2)}, u32[]{:S(2)}) collective-permute-start(s32[3,12]{1,0:T(4,128)S(1)} %fusion.1), channel_id=1, source_target_pairs={{0,1},{1,0},{2,3},{3,2},{4,5},{5,4},{6,7},{7,6},{8,9},{9,8},{10,11... | collective-permute-start | bytes 440 | tf_op jit(solution)/shard_map/ppermute | solution.py:22
  27.5 28.3 %all-to-all-start = ((f32[8,192,128]{2,1,0:T(8,128)}), f32[8,192,128]{2,1,0:T(8,128)S(1)}, u32[]{:S(2)}, u32[]{:S(2)}) async-start(f32[8,192,128]{2,1,0:T(8,128)} %broadcast_select_fusion), calls=%async_computation | async-start | bytes 1572864 | tf_op jit(solution)/shard_map/all_to_all | solution.py:235
  31.5 1.7 copy-start.2
  35.8 16.4 %collective-permute-start.5 = (f32[200,128]{1,0:T(8,128)S(1)}, f32[200,128]{1,0:T(8,128)S(1)}, u32[]{:S(2)}, u32[]{:S(2)}) collective-permute-start(f32[200,128]{1,0:T(8,128)S(1)} %select_maximum_fusion), channel_id=1, source_target_pairs={{0,448},{1,449},{2,450},{3,451},{4,452},{5,453},{6,454},{7,455},{8... | collective-permute-start | bytes 307208 | tf_op jit(solution)/shard_map/ppermute | solution.py:22
  52.2 6.3 %collective-permute-start.6 = (f32[2304,128]{1,0:T(8,128)}, f32[2304,128]{1,0:T(8,128)}, u32[]{:S(2)}, u32[]{:S(2)}) collective-permute-start(f32[2304,128]{1,0:T(8,128)} %collective-permute-done.3.mine_ref), channel_id=1, source_target_pairs={{0,1},{1,0},{2,3},{3,2},{4,5},{5,4},{6,7},{7,6},{8,9},{9,8},{10,11... | collective-permute-start | bytes 3538952 | tf_op jit(solution)/shard_map/ppermute | solution.py:22
  227.0 7.5 %collective-permute-start.8 = (f32[192,128]{1,0:T(8,128)S(1)}, f32[192,128]{1,0:T(8,128)S(1)}, u32[]{:S(2)}, u32[]{:S(2)}) collective-permute-start(f32[192,128]{1,0:T(8,128)S(1)} %get-tuple-element.48), channel_id=1, source_target_pairs={{0,64},{1,65},{2,66},{3,67},{4,68},{5,69},{6,70},{7,71},{8,72},{9,... | collective-permute-start | bytes 294920 | tf_op jit(solution)/shard_map/ppermute | solution.py:22
  230.4 34.7 %copy-start.4 = (f32[384,128]{1,0:T(8,128)S(1)}, f32[384,128]{1,0:T(8,128)}, u32[]{:S(2)}) copy-start(f32[384,128]{1,0:T(8,128)} %copy-done.3) | copy-start | bytes 589828
  235.3 19.0 %all-to-all-start.10 = ((f32[4,192,128]{2,1,0:T(8,128)}), f32[4,192,128]{2,1,0:T(8,128)S(1)}, u32[]{:S(2)}, u32[]{:S(2)}) async-start(f32[4,192,128]{2,1,0:T(8,128)} %broadcast_in_dim.64), calls=%async_computation.10 | async-start | bytes 786432 | tf_op jit(solution)/shard_map/all_to_all | solution.py:242
  238.8 0.7 collective-permute-start.7
  239.5 24.5 %collective-permute-start.9 = (f32[576,128]{1,0:T(8,128)S(1)}, f32[576,128]{1,0:T(8,128)S(1)}, u32[]{:S(2)}, u32[]{:S(2)}) collective-permute-start(f32[576,128]{1,0:T(8,128)S(1)} %collective-permute-done.7.mine_ref), channel_id=1, source_target_pairs={{0,1},{1,0},{2,3},{3,2},{4,5},{5,4},{6,7},{7,6},{8,9},{9,8},{10,11... | collective-permute-start | bytes 884744 | tf_op jit(solution)/shard_map/ppermute | solution.py:22
  254.4 10.6 %collective-permute-start.10 = (f32[192,128]{1,0:T(8,128)S(1)}, f32[192,128]{1,0:T(8,128)S(1)}, u32[]{:S(2)}, u32[]{:S(2)}) collective-permute-start(f32[192,128]{1,0:T(8,128)S(1)} %reduce_sum.9.mine_last_ref), channel_id=1, source_target_pairs={{0,1},{1,0},{2,3},{3,2},{4,5},{5,4},{6,7},{7,6},{8,9},{9,8},{10,11... | collective-permute-start | bytes 294920 | tf_op jit(solution)/shard_map/ppermute | solution.py:22

commit v5 on v4

--- a/solution.py
+++ b/solution.py
@@ -26,66 +26,56 @@
     return send(block, lambda p, w: (p, w ^ 1))
 
 
-def pack(field, half):
-    blocks = field.shape[0] // 128
-    part = field.reshape(blocks, 2, HALF, 2, HALF)[:, :, :, half]
-    return part.transpose(0, 2, 1, 3).reshape(blocks * HALF, 128)
-
-
-def split_tiles(first_slots, second_slots, core_ref, mine_ref, other_ref, out_ref):
-    for s, (at_first, at_second) in enumerate(zip(first_slots, second_slots)):
-        def read(at):
-            held, place = at
-            return (mine_ref if held == "mine" else other_ref)[place * 128:(place + 1) * 128]
-        tile = jnp.where(core_ref[0] == 0, read(at_first), read(at_second))
-        high = tile.astype(jnp.bfloat16)
-        low = (tile - high.astype(jnp.float32)).astype(jnp.bfloat16)
-        out_ref[0, 0:128, s * 128:(s + 1) * 128] = high
-        out_ref[0, 128:256, s * 128:(s + 1) * 128] = low
+def turned(field):
+    return field.reshape(-1, 128, 128).transpose(0, 2, 1)
+
+
+def split_tiles(rows, first_slots, second_slots, core_ref, mine_ref, other_ref, out_ref):
+    def read(i, at, slots):
+        held, place = at
+        ref = mine_ref if held == "mine" else other_ref
+        per_row = 1 + max(p for _, p in slots)
+        first = (i * per_row + place) * 128
+        return ref[first:first + 128]
+
+    for i in range(rows):
+        for s, (at_first, at_second) in enumerate(zip(first_slots, second_slots)):
+            tile = jnp.where(core_ref[0] == 0, read(i, at_first, first_slots), read(i, at_second, second_slots)).T
+            high = tile.astype(jnp.bfloat16)
+            low = (tile - high.astype(jnp.float32)).astype(jnp.bfloat16)
+            out_ref[i, s * 128:(s + 1) * 128, 0:128] = high
+            out_ref[i, s * 128:(s + 1) * 128, 128:256] = low
 
 
 def tile_parts(core, mine, other, rows, first_slots, second_slots):
-    slots = len(first_slots)
-    held = 1 + max(place for _, place in first_slots)
-    block = pl.BlockSpec((held * 128, 128), lambda i, core: (i, 0))
-    return pl.pallas_call(
-        functools.partial(split_tiles, first_slots, second_slots),
-        grid_spec=pltpu.PrefetchScalarGridSpec(
-            num_scalar_prefetch=1,
-            grid=(rows,),
-            in_specs=[block, block],
-            out_specs=pl.BlockSpec((1, 256, slots * 128), lambda i, core: (i, 0, 0)),
-        ),
-        out_shape=jax.ShapeDtypeStruct((rows, 256, slots * 128), jnp.bfloat16),
+    vmem = pl.BlockSpec(memory_space=pltpu.VMEM)
+    return pl.pallas_call(
+        functools.partial(split_tiles, rows, first_slots, second_slots),
+        in_specs=[pl.BlockSpec(memory_space=pltpu.SMEM), vmem, vmem],
+        out_specs=vmem,
+        out_shape=jax.ShapeDtypeStruct((rows, len(first_slots) * 128, 256), jnp.bfloat16),
         compiler_params=pltpu.CompilerParams(vmem_limit_bytes=VMEM_BYTES),
     )(core, mine, other)
 
 
 def multiply(index_ref, tiles_ref, scale_ref, source_ref, gathered_ref, out_ref):
     rows, slots = index_ref.shape
-    left = lax.broadcasted_iota(jnp.int32, (HALF, 128), 1) < HALF
     for i in range(rows):
         for s in range(slots):
-            gathered_ref[i, s * 128:(s + 1) * 128] = source_ref[index_ref[i, s]]
+            gathered_ref[i, :, s * 128:(s + 1) * 128] = source_ref[index_ref[i, s]]
     for i in range(rows):
-        both = jnp.dot(tiles_ref[i], gathered_ref[i], preferred_element_type=jnp.float32)
-        total = both[0:128] + both[128:256]
-        total = total + pltpu.roll(total, HALF, 1)
-        at = slice(i * HALF, (i + 1) * HALF)
-        out_ref[at] = jnp.where(left, total[0:HALF], total[HALF:128]) * scale_ref[at]
+        both = jnp.dot(gathered_ref[i], tiles_ref[i], preferred_element_type=jnp.float32)
+        total = both[0:HALF] + both[HALF:128]
+        out_ref[i * HALF:(i + 1) * HALF] = (total[:, 0:128] + total[:, 128:256]) * scale_ref[i:i + 1]
 
 
 def near_kernel(index_ref, tiles_ref, scale_ref, units_ref, near_ref, source_ref, gathered_ref):
-    left = lax.broadcasted_iota(jnp.int32, (HALF, 128), 1) < HALF
     count = units_ref.shape[0] // HALF
     for k in range(count):
         part = units_ref[k * HALF:(k + 1) * HALF]
-        high = part.astype(jnp.bfloat16).astype(jnp.float32)
-        low = part - high
-        top = jnp.where(left, high, pltpu.roll(low, HALF, 1))
-        bottom = jnp.where(left, pltpu.roll(high, HALF, 1), low)
-        source_ref[k, 0:HALF] = top.astype(jnp.bfloat16)
-        source_ref[k, HALF:128] = bottom.astype(jnp.bfloat16)
+        high = part.astype(jnp.bfloat16)
+        source_ref[k, 0:HALF] = high
+        source_ref[k, HALF:128] = (part - high.astype(jnp.float32)).astype(jnp.bfloat16)
     source_ref[count] = jnp.zeros((128, 128), jnp.bfloat16)
     multiply(index_ref, tiles_ref, scale_ref, source_ref, gathered_ref, near_ref)
 
@@ -111,7 +101,7 @@
         in_specs=[smem] + [vmem] * (inputs - 1),
         out_specs=jax.tree.map(lambda _: vmem, out_shape),
         out_shape=out_shape,
-        scratch_shapes=[pltpu.VMEM((rows, slots * 128, 128), jnp.bfloat16), *more_scratch],
+        scratch_shapes=[pltpu.VMEM((rows, 128, slots * 128), jnp.bfloat16), *more_scratch],
         compiler_params=pltpu.CompilerParams(vmem_limit_bytes=VMEM_BYTES),
         cost_estimate=pl.CostEstimate(flops=2 * rows * slots * 256 * 128 * 128, bytes_accessed=4 * 2**20, transcendentals=0),
     )
@@ -200,7 +190,6 @@
 
 def finish_kernel(core_ref, ordered_ref, root_ref, mine_ref, mine_last_ref, other_ref, other_last_ref, out_ref):
     out_ref[0] = ordered_ref[...]
-    left = lax.broadcasted_iota(jnp.int32, (HALF, 128), 1) < HALF
     first_core = core_ref[0] == 0
     blocks = ordered_ref.shape[0] // 128
     size = blocks * HALF
@@ -209,13 +198,8 @@
             at = b * HALF if hop == HOPS - 1 else hop * size + b * HALF
             mine = (mine_last_ref if hop == HOPS - 1 else mine_ref)[at:at + HALF]
             other = (other_last_ref if hop == HOPS - 1 else other_ref)[at:at + HALF]
-            a = jnp.where(first_core, mine, other)
-            c = jnp.where(first_core, other, mine)
-            first = b * 128
-            top = jnp.where(left, a, pltpu.roll(c, HALF, 1))
-            bottom = jnp.where(left, pltpu.roll(a, HALF, 1), c)
-            out_ref[hop + 1, first:first + HALF] = top * root_ref[first:first + HALF]
-            out_ref[hop + 1, first + HALF:first + 128] = bottom * root_ref[first + HALF:first + 128]
+            columns = jnp.concatenate([jnp.where(first_core, mine, other), jnp.where(first_core, other, mine)])
+            out_ref[hop + 1, b * 128:(b + 1) * 128] = (columns * root_ref[b:b + 1]).T
 
 
 def finish(core, ordered, root, fields):
@@ -271,13 +255,12 @@
     leaving = jnp.where(first_core, swapped[:, :mid], tile_values[:, mid:]).reshape(-1, 128)
 
     ordered = jnp.take(features, curve_order - rank_blk * features.shape[0], axis=0, mode="clip")
-    count = degrees.astype(jnp.float32)
-    inv_root = lax.rsqrt(count)[:, None]
-    wide = jnp.broadcast_to(inv_root, features.shape)
-    root = jnp.broadcast_to(count[:, None], features.shape) * wide
-    scale = pack(wide * wide, 0)
-    sent = wide * ordered
-    start = jnp.where(first_core, pack(sent, 0), pack(sent, 1))
+    count = degrees.astype(jnp.float32).reshape(rows, 128)
+    inv_root = lax.rsqrt(count)
+    root = count * inv_root
+    scale = inv_root * inv_root
+    sent = turned(ordered) * inv_root[:, None]
+    start = jnp.where(first_core, sent[:, :HALF], sent[:, HALF:]).reshape(-1, 128)
 
     def aligned(p, w):
         return p + 2 * span * (w // 2), w
@@ -291,8 +274,7 @@
     members = lines * pairs
     own, behind = send(start, aligned), send(start, behind_aligned)
     leaving_index = jnp.where(first_core, swapped_index, index).astype(jnp.float32)
-    index_rows = jnp.pad(leaving_index, ((0, 8 - rows), (0, 128 - slots)))
-    far_rows = jnp.concatenate([scale, index_rows])
+    far_rows = jnp.concatenate([scale, jnp.pad(leaving_index, ((0, 0), (0, 128 - slots)))])
     own, behind, leaving = lax.optimization_barrier((own, behind, leaving))
     came = send(leaving, lambda p, w: (p - span, w))
     every = [("mine", s) for s in range(slots)], [("other", s) for s in range(slots)]
@@ -307,8 +289,8 @@
         units = ring_exchange(chunks).reshape(-1, 128)
         if hop == 0:
             came, near_tiles, far_parts = lax.optimization_barrier((came, near_tiles, far_parts))
-            far_scale = far_parts[:rows * HALF]
-            far_index = far_parts[rows * HALF:][:rows, :slots].astype(jnp.int32)
+            far_scale = far_parts[:rows]
+            far_index = far_parts[rows:, :slots].astype(jnp.int32)
         near, source = near_product(near_index, near_tiles, scale, units)
         if hop == 0:
             rest = swap_cores(came)

time: 267 us -> 263 us (0.985)
  Pallas kernels: 19.6 us -> 16.1 us
  transfers between devices with their start and end apart: 13 -> 13, of which waited for: 5 -> 6; matrix products, arithmetic and copies ran while one was open for 3% -> 3% of each run, Pallas kernels for 2% -> 2%
where the time goes in v5:
time: 263 us; the launch traced here: 262 us
  blocking collectives  156 us (59%)
  starting transfers between devices  57.4 us (22%)
  waiting for transfers between devices  22.7 us (9%)
  Pallas kernels  16.1 us (6%)
  other arithmetic  5.67 us (2%)
  local copies, waits for them, and re-layouts  3.71 us (1%)
    all_to_all x6, blocking collectives, plane_exchange(): lax.all_to_all(pieces, ('blk', 'rep'), 0, 0, axis_index_groups=planes)  93 us
    all_to_all x3, blocking collectives, ring_exchange(): return lax.all_to_all(chunks, 'blk', 0, 0, axis_index_groups=rings)  62.9 us
    ppermute x11, starting transfers between devices, send(): return lax.ppermute(block, ('blk', 'rep'), route)  50.1 us
    ppermute x11, waiting for transfers between devices, send(): return lax.ppermute(block, ('blk', 'rep'), route)  21.9 us
  transfers between devices with their start and end apart: 13, of which 6 were waited for; matrix products, arithmetic and copies ran while one was open for 3% of the time, Pallas kernels for 2%

profile of v5, /device:TPU:1, one launch (start us, length us, event | category | flops | bytes accessed | tf_op | source)
XLA Modules:
  0.0 261.8 jit_solution(4821043106119877884)
XLA Ops:
  0.0 0.0 copy-start
  0.0 9.0 %collective-permute-start.2 = (f32[3,12,128,128]{3,2,1,0:T(8,128)}, f32[3,12,128,128]{3,2,1,0:T(8,128)}, u32[]{:S(2)}, u32[]{:S(2)}) collective-permute-start(f32[3,12,128,128]{3,2,1,0:T(8,128)} %param.7), channel_id=1, source_target_pairs={{0,1},{1,0},{2,3},{3,2},{4,5},{5,4},{6,7},{7,6},{8,9},{9,8},{10,11... | collective-permute-start | bytes 7077896 | tf_op jit(solution)/shard_map/ppermute | solution.py:22
  9.1 0.7 broadcast_subtract_fusion
  9.8 1.1 gather_fusion
  10.9 0.0 copy-start.4
  10.9 0.0 copy-start.5
  10.9 0.1 copy.15
  11.1 1.3 fusion.1
  12.4 0.7 collective-permute-start
  13.1 1.9 collective-permute-start.1
  15.0 0.0 collective-permute-done.2
  15.0 2.4 slice_select_fusion
  17.4 0.0 collective-permute-done
  17.4 4.0 %collective-permute-done.1 = f32[192,128]{1,0:T(8,128)S(1)} collective-permute-done((f32[192,128]{1,0:T(8,128)S(1)}, f32[192,128]{1,0:T(8,128)S(1)}, u32[]{:S(2)}, u32[]{:S(2)}) %collective-permute-start.1) | collective-permute-done | bytes 98336 | tf_op jit(solution)/shard_map/ppermute | solution.py:22
  21.5 1.9 collective-permute-start.3
  23.4 0.0 copy-done.4
  23.4 0.0 copy-done.5
  23.4 0.1 fusion
  23.5 2.7 %collective-permute-start.4 = (s32[3,12]{1,0:T(4,128)S(1)}, s32[3,12]{1,0:T(4,128)S(1)}, u32[]{:S(2)}, u32[]{:S(2)}) collective-permute-start(s32[3,12]{1,0:T(4,128)S(1)} %fusion), channel_id=1, source_target_pairs={{0,1},{1,0},{2,3},{3,2},{4,5},{5,4},{6,7},{7,6},{8,9},{9,8},{10,11... | collective-permute-start | bytes 440 | tf_op jit(solution)/shard_map/ppermute | solution.py:22
  26.2 1.0 broadcast_select_fusion
  27.2 3.9 %all-to-all-start = ((f32[8,192,128]{2,1,0:T(8,128)}), f32[8,192,128]{2,1,0:T(8,128)S(1)}, u32[]{:S(2)}, u32[]{:S(2)}) async-start(f32[8,192,128]{2,1,0:T(8,128)} %broadcast_select_fusion), calls=%async_computation | async-start | bytes 1572864 | tf_op jit(solution)/shard_map/all_to_all | solution.py:219
  31.1 0.0 collective-permute-done.4
  31.1 0.1 broadcast_select_fusion.1
  31.2 1.7 copy-done.2
  32.9 2.4 shard_map.64.tiles_ref
  35.3 2.2 collective-permute-start.5
  37.5 13.0 %collective-permute-done.5 = f32[6,128]{1,0:T(8,128)S(1)} collective-permute-done((f32[6,128]{1,0:T(8,128)S(1)}, f32[6,128]{1,0:T(8,128)S(1)}, u32[]{:S(2)}, u32[]{:S(2)}) %collective-permute-start.5) | collective-permute-done | bytes 3104 | tf_op jit(solution)/shard_map/ppermute | solution.py:22
  50.5 0.0 collective-permute-done.3.mine_ref
  50.5 3.5 %collective-permute-start.6 = (f32[2304,128]{1,0:T(8,128)}, f32[2304,128]{1,0:T(8,128)}, u32[]{:S(2)}, u32[]{:S(2)}) collective-permute-start(f32[2304,128]{1,0:T(8,128)} %collective-permute-done.3.mine_ref), channel_id=1, source_target_pairs={{0,1},{1,0},{2,3},{3,2},{4,5},{5,4},{6,7},{7,6},{8,9},{9,8},{10,11... | collective-permute-start | bytes 3538952 | tf_op jit(solution)/shard_map/ppermute | solution.py:22
  54.0 0.7 all-to-all-done
  54.7 1.2 shard_map.66
  56.0 0.8 collective-permute-done.6.other_ref
  56.8 2.3 shard_map.65.tiles_ref
  59.1 1.2 shard_map.67
  60.3 23.3 %all_to_all.55 = f32[32,1,1536]{2,1,0:T(1,128)S(1)} all-to-all(f32[32,1,1536]{2,1,0:T(1,128)S(1)} %bitcast.48), channel_id=1, replica_groups={{0,2,4,6,64,66,68,70,128,130,132,134,192,194,196,198,256,258,260,262,32..., dimensions={0} | all-to-all | bytes 393216 | tf_op jit(solution)/shard_map/all_to_all | solution.py:236
  83.6 14.8 %all_to_all.56 = f32[32,1,1536]{2,1,0:T(1,128)S(1)} all-to-all(f32[32,1,1536]{2,1,0:T(1,128)S(1)} %bitcast.43), channel_id=1, replica_groups={{0,2,4,6,64,66,68,70,128,130,132,134,192,194,196,198,256,258,260,262,32..., dimensions={0} | all-to-all | bytes 393216 | tf_op jit(solution)/shard_map/all_to_all | solution.py:236
  98.4 0.1 shard_map.69
  98.5 23.4 %all_to_all.57 = f32[8,192,128]{2,1,0:T(8,128)S(1)} all-to-all(f32[8,192,128]{2,1,0:T(8,128)S(1)} %get-tuple-element.38), channel_id=1, replica_groups={{0,8,16,24,32,40,48,56},{64,72,80,88,96,104,112,120},{128,136,144,152,1..., dimensions={0} | all-to-all | bytes 1572864 | tf_op jit(solution)/shard_map/all_to_all | solution.py:219
  122.0 1.2 shard_map.70
  123.2 1.2 shard_map.71
  124.4 15.2 %all_to_all.58 = f32[32,1,1536]{2,1,0:T(1,128)S(1)} all-to-all(f32[32,1,1536]{2,1,0:T(1,128)S(1)} %bitcast.49), channel_id=1, replica_groups={{0,2,4,6,64,66,68,70,128,130,132,134,192,194,196,198,256,258,260,262,32..., dimensions={0} | all-to-all | bytes 393216 | tf_op jit(solution)/shard_map/all_to_all | solution.py:236
  139.7 13.1 %all_to_all.59 = f32[32,1,1536]{2,1,0:T(1,128)S(1)} all-to-all(f32[32,1,1536]{2,1,0:T(1,128)S(1)} %bitcast.45), channel_id=1, replica_groups={{0,2,4,6,64,66,68,70,128,130,132,134,192,194,196,198,256,258,260,262,32..., dimensions={0} | all-to-all | bytes 393216 | tf_op jit(solution)/shard_map/all_to_all | solution.py:236
  152.8 0.1 shard_map.73
  152.9 20.9 %all_to_all.60 = f32[8,192,128]{2,1,0:T(8,128)S(1)} all-to-all(f32[8,192,128]{2,1,0:T(8,128)S(1)} %get-tuple-element.42), channel_id=1, replica_groups={{0,8,16,24,32,40,48,56},{64,72,80,88,96,104,112,120},{128,136,144,152,1..., dimensions={0} | all-to-all | bytes 1572864 | tf_op jit(solution)/shard_map/all_to_all | solution.py:219
  173.8 1.2 shard_map.74
  175.0 1.2 shard_map.75
  176.2 13.5 %all_to_all.61 = f32[32,1,1536]{2,1,0:T(1,128)S(1)} all-to-all(f32[32,1,1536]{2,1,0:T(1,128)S(1)} %bitcast.50), channel_id=1, replica_groups={{0,2,4,6,64,66,68,70,128,130,132,134,192,194,196,198,256,258,260,262,32..., dimensions={0} | all-to-all | bytes 393216 | tf_op jit(solution)/shard_map/all_to_all | solution.py:236
  189.7 13.1 %all_to_all.62 = f32[32,1,1536]{2,1,0:T(1,128)S(1)} all-to-all(f32[32,1,1536]{2,1,0:T(1,128)S(1)} %bitcast.47), channel_id=1, replica_groups={{0,2,4,6,64,66,68,70,128,130,132,134,192,194,196,198,256,258,260,262,32..., dimensions={0} | all-to-all | bytes 393216 | tf_op jit(solution)/shard_map/all_to_all | solution.py:236
  202.9 0.1 shard_map.77
  202.9 18.5 %all_to_all.63 = f32[8,192,128]{2,1,0:T(8,128)S(1)} all-to-all(f32[8,192,128]{2,1,0:T(8,128)S(1)} %get-tuple-element.46), channel_id=1, replica_groups={{0,8,16,24,32,40,48,56},{64,72,80,88,96,104,112,120},{128,136,144,152,1..., dimensions={0} | all-to-all | bytes 1572864 | tf_op jit(solution)/shard_map/all_to_all | solution.py:219
  221.5 1.2 shard_map.78
  222.7 3.3 %collective-permute-start.8 = (f32[192,128]{1,0:T(8,128)S(1)}, f32[192,128]{1,0:T(8,128)S(1)}, u32[]{:S(2)}, u32[]{:S(2)}) collective-permute-start(f32[192,128]{1,0:T(8,128)S(1)} %get-tuple-element.48), channel_id=1, source_target_pairs={{0,64},{1,65},{2,66},{3,67},{4,68},{5,69},{6,70},{7,71},{8,72},{9,... | collective-permute-start | bytes 294920 | tf_op jit(solution)/shard_map/ppermute | solution.py:22
  226.1 1.2 shard_map.79
  227.3 3.2 %collective-permute-done.8 = f32[192,128]{1,0:T(8,128)S(1)} collective-permute-done((f32[192,128]{1,0:T(8,128)S(1)}, f32[192,128]{1,0:T(8,128)S(1)}, u32[]{:S(2)}, u32[]{:S(2)}) %collective-permute-start.8) | collective-permute-done | bytes 98336 | tf_op jit(solution)/shard_map/ppermute | solution.py:22
  230.5 0.8 broadcast_in_dim.45
  231.3 3.5 %all-to-all-start.10 = ((f32[4,192,128]{2,1,0:T(8,128)}), f32[4,192,128]{2,1,0:T(8,128)S(1)}, u32[]{:S(2)}, u32[]{:S(2)}) async-start(f32[4,192,128]{2,1,0:T(8,128)} %broadcast_in_dim.45), calls=%async_computation.10 | async-start | bytes 786432 | tf_op jit(solution)/shard_map/all_to_all | solution.py:226
  234.8 0.7 collective-permute-start.7
  235.5 0.0 collective-permute-done.7.mine_ref
  235.5 14.4 %collective-permute-start.9 = (f32[576,128]{1,0:T(8,128)S(1)}, f32[576,128]{1,0:T(8,128)S(1)}, u32[]{:S(2)}, u32[]{:S(2)}) collective-permute-start(f32[576,128]{1,0:T(8,128)S(1)} %collective-permute-done.7.mine_ref), channel_id=1, source_target_pairs={{0,1},{1,0},{2,3},{3,2},{4,5},{5,4},{6,7},{7,6},{8,9},{9,8},{10,11... | collective-permute-start | bytes 884744 | tf_op jit(solution)/shard_map/ppermute | solution.py:22
  249.9 0.0 all-to-all-done.10
  250.0 9.6 %collective-permute-start.10 = (f32[192,128]{1,0:T(8,128)S(1)}, f32[192,128]{1,0:T(8,128)S(1)}, u32[]{:S(2)}, u32[]{:S(2)}) collective-permute-start(f32[192,128]{1,0:T(8,128)S(1)} %reduce_sum.9.mine_last_ref), channel_id=1, source_target_pairs={{0,1},{1,0},{2,3},{3,2},{4,5},{5,4},{6,7},{7,6},{8,9},{9,8},{10,11... | collective-permute-start | bytes 294920 | tf_op jit(solution)/shard_map/ppermute | solution.py:22
  259.6 0.0 collective-permute-done.9.other_ref
  259.6 0.9 collective-permute-done.10.other_last_ref
  260.5 1.2 shard_map.80
  (19 shorter events, 0.2 us)
Async XLA Ops:
  0.0 9.8 %copy-start = (f32[384,128]{1,0:T(8,128)S(1)}, f32[384,128]{1,0:T(8,128)}, u32[]{:S(2)}) copy-start(f32[384,128]{1,0:T(8,128)} %param.6) | copy-start | bytes 589828
  0.0 15.0 %copy-start.1 = (f32[3,12,128,128]{3,2,1,0:T(8,128)S(1)}, f32[3,12,128,128]{3,2,1,0:T(8,128)}, u32[]{:S(2)}) copy-start(f32[3,12,128,128]{3,2,1,0:T(8,128)} %param.7) | copy-start | bytes 7077892
  0.0 15.0 %collective-permute-start.2 = (f32[3,12,128,128]{3,2,1,0:T(8,128)}, f32[3,12,128,128]{3,2,1,0:T(8,128)}, u32[]{:S(2)}, u32[]{:S(2)}) collective-permute-start(f32[3,12,128,128]{3,2,1,0:T(8,128)} %param.7), channel_id=1, source_target_pairs={{0,1},{1,0},{2,3},{3,2},{4,5},{5,4},{6,7},{7,6},{8,9},{9,8},{10,11... | collective-permute-start | bytes 7077896 | tf_op jit(solution)/shard_map/ppermute | solution.py:22
  10.9 12.5 %copy-start.4 = (s32[3,12]{1,0:T(4,128)S(1)}, s32[3,12]{1,0:T(4,128)}, u32[]{:S(2)}) copy-start(s32[3,12]{1,0:T(4,128)} %param.8) | copy-start | bytes 436
  10.9 12.5 %copy-start.5 = (s32[3,1]{0,1:T(1,128)S(1)}, s32[3,1]{0,1:T(1,128)}, u32[]{:S(2)}) copy-start(s32[3,1]{0,1:T(1,128)} %param.9) | copy-start | bytes 40
  12.4 5.1 %collective-permute-start = (f32[192,128]{1,0:T(8,128)S(1)}, f32[192,128]{1,0:T(8,128)S(1)}, u32[]{:S(2)}, u32[]{:S(2)}) collective-permute-start(f32[192,128]{1,0:T(8,128)S(1)} %bitcast.51), channel_id=1, source_target_pairs={{0,0},{1,1},{2,130},{3,131},{4,260},{5,261},{6,390},{7,391},{8,8},... | collective-permute-start | bytes 294920 | tf_op jit(solution)/shard_map/ppermute | solution.py:22
  13.1 8.4 %collective-permute-start.1 = (f32[192,128]{1,0:T(8,128)S(1)}, f32[192,128]{1,0:T(8,128)S(1)}, u32[]{:S(2)}, u32[]{:S(2)}) collective-permute-start(f32[192,128]{1,0:T(8,128)S(1)} %bitcast.52), channel_id=1, source_target_pairs={{0,64},{1,65},{2,194},{3,195},{4,324},{5,325},{6,454},{7,455},{8,7... | collective-permute-start | bytes 294920 | tf_op jit(solution)/shard_map/ppermute | solution.py:22
  21.5 29.0 %collective-permute-start.3 = (f32[2304,128]{1,0:T(8,128)}, f32[2304,128]{1,0:T(8,128)}, u32[]{:S(2)}, u32[]{:S(2)}) collective-permute-start(f32[2304,128]{1,0:T(8,128)} %bitcast.6), channel_id=1, source_target_pairs={{0,448},{1,449},{2,450},{3,451},{4,452},{5,453},{6,454},{7,455},{8... | collective-permute-start | bytes 3538952 | tf_op jit(solution)/shard_map/ppermute | solution.py:22
  23.5 7.6 %collective-permute-start.4 = (s32[3,12]{1,0:T(4,128)S(1)}, s32[3,12]{1,0:T(4,128)S(1)}, u32[]{:S(2)}, u32[]{:S(2)}) collective-permute-start(s32[3,12]{1,0:T(4,128)S(1)} %fusion), channel_id=1, source_target_pairs={{0,1},{1,0},{2,3},{3,2},{4,5},{5,4},{6,7},{7,6},{8,9},{9,8},{10,11... | collective-permute-start | bytes 440 | tf_op jit(solution)/shard_map/ppermute | solution.py:22
  27.2 27.5 %all-to-all-start = ((f32[8,192,128]{2,1,0:T(8,128)}), f32[8,192,128]{2,1,0:T(8,128)S(1)}, u32[]{:S(2)}, u32[]{:S(2)}) async-start(f32[8,192,128]{2,1,0:T(8,128)} %broadcast_select_fusion), calls=%async_computation | async-start | bytes 1572864 | tf_op jit(solution)/shard_map/all_to_all | solution.py:219
  31.2 1.7 copy-start.2
  35.3 15.2 %collective-permute-start.5 = (f32[6,128]{1,0:T(8,128)S(1)}, f32[6,128]{1,0:T(8,128)S(1)}, u32[]{:S(2)}, u32[]{:S(2)}) collective-permute-start(f32[6,128]{1,0:T(8,128)S(1)} %select_maximum_fusion), channel_id=1, source_target_pairs={{0,448},{1,449},{2,450},{3,451},{4,452},{5,453},{6,454},{7,455},{8... | collective-permute-start | bytes 9224 | tf_op jit(solution)/shard_map/ppermute | solution.py:22
  50.5 6.3 %collective-permute-start.6 = (f32[2304,128]{1,0:T(8,128)}, f32[2304,128]{1,0:T(8,128)}, u32[]{:S(2)}, u32[]{:S(2)}) collective-permute-start(f32[2304,128]{1,0:T(8,128)} %collective-permute-done.3.mine_ref), channel_id=1, source_target_pairs={{0,1},{1,0},{2,3},{3,2},{4,5},{5,4},{6,7},{7,6},{8,9},{9,8},{10,11... | collective-permute-start | bytes 3538952 | tf_op jit(solution)/shard_map/ppermute | solution.py:22
  222.7 7.8 %collective-permute-start.8 = (f32[192,128]{1,0:T(8,128)S(1)}, f32[192,128]{1,0:T(8,128)S(1)}, u32[]{:S(2)}, u32[]{:S(2)}) collective-permute-start(f32[192,128]{1,0:T(8,128)S(1)} %get-tuple-element.48), channel_id=1, source_target_pairs={{0,64},{1,65},{2,66},{3,67},{4,68},{5,69},{6,70},{7,71},{8,72},{9,... | collective-permute-start | bytes 294920 | tf_op jit(solution)/shard_map/ppermute | solution.py:22
  226.1 34.5 %copy-start.3 = (f32[3,128]{1,0:T(4,128)S(1)}, f32[3,128]{1,0:T(4,128)}, u32[]{:S(2)}) copy-start(f32[3,128]{1,0:T(4,128)} %get-tuple-element.52.root_ref) | copy-start | bytes 4612
  231.3 18.7 %all-to-all-start.10 = ((f32[4,192,128]{2,1,0:T(8,128)}), f32[4,192,128]{2,1,0:T(8,128)S(1)}, u32[]{:S(2)}, u32[]{:S(2)}) async-start(f32[4,192,128]{2,1,0:T(8,128)} %broadcast_in_dim.45), calls=%async_computation.10 | async-start | bytes 786432 | tf_op jit(solution)/shard_map/all_to_all | solution.py:226
  234.8 0.7 collective-permute-start.7
  235.5 24.1 %collective-permute-start.9 = (f32[576,128]{1,0:T(8,128)S(1)}, f32[576,128]{1,0:T(8,128)S(1)}, u32[]{:S(2)}, u32[]{:S(2)}) collective-permute-start(f32[576,128]{1,0:T(8,128)S(1)} %collective-permute-done.7.mine_ref), channel_id=1, source_target_pairs={{0,1},{1,0},{2,3},{3,2},{4,5},{5,4},{6,7},{7,6},{8,9},{9,8},{10,11... | collective-permute-start | bytes 884744 | tf_op jit(solution)/shard_map/ppermute | solution.py:22
  250.0 10.6 %collective-permute-start.10 = (f32[192,128]{1,0:T(8,128)S(1)}, f32[192,128]{1,0:T(8,128)S(1)}, u32[]{:S(2)}, u32[]{:S(2)}) collective-permute-start(f32[192,128]{1,0:T(8,128)S(1)} %reduce_sum.9.mine_last_ref), channel_id=1, source_target_pairs={{0,1},{1,0},{2,3},{3,2},{4,5},{5,4},{6,7},{7,6},{8,9},{9,8},{10,11... | collective-permute-start | bytes 294920 | tf_op jit(solution)/shard_map/ppermute | solution.py:22

commit v6 on v5

--- a/solution.py
+++ b/solution.py
@@ -127,11 +127,15 @@
     return product_call(last_kernel, 4, rows, slots, sums)(index, tiles, scale, source)
 
 
+def member_of(line, pair, pairs):
+    return line // 2 * 2 * pairs + 2 * pair + line % 2
+
+
 def piece_sums(came_ref, lines, pairs):
     piece = came_ref.shape[0] // (2 * lines * pairs)
 
     def read(line, pair, which):
-        first = (2 * (line * pairs + pair) + which) * piece
+        first = (2 * member_of(line, pair, pairs) + which) * piece
         return came_ref[first:first + piece]
 
     sums = []
@@ -149,7 +153,7 @@
     piece = sums[0].shape[0]
     for line in range(lines):
         for pair in range(pairs):
-            first = 2 * (line * pairs + pair) * piece
+            first = 2 * member_of(line, pair, pairs) * piece
             out_ref[first:first + piece] = sums[(line - 2 * pair) % lines]
             out_ref[first + piece:first + 2 * piece] = sums[(line - 2 * pair - 1) % lines]
 
@@ -219,17 +223,32 @@
     return lax.all_to_all(chunks, "blk", 0, 0, axis_index_groups=rings)
 
 
-def pair_exchange(block, pairs):
+def copies_kernel(near_ref, far_ref, out_ref):
+    total = near_ref[...] + far_ref[...]
+    for pair in range(out_ref.shape[0]):
+        out_ref[pair] = total
+
+
+def pair_exchange(near, far, pairs):
+    vmem = pl.BlockSpec(memory_space=pltpu.VMEM)
+    copies = pl.pallas_call(
+        copies_kernel,
+        in_specs=[vmem, vmem],
+        out_specs=vmem,
+        out_shape=jax.ShapeDtypeStruct((pairs, *near.shape), jnp.float32),
+        compiler_params=pltpu.CompilerParams(vmem_limit_bytes=VMEM_BYTES),
+    )(near, far)
     cycle, groups = lax.axis_size("blk"), lax.axis_size("rep")
     sets = [[p * groups + w for w in range(core, groups, 2)] for p in range(cycle) for core in range(2)]
-    copies = jnp.broadcast_to(block[None], (pairs, *block.shape))
     return lax.all_to_all(copies, ("blk", "rep"), 0, 0, axis_index_groups=sets)
 
 
 def plane_exchange(block, span):
     cycle, groups = lax.axis_size("blk"), lax.axis_size("rep")
+    pairs = groups // 2
+    places = sorted((member_of(line, pair, pairs), line, pair) for line in range(cycle // span) for pair in range(pairs))
     planes = [
-        [p * groups + w for p in range(y, cycle, span) for w in range(core, groups, 2)]
+        [(line * span + y) * groups + 2 * pair + core for _, line, pair in places]
         for y in range(span) for core in range(2)
     ]
     pieces = block.reshape(len(planes[0]), 1, -1)
@@ -306,8 +325,7 @@
     units = ring_exchange(chunks).reshape(-1, 128)
     far, source = near_product(far_index, far_tiles, far_scale, units)
     near = last_product(near_index, near_tiles, scale, source)
-    chip = near + send(far, lambda p, w: (p + span, w))
-    last = pair_exchange(chip, pairs).sum(axis=0)
+    last = pair_exchange(near, send(far, lambda p, w: (p + span, w)), pairs).sum(axis=0)
     return finish(core_ref, ordered, root, [mine, last, swap_cores(mine), swap_cores(last)])
 
 

time: 263 us -> 261 us (level)
  no operation moved by 1% of the time
where the time goes in v6:
time: 261 us; the launch traced here: 260 us
  blocking collectives  155 us (59%)
  starting transfers between devices  57.2 us (22%)
  waiting for transfers between devices  22.6 us (9%)
  Pallas kernels  16.8 us (6%)
  other arithmetic  5.65 us (2%)
  local copies, waits for them, and re-layouts  2.94 us (1%)
    all_to_all x6, blocking collectives, plane_exchange(): lax.all_to_all(pieces, ('blk', 'rep'), 0, 0, axis_index_groups=planes)  93.5 us
    all_to_all x3, blocking collectives, ring_exchange(): return lax.all_to_all(chunks, 'blk', 0, 0, axis_index_groups=rings)  61.1 us
    ppermute x11, starting transfers between devices, send(): return lax.ppermute(block, ('blk', 'rep'), route)  49.9 us
    ppermute x11, waiting for transfers between devices, send(): return lax.ppermute(block, ('blk', 'rep'), route)  21.9 us
  transfers between devices with their start and end apart: 13, of which 6 were waited for; matrix products, arithmetic and copies ran while one was open for 3% of the time, Pallas kernels for 2%

profile of v6, /device:TPU:1, one launch (start us, length us, event | category | flops | bytes accessed | tf_op | source)
XLA Modules:
  0.0 260.2 jit_solution(4201459051801372437)
XLA Ops:
  0.0 0.0 copy-start
  0.0 9.0 %collective-permute-start.2 = (f32[3,12,128,128]{3,2,1,0:T(8,128)}, f32[3,12,128,128]{3,2,1,0:T(8,128)}, u32[]{:S(2)}, u32[]{:S(2)}) collective-permute-start(f32[3,12,128,128]{3,2,1,0:T(8,128)} %param.7), channel_id=1, source_target_pairs={{0,1},{1,0},{2,3},{3,2},{4,5},{5,4},{6,7},{7,6},{8,9},{9,8},{10,11... | collective-permute-start | bytes 7077896 | tf_op jit(solution)/shard_map/ppermute | solution.py:22
  9.1 0.7 broadcast_subtract_fusion
  9.8 1.1 gather_fusion
  10.9 0.0 copy-start.4
  10.9 0.0 copy-start.5
  10.9 0.1 copy.8
  11.1 1.3 fusion.1
  12.4 0.7 collective-permute-start
  13.1 1.9 collective-permute-start.1
  15.0 0.0 collective-permute-done.2
  15.0 2.4 slice_select_fusion
  17.4 0.0 collective-permute-done
  17.4 4.0 %collective-permute-done.1 = f32[192,128]{1,0:T(8,128)S(1)} collective-permute-done((f32[192,128]{1,0:T(8,128)S(1)}, f32[192,128]{1,0:T(8,128)S(1)}, u32[]{:S(2)}, u32[]{:S(2)}) %collective-permute-start.1) | collective-permute-done | bytes 98336 | tf_op jit(solution)/shard_map/ppermute | solution.py:22
  21.5 1.9 collective-permute-start.3
  23.4 0.0 copy-done.4
  23.4 0.0 copy-done.5
  23.4 0.1 fusion
  23.5 2.7 %collective-permute-start.4 = (s32[3,12]{1,0:T(4,128)S(1)}, s32[3,12]{1,0:T(4,128)S(1)}, u32[]{:S(2)}, u32[]{:S(2)}) collective-permute-start(s32[3,12]{1,0:T(4,128)S(1)} %fusion), channel_id=1, source_target_pairs={{0,1},{1,0},{2,3},{3,2},{4,5},{5,4},{6,7},{7,6},{8,9},{9,8},{10,11... | collective-permute-start | bytes 440 | tf_op jit(solution)/shard_map/ppermute | solution.py:22
  26.2 1.0 broadcast_select_fusion
  27.2 3.9 %all-to-all-start = ((f32[8,192,128]{2,1,0:T(8,128)}), f32[8,192,128]{2,1,0:T(8,128)S(1)}, u32[]{:S(2)}, u32[]{:S(2)}) async-start(f32[8,192,128]{2,1,0:T(8,128)} %broadcast_select_fusion), calls=%async_computation | async-start | bytes 1572864 | tf_op jit(solution)/shard_map/all_to_all | solution.py:223
  31.1 0.0 collective-permute-done.4
  31.1 0.1 broadcast_select_fusion.1
  31.2 1.7 copy-done.2
  32.9 2.4 shard_map.64.tiles_ref
  35.3 2.2 collective-permute-start.5
  37.5 13.0 %collective-permute-done.5 = f32[6,128]{1,0:T(8,128)S(1)} collective-permute-done((f32[6,128]{1,0:T(8,128)S(1)}, f32[6,128]{1,0:T(8,128)S(1)}, u32[]{:S(2)}, u32[]{:S(2)}) %collective-permute-start.5) | collective-permute-done | bytes 3104 | tf_op jit(solution)/shard_map/ppermute | solution.py:22
  50.5 0.0 collective-permute-done.3.mine_ref
  50.5 3.5 %collective-permute-start.6 = (f32[2304,128]{1,0:T(8,128)}, f32[2304,128]{1,0:T(8,128)}, u32[]{:S(2)}, u32[]{:S(2)}) collective-permute-start(f32[2304,128]{1,0:T(8,128)} %collective-permute-done.3.mine_ref), channel_id=1, source_target_pairs={{0,1},{1,0},{2,3},{3,2},{4,5},{5,4},{6,7},{7,6},{8,9},{9,8},{10,11... | collective-permute-start | bytes 3538952 | tf_op jit(solution)/shard_map/ppermute | solution.py:22
  54.0 0.7 all-to-all-done
  54.7 1.2 shard_map.66
  56.0 0.8 collective-permute-done.6.other_ref
  56.8 2.3 shard_map.65.tiles_ref
  59.1 1.2 shard_map.67
  60.3 23.6 %all_to_all.55 = f32[32,1,1536]{2,1,0:T(1,128)S(1)} all-to-all(f32[32,1,1536]{2,1,0:T(1,128)S(1)} %bitcast.48), channel_id=1, replica_groups={{0,64,2,66,4,68,6,70,128,192,130,194,132,196,134,198,256,320,258,322,26..., dimensions={0} | all-to-all | bytes 393216 | tf_op jit(solution)/shard_map/all_to_all | solution.py:255
  84.0 14.6 %all_to_all.56 = f32[32,1,1536]{2,1,0:T(1,128)S(1)} all-to-all(f32[32,1,1536]{2,1,0:T(1,128)S(1)} %bitcast.43), channel_id=1, replica_groups={{0,64,2,66,4,68,6,70,128,192,130,194,132,196,134,198,256,320,258,322,26..., dimensions={0} | all-to-all | bytes 393216 | tf_op jit(solution)/shard_map/all_to_all | solution.py:255
  98.6 0.1 shard_map.69
  98.7 22.7 %all_to_all.57 = f32[8,192,128]{2,1,0:T(8,128)S(1)} all-to-all(f32[8,192,128]{2,1,0:T(8,128)S(1)} %get-tuple-element.38), channel_id=1, replica_groups={{0,8,16,24,32,40,48,56},{64,72,80,88,96,104,112,120},{128,136,144,152,1..., dimensions={0} | all-to-all | bytes 1572864 | tf_op jit(solution)/shard_map/all_to_all | solution.py:223
  121.4 1.2 shard_map.70
  122.6 1.2 shard_map.71
  123.9 15.0 %all_to_all.58 = f32[32,1,1536]{2,1,0:T(1,128)S(1)} all-to-all(f32[32,1,1536]{2,1,0:T(1,128)S(1)} %bitcast.49), channel_id=1, replica_groups={{0,64,2,66,4,68,6,70,128,192,130,194,132,196,134,198,256,320,258,322,26..., dimensions={0} | all-to-all | bytes 393216 | tf_op jit(solution)/shard_map/all_to_all | solution.py:255
  138.8 13.3 %all_to_all.59 = f32[32,1,1536]{2,1,0:T(1,128)S(1)} all-to-all(f32[32,1,1536]{2,1,0:T(1,128)S(1)} %bitcast.45), channel_id=1, replica_groups={{0,64,2,66,4,68,6,70,128,192,130,194,132,196,134,198,256,320,258,322,26..., dimensions={0} | all-to-all | bytes 393216 | tf_op jit(solution)/shard_map/all_to_all | solution.py:255
  152.1 0.1 shard_map.73
  152.2 19.4 %all_to_all.60 = f32[8,192,128]{2,1,0:T(8,128)S(1)} all-to-all(f32[8,192,128]{2,1,0:T(8,128)S(1)} %get-tuple-element.42), channel_id=1, replica_groups={{0,8,16,24,32,40,48,56},{64,72,80,88,96,104,112,120},{128,136,144,152,1..., dimensions={0} | all-to-all | bytes 1572864 | tf_op jit(solution)/shard_map/all_to_all | solution.py:223
  171.6 1.2 shard_map.74
  172.9 1.2 shard_map.75
  174.1 13.8 %all_to_all.61 = f32[32,1,1536]{2,1,0:T(1,128)S(1)} all-to-all(f32[32,1,1536]{2,1,0:T(1,128)S(1)} %bitcast.50), channel_id=1, replica_groups={{0,64,2,66,4,68,6,70,128,192,130,194,132,196,134,198,256,320,258,322,26..., dimensions={0} | all-to-all | bytes 393216 | tf_op jit(solution)/shard_map/all_to_all | solution.py:255
  188.0 13.2 %all_to_all.62 = f32[32,1,1536]{2,1,0:T(1,128)S(1)} all-to-all(f32[32,1,1536]{2,1,0:T(1,128)S(1)} %bitcast.47), channel_id=1, replica_groups={{0,64,2,66,4,68,6,70,128,192,130,194,132,196,134,198,256,320,258,322,26..., dimensions={0} | all-to-all | bytes 393216 | tf_op jit(solution)/shard_map/all_to_all | solution.py:255
  201.1 0.1 shard_map.77
  201.2 19.0 %all_to_all.63 = f32[8,192,128]{2,1,0:T(8,128)S(1)} all-to-all(f32[8,192,128]{2,1,0:T(8,128)S(1)} %get-tuple-element.46), channel_id=1, replica_groups={{0,8,16,24,32,40,48,56},{64,72,80,88,96,104,112,120},{128,136,144,152,1..., dimensions={0} | all-to-all | bytes 1572864 | tf_op jit(solution)/shard_map/all_to_all | solution.py:223
  220.2 1.2 shard_map.78
  221.4 3.4 %collective-permute-start.8 = (f32[192,128]{1,0:T(8,128)S(1)}, f32[192,128]{1,0:T(8,128)S(1)}, u32[]{:S(2)}, u32[]{:S(2)}) collective-permute-start(f32[192,128]{1,0:T(8,128)S(1)} %get-tuple-element.48), channel_id=1, source_target_pairs={{0,64},{1,65},{2,66},{3,67},{4,68},{5,69},{6,70},{7,71},{8,72},{9,... | collective-permute-start | bytes 294920 | tf_op jit(solution)/shard_map/ppermute | solution.py:22
  224.8 1.2 shard_map.79.near_ref
  226.0 3.2 %collective-permute-done.8.far_ref = f32[192,128]{1,0:T(8,128)S(1)} collective-permute-done((f32[192,128]{1,0:T(8,128)S(1)}, f32[192,128]{1,0:T(8,128)S(1)}, u32[]{:S(2)}, u32[]{:S(2)}) %collective-permute-start.8) | collective-permute-done | bytes 98336 | tf_op jit(solution)/shard_map/ppermute | solution.py:22
  229.2 0.8 shard_map.80
  230.0 3.5 %all-to-all-start.10 = ((f32[4,192,128]{2,1,0:T(8,128)}), f32[4,192,128]{2,1,0:T(8,128)S(1)}, u32[]{:S(2)}, u32[]{:S(2)}) async-start(f32[4,192,128]{2,1,0:T(8,128)} %shard_map.80), calls=%async_computation.10 | async-start | bytes 786432 | tf_op jit(solution)/shard_map/all_to_all | solution.py:243
  233.5 0.7 collective-permute-start.7
  234.2 0.0 collective-permute-done.7.mine_ref
  234.2 14.2 %collective-permute-start.9 = (f32[576,128]{1,0:T(8,128)S(1)}, f32[576,128]{1,0:T(8,128)S(1)}, u32[]{:S(2)}, u32[]{:S(2)}) collective-permute-start(f32[576,128]{1,0:T(8,128)S(1)} %collective-permute-done.7.mine_ref), channel_id=1, source_target_pairs={{0,1},{1,0},{2,3},{3,2},{4,5},{5,4},{6,7},{7,6},{8,9},{9,8},{10,11... | collective-permute-start | bytes 884744 | tf_op jit(solution)/shard_map/ppermute | solution.py:22
  248.4 0.0 all-to-all-done.10
  248.5 9.6 %collective-permute-start.10 = (f32[192,128]{1,0:T(8,128)S(1)}, f32[192,128]{1,0:T(8,128)S(1)}, u32[]{:S(2)}, u32[]{:S(2)}) collective-permute-start(f32[192,128]{1,0:T(8,128)S(1)} %reduce_sum.9.mine_last_ref), channel_id=1, source_target_pairs={{0,1},{1,0},{2,3},{3,2},{4,5},{5,4},{6,7},{7,6},{8,9},{9,8},{10,11... | collective-permute-start | bytes 294920 | tf_op jit(solution)/shard_map/ppermute | solution.py:22
  258.1 0.0 collective-permute-done.9.other_ref
  258.1 0.9 collective-permute-done.10.other_last_ref
  259.0 1.2 shard_map.81
  (18 shorter events, 0.2 us)
Async XLA Ops:
  0.0 9.8 %copy-start = (f32[384,128]{1,0:T(8,128)S(1)}, f32[384,128]{1,0:T(8,128)}, u32[]{:S(2)}) copy-start(f32[384,128]{1,0:T(8,128)} %param.6) | copy-start | bytes 589828
  0.0 15.0 %copy-start.1 = (f32[3,12,128,128]{3,2,1,0:T(8,128)S(1)}, f32[3,12,128,128]{3,2,1,0:T(8,128)}, u32[]{:S(2)}) copy-start(f32[3,12,128,128]{3,2,1,0:T(8,128)} %param.7) | copy-start | bytes 7077892
  0.0 15.0 %collective-permute-start.2 = (f32[3,12,128,128]{3,2,1,0:T(8,128)}, f32[3,12,128,128]{3,2,1,0:T(8,128)}, u32[]{:S(2)}, u32[]{:S(2)}) collective-permute-start(f32[3,12,128,128]{3,2,1,0:T(8,128)} %param.7), channel_id=1, source_target_pairs={{0,1},{1,0},{2,3},{3,2},{4,5},{5,4},{6,7},{7,6},{8,9},{9,8},{10,11... | collective-permute-start | bytes 7077896 | tf_op jit(solution)/shard_map/ppermute | solution.py:22
  10.9 12.5 %copy-start.4 = (s32[3,12]{1,0:T(4,128)S(1)}, s32[3,12]{1,0:T(4,128)}, u32[]{:S(2)}) copy-start(s32[3,12]{1,0:T(4,128)} %param.8) | copy-start | bytes 436
  10.9 12.5 %copy-start.5 = (s32[3,1]{0,1:T(1,128)S(1)}, s32[3,1]{0,1:T(1,128)}, u32[]{:S(2)}) copy-start(s32[3,1]{0,1:T(1,128)} %param.9) | copy-start | bytes 40
  12.4 5.1 %collective-permute-start = (f32[192,128]{1,0:T(8,128)S(1)}, f32[192,128]{1,0:T(8,128)S(1)}, u32[]{:S(2)}, u32[]{:S(2)}) collective-permute-start(f32[192,128]{1,0:T(8,128)S(1)} %bitcast.51), channel_id=1, source_target_pairs={{0,0},{1,1},{2,130},{3,131},{4,260},{5,261},{6,390},{7,391},{8,8},... | collective-permute-start | bytes 294920 | tf_op jit(solution)/shard_map/ppermute | solution.py:22
  13.1 8.4 %collective-permute-start.1 = (f32[192,128]{1,0:T(8,128)S(1)}, f32[192,128]{1,0:T(8,128)S(1)}, u32[]{:S(2)}, u32[]{:S(2)}) collective-permute-start(f32[192,128]{1,0:T(8,128)S(1)} %bitcast.52), channel_id=1, source_target_pairs={{0,64},{1,65},{2,194},{3,195},{4,324},{5,325},{6,454},{7,455},{8,7... | collective-permute-start | bytes 294920 | tf_op jit(solution)/shard_map/ppermute | solution.py:22
  21.5 29.0 %collective-permute-start.3 = (f32[2304,128]{1,0:T(8,128)}, f32[2304,128]{1,0:T(8,128)}, u32[]{:S(2)}, u32[]{:S(2)}) collective-permute-start(f32[2304,128]{1,0:T(8,128)} %bitcast.6), channel_id=1, source_target_pairs={{0,448},{1,449},{2,450},{3,451},{4,452},{5,453},{6,454},{7,455},{8... | collective-permute-start | bytes 3538952 | tf_op jit(solution)/shard_map/ppermute | solution.py:22
  23.5 7.6 %collective-permute-start.4 = (s32[3,12]{1,0:T(4,128)S(1)}, s32[3,12]{1,0:T(4,128)S(1)}, u32[]{:S(2)}, u32[]{:S(2)}) collective-permute-start(s32[3,12]{1,0:T(4,128)S(1)} %fusion), channel_id=1, source_target_pairs={{0,1},{1,0},{2,3},{3,2},{4,5},{5,4},{6,7},{7,6},{8,9},{9,8},{10,11... | collective-permute-start | bytes 440 | tf_op jit(solution)/shard_map/ppermute | solution.py:22
  27.2 27.5 %all-to-all-start = ((f32[8,192,128]{2,1,0:T(8,128)}), f32[8,192,128]{2,1,0:T(8,128)S(1)}, u32[]{:S(2)}, u32[]{:S(2)}) async-start(f32[8,192,128]{2,1,0:T(8,128)} %broadcast_select_fusion), calls=%async_computation | async-start | bytes 1572864 | tf_op jit(solution)/shard_map/all_to_all | solution.py:223
  31.2 1.7 copy-start.2
  35.3 15.2 %collective-permute-start.5 = (f32[6,128]{1,0:T(8,128)S(1)}, f32[6,128]{1,0:T(8,128)S(1)}, u32[]{:S(2)}, u32[]{:S(2)}) collective-permute-start(f32[6,128]{1,0:T(8,128)S(1)} %select_maximum_fusion), channel_id=1, source_target_pairs={{0,448},{1,449},{2,450},{3,451},{4,452},{5,453},{6,454},{7,455},{8... | collective-permute-start | bytes 9224 | tf_op jit(solution)/shard_map/ppermute | solution.py:22
  50.5 6.3 %collective-permute-start.6 = (f32[2304,128]{1,0:T(8,128)}, f32[2304,128]{1,0:T(8,128)}, u32[]{:S(2)}, u32[]{:S(2)}) collective-permute-start(f32[2304,128]{1,0:T(8,128)} %collective-permute-done.3.mine_ref), channel_id=1, source_target_pairs={{0,1},{1,0},{2,3},{3,2},{4,5},{5,4},{6,7},{7,6},{8,9},{9,8},{10,11... | collective-permute-start | bytes 3538952 | tf_op jit(solution)/shard_map/ppermute | solution.py:22
  221.4 7.8 %collective-permute-start.8 = (f32[192,128]{1,0:T(8,128)S(1)}, f32[192,128]{1,0:T(8,128)S(1)}, u32[]{:S(2)}, u32[]{:S(2)}) collective-permute-start(f32[192,128]{1,0:T(8,128)S(1)} %get-tuple-element.48), channel_id=1, source_target_pairs={{0,64},{1,65},{2,66},{3,67},{4,68},{5,69},{6,70},{7,71},{8,72},{9,... | collective-permute-start | bytes 294920 | tf_op jit(solution)/shard_map/ppermute | solution.py:22
  224.8 34.2 %copy-start.3 = (f32[3,128]{1,0:T(4,128)S(1)}, f32[3,128]{1,0:T(4,128)}, u32[]{:S(2)}) copy-start(f32[3,128]{1,0:T(4,128)} %get-tuple-element.52.root_ref) | copy-start | bytes 4612
  230.0 18.4 %all-to-all-start.10 = ((f32[4,192,128]{2,1,0:T(8,128)}), f32[4,192,128]{2,1,0:T(8,128)S(1)}, u32[]{:S(2)}, u32[]{:S(2)}) async-start(f32[4,192,128]{2,1,0:T(8,128)} %shard_map.80), calls=%async_computation.10 | async-start | bytes 786432 | tf_op jit(solution)/shard_map/all_to_all | solution.py:243
  233.5 0.7 collective-permute-start.7
  234.2 23.9 %collective-permute-start.9 = (f32[576,128]{1,0:T(8,128)S(1)}, f32[576,128]{1,0:T(8,128)S(1)}, u32[]{:S(2)}, u32[]{:S(2)}) collective-permute-start(f32[576,128]{1,0:T(8,128)S(1)} %collective-permute-done.7.mine_ref), channel_id=1, source_target_pairs={{0,1},{1,0},{2,3},{3,2},{4,5},{5,4},{6,7},{7,6},{8,9},{9,8},{10,11... | collective-permute-start | bytes 884744 | tf_op jit(solution)/shard_map/ppermute | solution.py:22
  248.5 10.6 %collective-permute-start.10 = (f32[192,128]{1,0:T(8,128)S(1)}, f32[192,128]{1,0:T(8,128)S(1)}, u32[]{:S(2)}, u32[]{:S(2)}) collective-permute-start(f32[192,128]{1,0:T(8,128)S(1)} %reduce_sum.9.mine_last_ref), channel_id=1, source_target_pairs={{0,1},{1,0},{2,3},{3,2},{4,5},{5,4},{6,7},{7,6},{8,9},{9,8},{10,11... | collective-permute-start | bytes 294920 | tf_op jit(solution)/shard_map/ppermute | solution.py:22

commit v7 on v6

--- a/solution.py
+++ b/solution.py
@@ -128,7 +128,7 @@
 
 
 def member_of(line, pair, pairs):
-    return line // 2 * 2 * pairs + 2 * pair + line % 2
+    return (2 * pair + line % 2) * pairs + line // 2
 
 
 def piece_sums(came_ref, lines, pairs):

time: 261 us -> 260 us (level)
  no operation moved by 1% of the time
where the time goes in v7:
time: 260 us; the launch traced here: 259 us
  blocking collectives  154 us (59%)
  starting transfers between devices  56.3 us (22%)
  waiting for transfers between devices  23.4 us (9%)
  Pallas kernels  16.8 us (6%)
  other arithmetic  5.65 us (2%)
  local copies, waits for them, and re-layouts  2.94 us (1%)
    all_to_all x6, blocking collectives, plane_exchange(): lax.all_to_all(pieces, ('blk', 'rep'), 0, 0, axis_index_groups=planes)  92.8 us
    all_to_all x3, blocking collectives, ring_exchange(): return lax.all_to_all(chunks, 'blk', 0, 0, axis_index_groups=rings)  61.1 us
    ppermute x11, starting transfers between devices, send(): return lax.ppermute(block, ('blk', 'rep'), route)  48.9 us
    ppermute x11, waiting for transfers between devices, send(): return lax.ppermute(block, ('blk', 'rep'), route)  22.7 us
  transfers between devices with their start and end apart: 13, of which 6 were waited for; matrix products, arithmetic and copies ran while one was open for 3% of the time, Pallas kernels for 2%

profile of v7, /device:TPU:1, one launch (start us, length us, event | category | flops | bytes accessed | tf_op | source)
XLA Modules:
  0.0 259.4 jit_solution(2155621781618732363)
XLA Ops:
  0.0 0.0 copy-start
  0.0 9.0 %collective-permute-start.2 = (f32[3,12,128,128]{3,2,1,0:T(8,128)}, f32[3,12,128,128]{3,2,1,0:T(8,128)}, u32[]{:S(2)}, u32[]{:S(2)}) collective-permute-start(f32[3,12,128,128]{3,2,1,0:T(8,128)} %param.7), channel_id=1, source_target_pairs={{0,1},{1,0},{2,3},{3,2},{4,5},{5,4},{6,7},{7,6},{8,9},{9,8},{10,11... | collective-permute-start | bytes 7077896 | tf_op jit(solution)/shard_map/ppermute | solution.py:22
  9.1 0.7 broadcast_subtract_fusion
  9.8 1.1 gather_fusion
  10.9 0.0 copy-start.4
  10.9 0.0 copy-start.5
  10.9 0.1 copy.8
  11.1 1.3 fusion.1
  12.4 0.7 collective-permute-start
  13.1 1.9 collective-permute-start.1
  15.0 0.0 collective-permute-done.2
  15.0 2.4 slice_select_fusion
  17.4 0.0 collective-permute-done
  17.4 4.0 %collective-permute-done.1 = f32[192,128]{1,0:T(8,128)S(1)} collective-permute-done((f32[192,128]{1,0:T(8,128)S(1)}, f32[192,128]{1,0:T(8,128)S(1)}, u32[]{:S(2)}, u32[]{:S(2)}) %collective-permute-start.1) | collective-permute-done | bytes 98336 | tf_op jit(solution)/shard_map/ppermute | solution.py:22
  21.5 1.9 collective-permute-start.3
  23.4 0.0 copy-done.4
  23.4 0.0 copy-done.5
  23.4 0.1 fusion
  23.5 2.7 %collective-permute-start.4 = (s32[3,12]{1,0:T(4,128)S(1)}, s32[3,12]{1,0:T(4,128)S(1)}, u32[]{:S(2)}, u32[]{:S(2)}) collective-permute-start(s32[3,12]{1,0:T(4,128)S(1)} %fusion), channel_id=1, source_target_pairs={{0,1},{1,0},{2,3},{3,2},{4,5},{5,4},{6,7},{7,6},{8,9},{9,8},{10,11... | collective-permute-start | bytes 440 | tf_op jit(solution)/shard_map/ppermute | solution.py:22
  26.2 1.0 broadcast_select_fusion
  27.2 3.9 %all-to-all-start = ((f32[8,192,128]{2,1,0:T(8,128)}), f32[8,192,128]{2,1,0:T(8,128)S(1)}, u32[]{:S(2)}, u32[]{:S(2)}) async-start(f32[8,192,128]{2,1,0:T(8,128)} %broadcast_select_fusion), calls=%async_computation | async-start | bytes 1572864 | tf_op jit(solution)/shard_map/all_to_all | solution.py:223
  31.1 0.0 collective-permute-done.4
  31.1 0.1 broadcast_select_fusion.1
  31.2 1.7 copy-done.2
  32.9 2.4 shard_map.64.tiles_ref
  35.3 2.2 collective-permute-start.5
  37.5 13.0 %collective-permute-done.5 = f32[6,128]{1,0:T(8,128)S(1)} collective-permute-done((f32[6,128]{1,0:T(8,128)S(1)}, f32[6,128]{1,0:T(8,128)S(1)}, u32[]{:S(2)}, u32[]{:S(2)}) %collective-permute-start.5) | collective-permute-done | bytes 3104 | tf_op jit(solution)/shard_map/ppermute | solution.py:22
  50.5 0.0 collective-permute-done.3.mine_ref
  50.5 3.5 %collective-permute-start.6 = (f32[2304,128]{1,0:T(8,128)}, f32[2304,128]{1,0:T(8,128)}, u32[]{:S(2)}, u32[]{:S(2)}) collective-permute-start(f32[2304,128]{1,0:T(8,128)} %collective-permute-done.3.mine_ref), channel_id=1, source_target_pairs={{0,1},{1,0},{2,3},{3,2},{4,5},{5,4},{6,7},{7,6},{8,9},{9,8},{10,11... | collective-permute-start | bytes 3538952 | tf_op jit(solution)/shard_map/ppermute | solution.py:22
  54.0 0.7 all-to-all-done
  54.7 1.2 shard_map.66
  56.0 0.8 collective-permute-done.6.other_ref
  56.8 2.3 shard_map.65.tiles_ref
  59.1 1.2 shard_map.67
  60.3 24.7 %all_to_all.55 = f32[32,1,1536]{2,1,0:T(1,128)S(1)} all-to-all(f32[32,1,1536]{2,1,0:T(1,128)S(1)} %bitcast.48), channel_id=1, replica_groups={{0,128,256,384,64,192,320,448,2,130,258,386,66,194,322,450,4,132,260,38..., dimensions={0} | all-to-all | bytes 393216 | tf_op jit(solution)/shard_map/all_to_all | solution.py:255
  85.1 13.9 %all_to_all.56 = f32[32,1,1536]{2,1,0:T(1,128)S(1)} all-to-all(f32[32,1,1536]{2,1,0:T(1,128)S(1)} %bitcast.43), channel_id=1, replica_groups={{0,128,256,384,64,192,320,448,2,130,258,386,66,194,322,450,4,132,260,38..., dimensions={0} | all-to-all | bytes 393216 | tf_op jit(solution)/shard_map/all_to_all | solution.py:255
  99.0 0.1 shard_map.69
  99.0 22.7 %all_to_all.57 = f32[8,192,128]{2,1,0:T(8,128)S(1)} all-to-all(f32[8,192,128]{2,1,0:T(8,128)S(1)} %get-tuple-element.38), channel_id=1, replica_groups={{0,8,16,24,32,40,48,56},{64,72,80,88,96,104,112,120},{128,136,144,152,1..., dimensions={0} | all-to-all | bytes 1572864 | tf_op jit(solution)/shard_map/all_to_all | solution.py:223
  121.7 1.2 shard_map.70
  123.0 1.2 shard_map.71
  124.2 14.4 %all_to_all.58 = f32[32,1,1536]{2,1,0:T(1,128)S(1)} all-to-all(f32[32,1,1536]{2,1,0:T(1,128)S(1)} %bitcast.49), channel_id=1, replica_groups={{0,128,256,384,64,192,320,448,2,130,258,386,66,194,322,450,4,132,260,38..., dimensions={0} | all-to-all | bytes 393216 | tf_op jit(solution)/shard_map/all_to_all | solution.py:255
  138.6 13.2 %all_to_all.59 = f32[32,1,1536]{2,1,0:T(1,128)S(1)} all-to-all(f32[32,1,1536]{2,1,0:T(1,128)S(1)} %bitcast.45), channel_id=1, replica_groups={{0,128,256,384,64,192,320,448,2,130,258,386,66,194,322,450,4,132,260,38..., dimensions={0} | all-to-all | bytes 393216 | tf_op jit(solution)/shard_map/all_to_all | solution.py:255
  151.8 0.1 shard_map.73
  151.9 19.0 %all_to_all.60 = f32[8,192,128]{2,1,0:T(8,128)S(1)} all-to-all(f32[8,192,128]{2,1,0:T(8,128)S(1)} %get-tuple-element.42), channel_id=1, replica_groups={{0,8,16,24,32,40,48,56},{64,72,80,88,96,104,112,120},{128,136,144,152,1..., dimensions={0} | all-to-all | bytes 1572864 | tf_op jit(solution)/shard_map/all_to_all | solution.py:223
  170.9 1.2 shard_map.74
  172.1 1.2 shard_map.75
  173.4 13.6 %all_to_all.61 = f32[32,1,1536]{2,1,0:T(1,128)S(1)} all-to-all(f32[32,1,1536]{2,1,0:T(1,128)S(1)} %bitcast.50), channel_id=1, replica_groups={{0,128,256,384,64,192,320,448,2,130,258,386,66,194,322,450,4,132,260,38..., dimensions={0} | all-to-all | bytes 393216 | tf_op jit(solution)/shard_map/all_to_all | solution.py:255
  187.0 13.1 %all_to_all.62 = f32[32,1,1536]{2,1,0:T(1,128)S(1)} all-to-all(f32[32,1,1536]{2,1,0:T(1,128)S(1)} %bitcast.47), channel_id=1, replica_groups={{0,128,256,384,64,192,320,448,2,130,258,386,66,194,322,450,4,132,260,38..., dimensions={0} | all-to-all | bytes 393216 | tf_op jit(solution)/shard_map/all_to_all | solution.py:255
  200.0 0.1 shard_map.77
  200.1 19.4 %all_to_all.63 = f32[8,192,128]{2,1,0:T(8,128)S(1)} all-to-all(f32[8,192,128]{2,1,0:T(8,128)S(1)} %get-tuple-element.46), channel_id=1, replica_groups={{0,8,16,24,32,40,48,56},{64,72,80,88,96,104,112,120},{128,136,144,152,1..., dimensions={0} | all-to-all | bytes 1572864 | tf_op jit(solution)/shard_map/all_to_all | solution.py:223
  219.5 1.2 shard_map.78
  220.8 2.6 collective-permute-start.8
  223.4 1.2 shard_map.79.near_ref
  224.6 4.0 %collective-permute-done.8.far_ref = f32[192,128]{1,0:T(8,128)S(1)} collective-permute-done((f32[192,128]{1,0:T(8,128)S(1)}, f32[192,128]{1,0:T(8,128)S(1)}, u32[]{:S(2)}, u32[]{:S(2)}) %collective-permute-start.8) | collective-permute-done | bytes 98336 | tf_op jit(solution)/shard_map/ppermute | solution.py:22
  228.6 0.8 shard_map.80
  229.3 3.5 %all-to-all-start.10 = ((f32[4,192,128]{2,1,0:T(8,128)}), f32[4,192,128]{2,1,0:T(8,128)S(1)}, u32[]{:S(2)}, u32[]{:S(2)}) async-start(f32[4,192,128]{2,1,0:T(8,128)} %shard_map.80), calls=%async_computation.10 | async-start | bytes 786432 | tf_op jit(solution)/shard_map/all_to_all | solution.py:243
  232.8 0.7 collective-permute-start.7
  233.5 0.0 collective-permute-done.7.mine_ref
  233.5 14.1 %collective-permute-start.9 = (f32[576,128]{1,0:T(8,128)S(1)}, f32[576,128]{1,0:T(8,128)S(1)}, u32[]{:S(2)}, u32[]{:S(2)}) collective-permute-start(f32[576,128]{1,0:T(8,128)S(1)} %collective-permute-done.7.mine_ref), channel_id=1, source_target_pairs={{0,1},{1,0},{2,3},{3,2},{4,5},{5,4},{6,7},{7,6},{8,9},{9,8},{10,11... | collective-permute-start | bytes 884744 | tf_op jit(solution)/shard_map/ppermute | solution.py:22
  247.6 0.0 all-to-all-done.10
  247.7 9.6 %collective-permute-start.10 = (f32[192,128]{1,0:T(8,128)S(1)}, f32[192,128]{1,0:T(8,128)S(1)}, u32[]{:S(2)}, u32[]{:S(2)}) collective-permute-start(f32[192,128]{1,0:T(8,128)S(1)} %reduce_sum.9.mine_last_ref), channel_id=1, source_target_pairs={{0,1},{1,0},{2,3},{3,2},{4,5},{5,4},{6,7},{7,6},{8,9},{9,8},{10,11... | collective-permute-start | bytes 294920 | tf_op jit(solution)/shard_map/ppermute | solution.py:22
  257.3 0.0 collective-permute-done.9.other_ref
  257.3 0.9 collective-permute-done.10.other_last_ref
  258.2 1.2 shard_map.81
  (18 shorter events, 0.2 us)
Async XLA Ops:
  0.0 9.8 %copy-start = (f32[384,128]{1,0:T(8,128)S(1)}, f32[384,128]{1,0:T(8,128)}, u32[]{:S(2)}) copy-start(f32[384,128]{1,0:T(8,128)} %param.6) | copy-start | bytes 589828
  0.0 15.0 %copy-start.1 = (f32[3,12,128,128]{3,2,1,0:T(8,128)S(1)}, f32[3,12,128,128]{3,2,1,0:T(8,128)}, u32[]{:S(2)}) copy-start(f32[3,12,128,128]{3,2,1,0:T(8,128)} %param.7) | copy-start | bytes 7077892
  0.0 15.0 %collective-permute-start.2 = (f32[3,12,128,128]{3,2,1,0:T(8,128)}, f32[3,12,128,128]{3,2,1,0:T(8,128)}, u32[]{:S(2)}, u32[]{:S(2)}) collective-permute-start(f32[3,12,128,128]{3,2,1,0:T(8,128)} %param.7), channel_id=1, source_target_pairs={{0,1},{1,0},{2,3},{3,2},{4,5},{5,4},{6,7},{7,6},{8,9},{9,8},{10,11... | collective-permute-start | bytes 7077896 | tf_op jit(solution)/shard_map/ppermute | solution.py:22
  10.9 12.5 %copy-start.4 = (s32[3,12]{1,0:T(4,128)S(1)}, s32[3,12]{1,0:T(4,128)}, u32[]{:S(2)}) copy-start(s32[3,12]{1,0:T(4,128)} %param.8) | copy-start | bytes 436
  10.9 12.5 %copy-start.5 = (s32[3,1]{0,1:T(1,128)S(1)}, s32[3,1]{0,1:T(1,128)}, u32[]{:S(2)}) copy-start(s32[3,1]{0,1:T(1,128)} %param.9) | copy-start | bytes 40
  12.4 5.1 %collective-permute-start = (f32[192,128]{1,0:T(8,128)S(1)}, f32[192,128]{1,0:T(8,128)S(1)}, u32[]{:S(2)}, u32[]{:S(2)}) collective-permute-start(f32[192,128]{1,0:T(8,128)S(1)} %bitcast.51), channel_id=1, source_target_pairs={{0,0},{1,1},{2,130},{3,131},{4,260},{5,261},{6,390},{7,391},{8,8},... | collective-permute-start | bytes 294920 | tf_op jit(solution)/shard_map/ppermute | solution.py:22
  13.1 8.4 %collective-permute-start.1 = (f32[192,128]{1,0:T(8,128)S(1)}, f32[192,128]{1,0:T(8,128)S(1)}, u32[]{:S(2)}, u32[]{:S(2)}) collective-permute-start(f32[192,128]{1,0:T(8,128)S(1)} %bitcast.52), channel_id=1, source_target_pairs={{0,64},{1,65},{2,194},{3,195},{4,324},{5,325},{6,454},{7,455},{8,7... | collective-permute-start | bytes 294920 | tf_op jit(solution)/shard_map/ppermute | solution.py:22
  21.5 29.0 %collective-permute-start.3 = (f32[2304,128]{1,0:T(8,128)}, f32[2304,128]{1,0:T(8,128)}, u32[]{:S(2)}, u32[]{:S(2)}) collective-permute-start(f32[2304,128]{1,0:T(8,128)} %bitcast.6), channel_id=1, source_target_pairs={{0,448},{1,449},{2,450},{3,451},{4,452},{5,453},{6,454},{7,455},{8... | collective-permute-start | bytes 3538952 | tf_op jit(solution)/shard_map/ppermute | solution.py:22
  23.5 7.6 %collective-permute-start.4 = (s32[3,12]{1,0:T(4,128)S(1)}, s32[3,12]{1,0:T(4,128)S(1)}, u32[]{:S(2)}, u32[]{:S(2)}) collective-permute-start(s32[3,12]{1,0:T(4,128)S(1)} %fusion), channel_id=1, source_target_pairs={{0,1},{1,0},{2,3},{3,2},{4,5},{5,4},{6,7},{7,6},{8,9},{9,8},{10,11... | collective-permute-start | bytes 440 | tf_op jit(solution)/shard_map/ppermute | solution.py:22
  27.2 27.5 %all-to-all-start = ((f32[8,192,128]{2,1,0:T(8,128)}), f32[8,192,128]{2,1,0:T(8,128)S(1)}, u32[]{:S(2)}, u32[]{:S(2)}) async-start(f32[8,192,128]{2,1,0:T(8,128)} %broadcast_select_fusion), calls=%async_computation | async-start | bytes 1572864 | tf_op jit(solution)/shard_map/all_to_all | solution.py:223
  31.2 1.7 copy-start.2
  35.3 15.2 %collective-permute-start.5 = (f32[6,128]{1,0:T(8,128)S(1)}, f32[6,128]{1,0:T(8,128)S(1)}, u32[]{:S(2)}, u32[]{:S(2)}) collective-permute-start(f32[6,128]{1,0:T(8,128)S(1)} %select_maximum_fusion), channel_id=1, source_target_pairs={{0,448},{1,449},{2,450},{3,451},{4,452},{5,453},{6,454},{7,455},{8... | collective-permute-start | bytes 9224 | tf_op jit(solution)/shard_map/ppermute | solution.py:22
  50.5 6.3 %collective-permute-start.6 = (f32[2304,128]{1,0:T(8,128)}, f32[2304,128]{1,0:T(8,128)}, u32[]{:S(2)}, u32[]{:S(2)}) collective-permute-start(f32[2304,128]{1,0:T(8,128)} %collective-permute-done.3.mine_ref), channel_id=1, source_target_pairs={{0,1},{1,0},{2,3},{3,2},{4,5},{5,4},{6,7},{7,6},{8,9},{9,8},{10,11... | collective-permute-start | bytes 3538952 | tf_op jit(solution)/shard_map/ppermute | solution.py:22
  220.8 7.8 %collective-permute-start.8 = (f32[192,128]{1,0:T(8,128)S(1)}, f32[192,128]{1,0:T(8,128)S(1)}, u32[]{:S(2)}, u32[]{:S(2)}) collective-permute-start(f32[192,128]{1,0:T(8,128)S(1)} %get-tuple-element.48), channel_id=1, source_target_pairs={{0,64},{1,65},{2,66},{3,67},{4,68},{5,69},{6,70},{7,71},{8,72},{9,... | collective-permute-start | bytes 294920 | tf_op jit(solution)/shard_map/ppermute | solution.py:22
  223.4 34.9 %copy-start.3 = (f32[3,128]{1,0:T(4,128)S(1)}, f32[3,128]{1,0:T(4,128)}, u32[]{:S(2)}) copy-start(f32[3,128]{1,0:T(4,128)} %get-tuple-element.52.root_ref) | copy-start | bytes 4612
  229.3 18.3 %all-to-all-start.10 = ((f32[4,192,128]{2,1,0:T(8,128)}), f32[4,192,128]{2,1,0:T(8,128)S(1)}, u32[]{:S(2)}, u32[]{:S(2)}) async-start(f32[4,192,128]{2,1,0:T(8,128)} %shard_map.80), calls=%async_computation.10 | async-start | bytes 786432 | tf_op jit(solution)/shard_map/all_to_all | solution.py:243
  232.8 0.7 collective-permute-start.7
  233.5 23.8 %collective-permute-start.9 = (f32[576,128]{1,0:T(8,128)S(1)}, f32[576,128]{1,0:T(8,128)S(1)}, u32[]{:S(2)}, u32[]{:S(2)}) collective-permute-start(f32[576,128]{1,0:T(8,128)S(1)} %collective-permute-done.7.mine_ref), channel_id=1, source_target_pairs={{0,1},{1,0},{2,3},{3,2},{4,5},{5,4},{6,7},{7,6},{8,9},{9,8},{10,11... | collective-permute-start | bytes 884744 | tf_op jit(solution)/shard_map/ppermute | solution.py:22
  247.7 10.6 %collective-permute-start.10 = (f32[192,128]{1,0:T(8,128)S(1)}, f32[192,128]{1,0:T(8,128)S(1)}, u32[]{:S(2)}, u32[]{:S(2)}) collective-permute-start(f32[192,128]{1,0:T(8,128)S(1)} %reduce_sum.9.mine_last_ref), channel_id=1, source_target_pairs={{0,1},{1,0},{2,3},{3,2},{4,5},{5,4},{6,7},{7,6},{8,9},{9,8},{10,11... | collective-permute-start | bytes 294920 | tf_op jit(solution)/shard_map/ppermute | solution.py:22
